TPU v7x, 512 devices: a whole 4x8x8 slice. The times are simulated.
512 devices in a mesh: dom: 128 (over z, y, core), sub: 4 (over x).
Axes of the slice: x: 4, y: 8, z: 8, core: 2. Of those that a mesh axis runs over, the one named last changes fastest.
Arguments:
- rhs: float32 [64, 8, 65536], P(None, None, ('dom', 'sub')), may hold values from -6 to 6
- guess: float32 [64, 8, 65536], P(None, None, ('dom', 'sub')), may hold values from -4 to 4
- diag_blocks: bfloat16 [2, 64, 64], replicated
- face_blocks: bfloat16 [6, 2, 64, 64], replicated, may hold values from -0.3125 to 0.3125
- smoother: bfloat16 [2, 64, 64], replicated
- coarse_inverse: bfloat16 [64, 64], replicated
- elem_type: int32 [65536], P(('dom', 'sub')), may hold values from 0 to 1
- face_type: int32 [6, 65536], P(None, ('dom', 'sub')), may hold values from 0 to 1
- neighbours: int32 [6, 65536], P(None, ('dom', 'sub')), may hold values from 0 to 239, as said below
- send_near: int32 [2, 16384], P(None, ('dom', 'sub')), may hold values from 0 to 127
- send_far: int32 [2, 4096], P(None, ('dom', 'sub')), may hold values from 0 to 127
- sub_send: int32 [4096], P(('dom', 'sub')), may hold values from 0 to 127
- partner: int32 [65536], P(('dom', 'sub')), may hold values from 0 to 143, as said below
- pair_send: int32 [8192], P(('dom', 'sub')), may hold values from 0 to 127, as said below
Outputs:
- solution: float32 [64, 8, 65536], P(None, None, ('dom', 'sub'))
- residual: float32 [64, 8, 65536], P(None, None, ('dom', 'sub'))
Inputs may be any that keep to these rules, and one draw needn't show every extreme that they name: `neighbours`: values below 128 are the device's own elements; the rest index its 112 received rows in the order of the first step. On each device the partner relation is mutual: local values pair two distinct local elements with each other; each value 128 + q for q below 16 appears exactly once, and the element holding it is entry q of the device's pair_send. `pair_send`: on each device the 16 entries are distinct; slot q pairs with slot q of the device whose sub index differs in the lowest bit.
All inputs are finite; a program needn't handle non-finite values.
Results may differ from a plain program's by a relative error of at most 0.012.
Values may be sent and summed in bfloat16 or wider, within the bound.
No kernel may reach another device: no remote copies, remote signals or barrier semaphores. Data moves between devices by JAX's collectives and lax.ppermute only.
A program may use at most 64 MiB of HBM per device.

v0:
```python
import jax
import jax.numpy as jnp
from jax import lax
from jax.sharding import PartitionSpec as P

SWEEPS = 2


def from_behind(array, axis, by):
    peers = lax.axis_size(axis)
    pairs = [(i, i + by) for i in range(peers) if 0 <= i + by < peers]
    return lax.ppermute(array, axis, pairs)


def partner_2(block, axis, stride):
    count = lax.axis_size(axis)
    route = []
    for low in range(count):
        high = low | 1 << stride
        if high != low and high < count:
            route += [(low, high), (high, low)]
    return lax.ppermute(block, axis, route)


def stack_apply(blocks, field_b, kinds):
    variants = blocks.shape[0]
    node_rows, rhs_width, elements = field_b.shape
    blank = jnp.zeros_like(field_b)
    pieces = [
        jnp.where(kinds[None, None, :] == variant, field_b, blank) for variant in range(variants)
    ]
    operand = jnp.concatenate(pieces, axis=0).reshape(variants * node_rows, rhs_width * elements)
    wide_blocks = jnp.concatenate([blocks[variant] for variant in range(variants)], axis=1)
    product = jnp.dot(wide_blocks, operand, preferred_element_type=jnp.float32)
    return product.reshape(node_rows, rhs_width, elements)


def body(
    rhs,
    guess,
    diag_blocks,
    face_blocks,
    smoother,
    coarse_inverse,
    elem_type,
    face_type,
    neighbours,
    send_near,
    send_far,
    sub_send,
    partner,
    pair_send,
):

    def apply_local(field_b):
        up_near = jnp.take(field_b, send_near[1], axis=2)
        down_near = jnp.take(field_b, send_near[0], axis=2)
        up_far = jnp.take(field_b, send_far[1], axis=2)
        down_far = jnp.take(field_b, send_far[0], axis=2)
        from_below = from_behind(up_near, "dom", 1)
        from_above = from_behind(down_near, "dom", -1)
        far_below = from_behind(up_far, "dom", 2)
        far_above = from_behind(down_far, "dom", -2)
        side_rows = lax.all_gather(jnp.take(field_b, sub_send, axis=2), "sub", axis=2, tiled=True)
        extended = jnp.concatenate(
            [field_b, from_below, from_above, far_below, far_above, side_rows], axis=2
        )
        total = stack_apply(diag_blocks, field_b, elem_type)
        for face_index in range(6):
            beside = jnp.take(extended, neighbours[face_index], axis=2)
            total = total + stack_apply(face_blocks[face_index], beside, face_type[face_index])
        return total

    iterate = guess
    for rounds in range(SWEEPS):
        sweep_res = rhs - apply_local(iterate.astype(jnp.bfloat16))
        iterate = iterate + stack_apply(smoother, sweep_res.astype(jnp.bfloat16), elem_type)
    residual = rhs - apply_local(iterate.astype(jnp.bfloat16))
    outgoing = jnp.take(residual, pair_send, axis=2)
    incoming = partner_2(outgoing.astype(jnp.bfloat16), "sub", 0).astype(outgoing.dtype)
    joined = jnp.concatenate([residual, incoming], axis=2)
    coarse = residual + jnp.take(joined, partner, axis=2)
    node_rows, rhs_width, elements = coarse.shape
    coarse_b = coarse.astype(jnp.bfloat16).reshape(node_rows, rhs_width * elements)
    update = jnp.dot(coarse_inverse, coarse_b, preferred_element_type=jnp.float32)
    solution = iterate + update.reshape(node_rows, rhs_width, elements)
    return (solution, residual)


def solution(mesh):
    in_specs = (
        P(None, None, ("dom", "sub")),
        P(None, None, ("dom", "sub")),
        P(),
        P(),
        P(),
        P(),
        P(("dom", "sub")),
        P(None, ("dom", "sub")),
        P(None, ("dom", "sub")),
        P(None, ("dom", "sub")),
        P(None, ("dom", "sub")),
        P(("dom", "sub")),
        P(("dom", "sub")),
        P(("dom", "sub")),
    )
    out_specs = (P(None, None, ("dom", "sub")), P(None, None, ("dom", "sub")))
    return jax.shard_map(body, mesh=mesh, in_specs=in_specs, out_specs=out_specs, check_vma=False)
```

profile of v0, /device:TPU:256, one launch (start us, length us, event | category | flops | bytes accessed | tf_op | source)
XLA Modules:
  0.0 147.1 jit_solution(16618105193743809623)
XLA Ops:
  0.7 0.7 broadcast_compare_fusion
  1.3 1.0 broadcast_select_fusion.27
  2.6 0.6 gather_fusion.2
  3.3 1.9 %collective-permute-start = (bf16[64,8,32]{2,0,1:T(8,128)(2,1)S(1)}, bf16[64,8,32]{2,0,1:T(8,128)(2,1)S(1)}, u32[]{:S(2)}, u32[]{:S(2)}) collective-permute-start(bf16[64,8,32]{2,0,1:T(8,128)(2,1)S(1)} %select_bitcast_fusion.5), channel_id=1, source_target_pairs={{0,4},{4,8},{8,12},{12,16},{16,20},{20,24},{24,28},{28,32},{32,36}... | collective-permute-start | bytes 98312 | tf_op jit(solution)/shard_map/ppermute | solution.py:12
  5.3 0.6 gather_fusion.3
  6.1 7.0 %collective-permute-start.1 = (bf16[64,8,32]{2,0,1:T(8,128)(2,1)S(1)}, bf16[64,8,32]{2,0,1:T(8,128)(2,1)S(1)}, u32[]{:S(2)}, u32[]{:S(2)}) collective-permute-start(bf16[64,8,32]{2,0,1:T(8,128)(2,1)S(1)} %select_bitcast_fusion.4), channel_id=1, source_target_pairs={{4,0},{8,4},{12,8},{16,12},{20,16},{24,20},{28,24},{32,28},{36,32}... | collective-permute-start | bytes 98312 | tf_op jit(solution)/shard_map/ppermute | solution.py:12
  13.1 0.6 gather_fusion.4
  13.7 1.9 %collective-permute-start.2 = (bf16[64,8,8]{0,1,2:T(8,128)(2,1)S(1)}, bf16[64,8,8]{0,1,2:T(8,128)(2,1)S(1)}, u32[]{:S(2)}, u32[]{:S(2)}) collective-permute-start(bf16[64,8,8]{0,1,2:T(8,128)(2,1)S(1)} %select_bitcast_fusion.14), channel_id=1, source_target_pairs={{0,8},{4,12},{8,16},{12,20},{16,24},{20,28},{24,32},{28,36},{32,40... | collective-permute-start | bytes 24584 | tf_op jit(solution)/shard_map/ppermute | solution.py:12
  15.7 0.6 gather_fusion.5
  16.3 7.2 %collective-permute-start.3 = (bf16[64,8,8]{0,1,2:T(8,128)(2,1)S(1)}, bf16[64,8,8]{0,1,2:T(8,128)(2,1)S(1)}, u32[]{:S(2)}, u32[]{:S(2)}) collective-permute-start(bf16[64,8,8]{0,1,2:T(8,128)(2,1)S(1)} %select_bitcast_fusion.13), channel_id=1, source_target_pairs={{8,0},{12,4},{16,8},{20,12},{24,16},{28,20},{32,24},{36,28},{40,32... | collective-permute-start | bytes 24584 | tf_op jit(solution)/shard_map/ppermute | solution.py:12
  24.0 0.5 copy-done.4
  24.5 0.6 gather_fusion.6
  25.6 12.2 %all_gather.9 = bf16[64,8,32]{0,1,2:T(8,128)(2,1)S(1)} all-gather(bf16[64,8,8]{0,1,2:T(8,128)(2,1)S(1)} %select_bitcast_fusion.12), channel_id=1, replica_groups=mesh['dom'=128,'sub'=4] {'sub'}, dimensions={2}, use_global_device_ids=true | all-gather | bytes 40960 | tf_op jit(solution)/shard_map/all_gather | solution.py:64
  38.5 0.3 copy.269
  38.8 0.7 gather_fusion.7
  40.0 0.7 gather_fusion.8
  41.1 0.7 gather_fusion.9
  42.2 0.7 gather_fusion.10
  43.4 0.7 gather_fusion.11
  44.5 0.7 gather_fusion.12
  47.0 0.7 copy-done.1
  47.7 0.3 broadcast_select_fusion.26
  48.2 0.7 copy-done.2
  49.4 0.6 gather_fusion.13
  50.0 0.6 gather_fusion.14
  50.6 0.6 gather_fusion.15
  51.1 0.6 gather_fusion.16
  51.7 0.6 gather_fusion.17
  52.9 1.9 %collective-permute-start.4 = (bf16[64,8,32]{2,0,1:T(8,128)(2,1)S(1)}, bf16[64,8,32]{2,0,1:T(8,128)(2,1)S(1)}, u32[]{:S(2)}, u32[]{:S(2)}) collective-permute-start(bf16[64,8,32]{2,0,1:T(8,128)(2,1)S(1)} %select_bitcast_fusion.3), channel_id=1, source_target_pairs={{0,4},{4,8},{8,12},{12,16},{16,20},{20,24},{24,28},{28,32},{32,36}... | collective-permute-start | bytes 98312 | tf_op jit(solution)/shard_map/ppermute | solution.py:12
  55.0 7.0 %collective-permute-start.5 = (bf16[64,8,32]{2,0,1:T(8,128)(2,1)S(1)}, bf16[64,8,32]{2,0,1:T(8,128)(2,1)S(1)}, u32[]{:S(2)}, u32[]{:S(2)}) collective-permute-start(bf16[64,8,32]{2,0,1:T(8,128)(2,1)S(1)} %select_bitcast_fusion.2), channel_id=1, source_target_pairs={{4,0},{8,4},{12,8},{16,12},{20,16},{24,20},{28,24},{32,28},{36,32}... | collective-permute-start | bytes 98312 | tf_op jit(solution)/shard_map/ppermute | solution.py:12
  62.1 1.9 %collective-permute-start.6 = (bf16[64,8,8]{0,1,2:T(8,128)(2,1)S(1)}, bf16[64,8,8]{0,1,2:T(8,128)(2,1)S(1)}, u32[]{:S(2)}, u32[]{:S(2)}) collective-permute-start(bf16[64,8,8]{0,1,2:T(8,128)(2,1)S(1)} %select_bitcast_fusion.11), channel_id=1, source_target_pairs={{0,8},{4,12},{8,16},{12,20},{16,24},{20,28},{24,32},{28,36},{32,40... | collective-permute-start | bytes 24584 | tf_op jit(solution)/shard_map/ppermute | solution.py:12
  64.1 7.2 %collective-permute-start.7 = (bf16[64,8,8]{0,1,2:T(8,128)(2,1)S(1)}, bf16[64,8,8]{0,1,2:T(8,128)(2,1)S(1)}, u32[]{:S(2)}, u32[]{:S(2)}) collective-permute-start(bf16[64,8,8]{0,1,2:T(8,128)(2,1)S(1)} %select_bitcast_fusion.10), channel_id=1, source_target_pairs={{8,0},{12,4},{16,8},{20,12},{24,16},{28,20},{32,24},{36,28},{40,32... | collective-permute-start | bytes 24584 | tf_op jit(solution)/shard_map/ppermute | solution.py:12
  71.4 12.0 %all_gather.10 = bf16[64,8,32]{0,1,2:T(8,128)(2,1)S(1)} all-gather(bf16[64,8,8]{0,1,2:T(8,128)(2,1)S(1)} %select_bitcast_fusion.9), channel_id=1, replica_groups=mesh['dom'=128,'sub'=4] {'sub'}, dimensions={2}, use_global_device_ids=true | all-gather | bytes 40960 | tf_op jit(solution)/shard_map/all_gather | solution.py:64
  84.2 0.3 copy.301
  84.5 0.7 gather_fusion.18
  85.1 0.7 gather_fusion.19
  85.8 0.7 gather_fusion.20
  86.5 0.7 gather_fusion.21
  87.2 0.7 gather_fusion.22
  87.9 0.7 gather_fusion.23
  92.6 0.3 broadcast_select_fusion.24
  93.6 0.6 gather_fusion.24
  94.2 0.6 gather_fusion.25
  94.8 0.6 gather_fusion.26
  95.3 0.6 gather_fusion.27
  95.9 0.6 gather_fusion.28
  97.1 1.9 %collective-permute-start.8 = (bf16[64,8,32]{2,0,1:T(8,128)(2,1)S(1)}, bf16[64,8,32]{2,0,1:T(8,128)(2,1)S(1)}, u32[]{:S(2)}, u32[]{:S(2)}) collective-permute-start(bf16[64,8,32]{2,0,1:T(8,128)(2,1)S(1)} %select_bitcast_fusion.1), channel_id=1, source_target_pairs={{0,4},{4,8},{8,12},{12,16},{16,20},{20,24},{24,28},{28,32},{32,36}... | collective-permute-start | bytes 98312 | tf_op jit(solution)/shard_map/ppermute | solution.py:12
  99.2 7.0 %collective-permute-start.9 = (bf16[64,8,32]{2,0,1:T(8,128)(2,1)S(1)}, bf16[64,8,32]{2,0,1:T(8,128)(2,1)S(1)}, u32[]{:S(2)}, u32[]{:S(2)}) collective-permute-start(bf16[64,8,32]{2,0,1:T(8,128)(2,1)S(1)} %select_bitcast_fusion), channel_id=1, source_target_pairs={{4,0},{8,4},{12,8},{16,12},{20,16},{24,20},{28,24},{32,28},{36,32}... | collective-permute-start | bytes 98312 | tf_op jit(solution)/shard_map/ppermute | solution.py:12
  106.3 1.9 %collective-permute-start.10 = (bf16[64,8,8]{0,1,2:T(8,128)(2,1)S(1)}, bf16[64,8,8]{0,1,2:T(8,128)(2,1)S(1)}, u32[]{:S(2)}, u32[]{:S(2)}) collective-permute-start(bf16[64,8,8]{0,1,2:T(8,128)(2,1)S(1)} %select_bitcast_fusion.8), channel_id=1, source_target_pairs={{0,8},{4,12},{8,16},{12,20},{16,24},{20,28},{24,32},{28,36},{32,40... | collective-permute-start | bytes 24584 | tf_op jit(solution)/shard_map/ppermute | solution.py:12
  108.3 7.2 %collective-permute-start.11 = (bf16[64,8,8]{0,1,2:T(8,128)(2,1)S(1)}, bf16[64,8,8]{0,1,2:T(8,128)(2,1)S(1)}, u32[]{:S(2)}, u32[]{:S(2)}) collective-permute-start(bf16[64,8,8]{0,1,2:T(8,128)(2,1)S(1)} %select_bitcast_fusion.7), channel_id=1, source_target_pairs={{8,0},{12,4},{16,8},{20,12},{24,16},{28,20},{32,24},{36,28},{40,32... | collective-permute-start | bytes 24584 | tf_op jit(solution)/shard_map/ppermute | solution.py:12
  115.6 11.9 %all_gather.11 = bf16[64,8,32]{0,1,2:T(8,128)(2,1)S(1)} all-gather(bf16[64,8,8]{0,1,2:T(8,128)(2,1)S(1)} %select_bitcast_fusion.6), channel_id=1, replica_groups=mesh['dom'=128,'sub'=4] {'sub'}, dimensions={2}, use_global_device_ids=true | all-gather | bytes 40960 | tf_op jit(solution)/shard_map/all_gather | solution.py:64
  128.5 0.7 gather_fusion.30
  129.2 0.7 gather_fusion.29
  129.9 0.7 gather_fusion.32
  130.5 0.7 gather_fusion.31
  131.2 0.7 gather_fusion.34
  131.9 0.7 gather_fusion.33
  137.1 0.6 gather_fusion
  137.8 3.1 %collective-permute-start.12 = (bf16[64,8,16]{2,0,1:T(8,128)(2,1)S(1)}, bf16[64,8,16]{2,0,1:T(8,128)(2,1)S(1)}, u32[]{:S(2)}, u32[]{:S(2)}) collective-permute-start(bf16[64,8,16]{2,0,1:T(8,128)(2,1)S(1)} %fusion.32), channel_id=1, source_target_pairs={{0,1},{1,0},{2,3},{3,2},{4,5},{5,4},{6,7},{7,6},{8,9},{9,8},{10,11... | collective-permute-start | bytes 49160 | tf_op jit(solution)/shard_map/ppermute | solution.py:22
  141.0 0.9 copy.358
  141.8 2.9 %collective-permute-done.12 = bf16[64,8,16]{2,0,1:T(8,128)(2,1)S(1)} collective-permute-done((bf16[64,8,16]{2,0,1:T(8,128)(2,1)S(1)}, bf16[64,8,16]{2,0,1:T(8,128)(2,1)S(1)}, u32[]{:S(2)}, u32[]{:S(2)}) %collective-permute-start.12) | collective-permute-done | bytes 16416 | tf_op jit(solution)/shard_map/ppermute | solution.py:22
  144.7 0.3 copy.353
  145.1 0.8 gather_fusion.1
  146.3 0.9 copy.357
  (209 shorter events, 19.6 us)
Async XLA Ops:
  0.6 145.4 %copy-start = (bf16[64,64]{1,0:T(8,128)(2,1)S(1)}, bf16[64,64]{1,0:T(8,128)(2,1)}, u32[]{:S(2)}) copy-start(bf16[64,64]{1,0:T(8,128)(2,1)} %param.25) | copy-start | bytes 24580
  0.6 1.9 %copy-start.8 = (s32[2,32]{1,0:T(2,128)S(1)}, s32[2,32]{1,0:T(2,128)}, u32[]{:S(2)}) copy-start(s32[2,32]{1,0:T(2,128)} %param.29) | copy-start | bytes 772
  3.2 9.9 %copy-start.9 = (s32[2,8]{1,0:T(2,128)S(1)}, s32[2,8]{1,0:T(2,128)}, u32[]{:S(2)}) copy-start(s32[2,8]{1,0:T(2,128)} %param.30) | copy-start | bytes 196
  3.3 34.9 %collective-permute-start = (bf16[64,8,32]{2,0,1:T(8,128)(2,1)S(1)}, bf16[64,8,32]{2,0,1:T(8,128)(2,1)S(1)}, u32[]{:S(2)}, u32[]{:S(2)}) collective-permute-start(bf16[64,8,32]{2,0,1:T(8,128)(2,1)S(1)} %select_bitcast_fusion.5), channel_id=1, source_target_pairs={{0,4},{4,8},{8,12},{12,16},{16,20},{20,24},{24,28},{28,32},{32,36}... | collective-permute-start | bytes 98312 | tf_op jit(solution)/shard_map/ppermute | solution.py:12
  5.9 17.7 %copy-start.10 = (s32[8]{0:T(128)S(1)}, s32[8]{0:T(128)}, u32[]{:S(2)}) copy-start(s32[8]{0:T(128)} %param.31) | copy-start | bytes 100
  5.9 17.7 %copy-start.11 = (s32[16]{0:T(128)S(1)}, s32[16]{0:T(128)}, u32[]{:S(2)}) copy-start(s32[16]{0:T(128)} %param.33) | copy-start | bytes 196
  5.9 17.7 %copy-start.12 = (s32[128]{0:T(128)S(1)}, s32[128]{0:T(128)}, u32[]{:S(2)}) copy-start(s32[128]{0:T(128)} %param.32) | copy-start | bytes 1540
  6.1 32.2 %collective-permute-start.1 = (bf16[64,8,32]{2,0,1:T(8,128)(2,1)S(1)}, bf16[64,8,32]{2,0,1:T(8,128)(2,1)S(1)}, u32[]{:S(2)}, u32[]{:S(2)}) collective-permute-start(bf16[64,8,32]{2,0,1:T(8,128)(2,1)S(1)} %select_bitcast_fusion.4), channel_id=1, source_target_pairs={{4,0},{8,4},{12,8},{16,12},{20,16},{24,20},{28,24},{32,28},{36,32}... | collective-permute-start | bytes 98312 | tf_op jit(solution)/shard_map/ppermute | solution.py:12
  13.7 24.2 %collective-permute-start.2 = (bf16[64,8,8]{0,1,2:T(8,128)(2,1)S(1)}, bf16[64,8,8]{0,1,2:T(8,128)(2,1)S(1)}, u32[]{:S(2)}, u32[]{:S(2)}) collective-permute-start(bf16[64,8,8]{0,1,2:T(8,128)(2,1)S(1)} %select_bitcast_fusion.14), channel_id=1, source_target_pairs={{0,8},{4,12},{8,16},{12,20},{16,24},{20,28},{24,32},{28,36},{32,40... | collective-permute-start | bytes 24584 | tf_op jit(solution)/shard_map/ppermute | solution.py:12
  16.3 21.8 %collective-permute-start.3 = (bf16[64,8,8]{0,1,2:T(8,128)(2,1)S(1)}, bf16[64,8,8]{0,1,2:T(8,128)(2,1)S(1)}, u32[]{:S(2)}, u32[]{:S(2)}) collective-permute-start(bf16[64,8,8]{0,1,2:T(8,128)(2,1)S(1)} %select_bitcast_fusion.13), channel_id=1, source_target_pairs={{8,0},{12,4},{16,8},{20,12},{24,16},{28,20},{32,24},{36,28},{40,32... | collective-permute-start | bytes 24584 | tf_op jit(solution)/shard_map/ppermute | solution.py:12
  23.7 0.8 copy-start.4
  23.7 0.8 copy-start.6
  23.7 1.3 copy-start.7
  23.7 1.4 copy-start.3
  23.8 1.4 copy-start.5
  46.7 1.0 copy-start.1
  47.9 1.0 copy-start.2
  52.9 30.9 %collective-permute-start.4 = (bf16[64,8,32]{2,0,1:T(8,128)(2,1)S(1)}, bf16[64,8,32]{2,0,1:T(8,128)(2,1)S(1)}, u32[]{:S(2)}, u32[]{:S(2)}) collective-permute-start(bf16[64,8,32]{2,0,1:T(8,128)(2,1)S(1)} %select_bitcast_fusion.3), channel_id=1, source_target_pairs={{0,4},{4,8},{8,12},{12,16},{16,20},{20,24},{24,28},{28,32},{32,36}... | collective-permute-start | bytes 98312 | tf_op jit(solution)/shard_map/ppermute | solution.py:12
  55.0 28.9 %collective-permute-start.5 = (bf16[64,8,32]{2,0,1:T(8,128)(2,1)S(1)}, bf16[64,8,32]{2,0,1:T(8,128)(2,1)S(1)}, u32[]{:S(2)}, u32[]{:S(2)}) collective-permute-start(bf16[64,8,32]{2,0,1:T(8,128)(2,1)S(1)} %select_bitcast_fusion.2), channel_id=1, source_target_pairs={{4,0},{8,4},{12,8},{16,12},{20,16},{24,20},{28,24},{32,28},{36,32}... | collective-permute-start | bytes 98312 | tf_op jit(solution)/shard_map/ppermute | solution.py:12
  62.1 21.5 %collective-permute-start.6 = (bf16[64,8,8]{0,1,2:T(8,128)(2,1)S(1)}, bf16[64,8,8]{0,1,2:T(8,128)(2,1)S(1)}, u32[]{:S(2)}, u32[]{:S(2)}) collective-permute-start(bf16[64,8,8]{0,1,2:T(8,128)(2,1)S(1)} %select_bitcast_fusion.11), channel_id=1, source_target_pairs={{0,8},{4,12},{8,16},{12,20},{16,24},{20,28},{24,32},{28,36},{32,40... | collective-permute-start | bytes 24584 | tf_op jit(solution)/shard_map/ppermute | solution.py:12
  64.1 19.6 %collective-permute-start.7 = (bf16[64,8,8]{0,1,2:T(8,128)(2,1)S(1)}, bf16[64,8,8]{0,1,2:T(8,128)(2,1)S(1)}, u32[]{:S(2)}, u32[]{:S(2)}) collective-permute-start(bf16[64,8,8]{0,1,2:T(8,128)(2,1)S(1)} %select_bitcast_fusion.10), channel_id=1, source_target_pairs={{8,0},{12,4},{16,8},{20,12},{24,16},{28,20},{32,24},{36,28},{40,32... | collective-permute-start | bytes 24584 | tf_op jit(solution)/shard_map/ppermute | solution.py:12
  97.1 30.8 %collective-permute-start.8 = (bf16[64,8,32]{2,0,1:T(8,128)(2,1)S(1)}, bf16[64,8,32]{2,0,1:T(8,128)(2,1)S(1)}, u32[]{:S(2)}, u32[]{:S(2)}) collective-permute-start(bf16[64,8,32]{2,0,1:T(8,128)(2,1)S(1)} %select_bitcast_fusion.1), channel_id=1, source_target_pairs={{0,4},{4,8},{8,12},{12,16},{16,20},{20,24},{24,28},{28,32},{32,36}... | collective-permute-start | bytes 98312 | tf_op jit(solution)/shard_map/ppermute | solution.py:12
  99.2 28.7 %collective-permute-start.9 = (bf16[64,8,32]{2,0,1:T(8,128)(2,1)S(1)}, bf16[64,8,32]{2,0,1:T(8,128)(2,1)S(1)}, u32[]{:S(2)}, u32[]{:S(2)}) collective-permute-start(bf16[64,8,32]{2,0,1:T(8,128)(2,1)S(1)} %select_bitcast_fusion), channel_id=1, source_target_pairs={{4,0},{8,4},{12,8},{16,12},{20,16},{24,20},{28,24},{32,28},{36,32}... | collective-permute-start | bytes 98312 | tf_op jit(solution)/shard_map/ppermute | solution.py:12
  106.3 21.3 %collective-permute-start.10 = (bf16[64,8,8]{0,1,2:T(8,128)(2,1)S(1)}, bf16[64,8,8]{0,1,2:T(8,128)(2,1)S(1)}, u32[]{:S(2)}, u32[]{:S(2)}) collective-permute-start(bf16[64,8,8]{0,1,2:T(8,128)(2,1)S(1)} %select_bitcast_fusion.8), channel_id=1, source_target_pairs={{0,8},{4,12},{8,16},{12,20},{16,24},{20,28},{24,32},{28,36},{32,40... | collective-permute-start | bytes 24584 | tf_op jit(solution)/shard_map/ppermute | solution.py:12
  108.3 19.5 %collective-permute-start.11 = (bf16[64,8,8]{0,1,2:T(8,128)(2,1)S(1)}, bf16[64,8,8]{0,1,2:T(8,128)(2,1)S(1)}, u32[]{:S(2)}, u32[]{:S(2)}) collective-permute-start(bf16[64,8,8]{0,1,2:T(8,128)(2,1)S(1)} %select_bitcast_fusion.7), channel_id=1, source_target_pairs={{8,0},{12,4},{16,8},{20,12},{24,16},{28,20},{32,24},{36,28},{40,32... | collective-permute-start | bytes 24584 | tf_op jit(solution)/shard_map/ppermute | solution.py:12
  137.8 6.9 %collective-permute-start.12 = (bf16[64,8,16]{2,0,1:T(8,128)(2,1)S(1)}, bf16[64,8,16]{2,0,1:T(8,128)(2,1)S(1)}, u32[]{:S(2)}, u32[]{:S(2)}) collective-permute-start(bf16[64,8,16]{2,0,1:T(8,128)(2,1)S(1)} %fusion.32), channel_id=1, source_target_pairs={{0,1},{1,0},{2,3},{3,2},{4,5},{5,4},{6,7},{7,6},{8,9},{9,8},{10,11... | collective-permute-start | bytes 49160 | tf_op jit(solution)/shard_map/ppermute | solution.py:22
where the time goes:
time: 148 us; the launch traced here: 147 us
  starting transfers between devices  57.2 us (39%)
  local copies, waits for them, and re-layouts  39 us (26%)
  blocking collectives  36.1 us (24%)
  matrix products  6.08 us (4%)
  other arithmetic  3.72 us (3%)
  waiting for transfers between devices  2.89 us (2%)
  between operations  2.13 us (1%)
    ppermute x12, starting transfers between devices, from_behind(): return lax.ppermute(array, axis, pairs)  54.1 us
    all_gather x3, blocking collectives, apply_local(): lax.all_gather(jnp.take(field_b, sub_send, axis=2), 'sub', axis=2, tiled=...  36.1 us
    gather x36, local copies, waits for them, and re-layouts, apply_local(): beside = jnp.take(extended, neighbours[face_index], axis=2)  16 us
    dot_general x23, matrix products, stack_apply(): product = jnp.dot(wide_blocks, operand, preferred_element_type=jnp.float32)  5.91 us
    concatenate x23, local copies, waits for them, and re-layouts, stack_apply(): jnp.concatenate(pieces, axis=0)  4.08 us
    unnamed x28, local copies, waits for them, and re-layouts  3.7 us
    ppermute x1, starting transfers between devices, partner_2(): return lax.ppermute(block, axis, route)  3.12 us
  transfers between devices with their start and end apart: 13, of which 1 were waited for; matrix products, arithmetic and copies ran while one was open for 4% of the time, Pallas kernels for 0%

commit v1 on v0

v1 whole, which is shorter than its diff:
```python
import functools

import jax
import jax.numpy as jnp
from jax import lax
from jax.experimental import pallas as pl
from jax.experimental.pallas import tpu as pltpu
from jax.sharding import PartitionSpec as P

SWEEPS = 2
DOF = 64
RHS = 8
E = 128
FACES = 6
ROWS = DOF * RHS
BF = jnp.bfloat16
F32 = jnp.float32

SPLIT = (32, 32, 16, 16, 32)
HALO = sum(SPLIT)
PAIRS = 16


def swap(array, axis, pairs):
    count = lax.axis_size(axis)
    route = []
    for low, high in pairs:
        if high < count:
            route += [(low, high), (high, low)]
    return lax.ppermute(array, axis, route)


def spec():
    return pl.BlockSpec(memory_space=pltpu.VMEM)


def call(kernel, outs, *args, flops=0, scalars=0):
    specs = [pl.BlockSpec(memory_space=pltpu.SMEM)] * scalars
    specs += [spec()] * (len(args) - scalars)
    moved = sum(a.size * a.dtype.itemsize for a in args)
    return pl.pallas_call(
        kernel,
        out_shape=[jax.ShapeDtypeStruct(s, d) for s, d in outs],
        in_specs=specs,
        out_specs=[spec()] * len(outs),
        cost_estimate=pl.CostEstimate(flops=flops, bytes_accessed=moved, transcendentals=0),
        compiler_params=pltpu.CompilerParams(vmem_limit_bytes=32 << 20),
    )(*args)


def iota(shape, dim):
    return lax.broadcasted_iota(jnp.int32, shape, dim)


def column(row):
    count = row.shape[1]
    wide = jnp.broadcast_to(row.astype(F32), (count, count))
    kept = jnp.where(iota((count, count), 0) == iota((count, count), 1), wide, 0.0)
    return jnp.sum(kept, axis=1, keepdims=True).astype(jnp.int32)


def picker(row):
    count = row.shape[1]
    return jnp.where(iota((count, E), 1) == column(row), 1.0, 0.0).astype(BF)


def send(choice, field, refs):
    rows = lax.dot_general(choice, field, (((1,), (1,)), ((), ())), preferred_element_type=F32).astype(BF)
    start = 0
    for ref in refs:
        ref[...] = rows[start : start + ref.shape[0]]
        start += ref.shape[0]


def pack_kernel(odd_ref, guess, near, far, sub, pair, field_ref, choice_ref, *messages):
    odd_core = odd_ref[0] == 1
    odd_chip = odd_ref[1] == 1
    for r in range(RHS):
        field_ref[r * DOF : (r + 1) * DOF, :] = guess[pl.ds(r, DOF, stride=RHS), :].astype(BF)
    lower, higher = near[0:1, :], near[1:2, :]
    far_lower, far_higher = far[0:1, :], far[1:2, :]
    blank = jnp.zeros((8, E), BF)
    side = picker(sub[...])
    choice = jnp.concatenate(
        [
            picker(jnp.where(odd_core, lower, higher)),
            picker(jnp.where(odd_core, higher, lower)),
            picker(jnp.where(odd_chip, far_lower, far_higher)),
            blank,
            picker(jnp.where(odd_chip, far_higher, far_lower)),
            blank,
            side,
            side,
            side,
            side,
            picker(pair[...]),
        ],
        axis=0,
    )
    choice_ref[...] = choice
    send(choice[:HALO], field_ref[...], messages)


def prep_kernel(odd_ref, diag, face, smooth, elem_type, face_type, neighbours, partner, pick_ref, mask_ref, wide_ref, smooth_ref, mate_ref):
    odd_core = odd_ref[0]
    odd_chip = odd_ref[1]
    for d in range(FACES):
        k = neighbours[d : d + 1, :]
        below = jnp.where(odd_core == 1, 0, 32)
        above = jnp.where(odd_core == 1, 0, -32)
        far_below = jnp.where(odd_chip == 1, 0, 16)
        far_above = jnp.where(odd_chip == 1, 8, -8)
        shift = jnp.where(k < 208, far_above, 16)
        shift = jnp.where(k < 200, far_below, shift)
        shift = jnp.where(k < 192, above, shift)
        shift = jnp.where(k < 160, below, shift)
        place = k + jnp.where(k < 128, 0, shift)
        hot = jnp.where(iota((E + HALO, E), 0) == place, 1.0, 0.0)
        pick_ref[:, d * E : (d + 1) * E] = hot.astype(BF)
    for d in range(FACES + 1):
        kinds = elem_type[...] if d == 0 else face_type[d - 1 : d, :]
        for t in range(2):
            mask = jnp.where(jnp.broadcast_to(kinds, (16, E)) == t, 1.0, 0.0)
            mask_ref[2 * d + t] = mask.astype(BF)
        pair = (diag[0], diag[1]) if d == 0 else (face[d - 1, 0], face[d - 1, 1])
        wide_ref[:, d * 2 * DOF : (d + 1) * 2 * DOF] = jnp.concatenate(pair, axis=1)
    smooth_ref[...] = jnp.concatenate([smooth[0], smooth[1]], axis=1)
    mate_ref[...] = jnp.where(iota((E + PAIRS, E), 0) == partner[...], 1.0, 0.0).astype(BF)


def masked(block, mask):
    full = jnp.concatenate([mask] * (DOF // 16), axis=0)
    return block * full


def residual_of(field_ref, halo, pick, masks, wide, rhs, take):
    near = jnp.concatenate([ref[...] for ref in halo], axis=0)
    field = field_ref[...]
    beside = jnp.dot(field, pick[:E, :], preferred_element_type=F32)
    beside = beside + lax.dot_general(near, pick[E:, :], (((0,), (0,)), ((), ())), preferred_element_type=F32)
    beside = beside.astype(BF)
    for r in range(0, RHS, 2):
        halves = []
        for s in (r, r + 1):
            stack = []
            for d in range(FACES + 1):
                block = field[s * DOF : (s + 1) * DOF, :] if d == 0 else beside[s * DOF : (s + 1) * DOF, (d - 1) * E : d * E]
                stack += [masked(block, masks[2 * d]), masked(block, masks[2 * d + 1])]
            halves.append(jnp.concatenate(stack, axis=0))
        product = jnp.dot(wide[...], jnp.concatenate(halves, axis=1), preferred_element_type=F32)
        right = jnp.concatenate([rhs[pl.ds(s, DOF, stride=RHS), :] for s in (r, r + 1)], axis=1)
        take(r, right - product)


def sweep_kernel(first, field_ref, n1, n2, f1, f2, side, pick, masks, wide, smooth, rhs, before, choice, after, next_field, *messages):
    def take(r, residual):
        rounded = residual.astype(BF)
        halves = []
        for i in range(2):
            block = rounded[:, i * E : (i + 1) * E]
            halves.append(jnp.concatenate([masked(block, masks[0]), masked(block, masks[1])], axis=0))
        change = jnp.dot(smooth[...], jnp.concatenate(halves, axis=1), preferred_element_type=F32)
        for i in range(2):
            s = r + i
            rows = slice(s * DOF, (s + 1) * DOF)
            old = before[pl.ds(s, DOF, stride=RHS), :] if first else before[rows, :]
            new = old + change[:, i * E : (i + 1) * E]
            after[rows, :] = new
            next_field[rows, :] = new.astype(BF)

    residual_of(field_ref, (n1, n2, f1, f2, side), pick, masks, wide, rhs, take)
    send(choice[:HALO, :], next_field[...], messages)


def residual_kernel(field_ref, n1, n2, f1, f2, side, pick, masks, wide, rhs, choice, residual_ref, rounded_ref, rest_ref, message):
    def take(r, residual):
        for i in range(2):
            s = r + i
            part = residual[:, i * E : (i + 1) * E]
            residual_ref[pl.ds(s, DOF, stride=RHS), :] = part
            rounded = part.astype(BF)
            rounded_ref[s * DOF : (s + 1) * DOF, :] = rounded
            rest_ref[s * DOF : (s + 1) * DOF, :] = (part - rounded.astype(F32)).astype(BF)

    residual_of(field_ref, (n1, n2, f1, f2, side), pick, masks, wide, rhs, take)
    send(choice[HALO:, :], rounded_ref[...], (message,))


def coarse_kernel(residual_ref, rounded_ref, rest_ref, incoming, mate, inverse, iterate, solution_ref):
    local = mate[:E, :]
    mates = jnp.dot(rounded_ref[...], local, preferred_element_type=F32)
    mates = mates + jnp.dot(rest_ref[...], local, preferred_element_type=F32)
    mates = mates + lax.dot_general(incoming[...], mate[E:, :], (((0,), (0,)), ((), ())), preferred_element_type=F32)
    for r in range(0, RHS, 2):
        halves = []
        for s in (r, r + 1):
            coarse = residual_ref[pl.ds(s, DOF, stride=RHS), :] + mates[s * DOF : (s + 1) * DOF, :]
            halves.append(coarse.astype(BF))
        update = jnp.dot(inverse[...], jnp.concatenate(halves, axis=1), preferred_element_type=F32)
        for i in range(2):
            s = r + i
            solution_ref[pl.ds(s, DOF, stride=RHS), :] = iterate[s * DOF : (s + 1) * DOF, :] + update[:, i * E : (i + 1) * E]


def body(
    rhs,
    guess,
    diag_blocks,
    face_blocks,
    smoother,
    coarse_inverse,
    elem_type,
    face_type,
    neighbours,
    send_near,
    send_far,
    sub_send,
    partner,
    pair_send,
):
    a = lax.axis_index("dom")
    odd = jnp.stack([a % 2, (a // 2) % 2]).astype(jnp.int32)
    doms = lax.axis_size("dom")
    rhs = rhs.reshape(ROWS, E)
    guess = guess.reshape(ROWS, E)
    inside = [(i, i + 1) for i in range(0, doms, 2)]
    across = [(i + 1, i + 2) for i in range(0, doms, 2)]
    far_one = [(i + j, i + j + 2) for i in range(0, doms, 4) for j in range(2)]
    far_two = [(i + j + 2, i + j + 4) for i in range(0, doms, 4) for j in range(2)]

    def exchange(messages):
        n1, n2, f1, f2, side = messages
        return (
            swap(n1, "dom", inside),
            swap(n2, "dom", across),
            swap(f1, "dom", far_one),
            swap(f2, "dom", far_two),
            lax.all_to_all(side, "sub", 0, 0, tiled=True),
        )

    message_outs = [((n, ROWS), BF) for n in SPLIT]
    field, choice, *messages = call(
        pack_kernel,
        [((ROWS, E), BF), ((HALO + PAIRS, E), BF)] + message_outs,
        odd,
        guess,
        send_near,
        send_far,
        sub_send.reshape(1, -1),
        pair_send.reshape(1, -1),
        flops=2 * HALO * E * ROWS,
        scalars=1,
    )
    halo = exchange(messages)
    pick, masks, wide, smooth, mate = call(
        prep_kernel,
        [
            ((E + HALO, FACES * E), BF),
            ((2 * FACES + 2, 16, E), BF),
            ((DOF, 2 * DOF * (FACES + 1)), BF),
            ((DOF, 2 * DOF), BF),
            ((E + PAIRS, E), BF),
        ],
        odd,
        diag_blocks,
        face_blocks,
        smoother,
        elem_type.reshape(1, -1),
        face_type,
        neighbours,
        partner.reshape(1, -1),
        flops=1000000,
        scalars=1,
    )
    work = 2 * ROWS * (E + HALO) * FACES * E + 2 * DOF * 14 * DOF * RHS * E
    iterate = guess
    for rounds in range(SWEEPS):
        iterate, field, *messages = call(
            functools.partial(sweep_kernel, rounds == 0),
            [((ROWS, E), F32), ((ROWS, E), BF)] + message_outs,
            field,
            *halo,
            pick,
            masks,
            wide,
            smooth,
            rhs,
            iterate,
            choice,
            flops=work,
        )
        halo = exchange(messages)
    residual, rounded, rest, message = call(
        residual_kernel,
        [((ROWS, E), F32), ((ROWS, E), BF), ((ROWS, E), BF), ((PAIRS, ROWS), BF)],
        field,
        *halo,
        pick,
        masks,
        wide,
        rhs,
        choice,
        flops=work,
    )
    subs = lax.axis_size("sub")
    incoming = swap(message, "sub", [(i, i + 1) for i in range(0, subs, 2)])
    (solved,) = call(
        coarse_kernel,
        [((ROWS, E), F32)],
        residual,
        rounded,
        rest,
        incoming,
        mate,
        coarse_inverse,
        iterate,
        flops=work // 4,
    )
    shape = (DOF, RHS, E)
    return (solved.reshape(shape), residual.reshape(shape))


def solution(mesh):
    block = P(None, None, ("dom", "sub"))
    flat = P(("dom", "sub"))
    listed = P(None, ("dom", "sub"))
    in_specs = (block, block, P(), P(), P(), P(), flat, listed, listed, listed, listed, flat, flat, flat)
    return jax.shard_map(body, mesh=mesh, in_specs=in_specs, out_specs=(block, block), check_vma=False)
```

time: 148 us -> 84.9 us (0.57)
  the two profiles are of different devices: /device:TPU:256 before, /device:TPU:258 now
where the time goes in v1:
time: 84.9 us; the launch traced here: 84.1 us
  starting transfers between devices  49.5 us (58%)
  waiting for transfers between devices  19.1 us (22%)
  Pallas kernels  9.64 us (11%)
  local copies, waits for them, and re-layouts  4.82 us (6%)
  between operations  0.93 us (1%)
    ppermute x13, starting transfers between devices, swap(): return lax.ppermute(array, axis, route)  35.1 us
    ppermute x13, waiting for transfers between devices, swap(): return lax.ppermute(array, axis, route)  19.1 us
    all_to_all x3, starting transfers between devices, exchange(): lax.all_to_all(side, 'sub', 0, 0, tiled=True)  14.5 us
    pallas_call x6, Pallas kernels, call(): pl.pallas_call(kernel, out_shape=[jax.ShapeDtypeStruct(s, d) for s, d in...  9.64 us
    unnamed x32, local copies, waits for them, and re-layouts  4.82 us
  transfers between devices with their start and end apart: 16, of which 6 were waited for; matrix products, arithmetic and copies ran while one was open for 0% of the time, Pallas kernels for 1%

profile of v1, /device:TPU:258, one launch (start us, length us, event | category | flops | bytes accessed | tf_op | source)
XLA Modules:
  0.0 84.1 jit_solution(14021606324326467239)
XLA Ops:
  0.6 0.0 copy-start.13
  0.6 0.0 copy-start.9
  0.7 0.0 copy-start.10
  0.7 0.0 copy-start.11
  0.7 0.0 copy-start.6
  0.7 0.0 copy-start.8
  0.7 0.0 copy-start.5
  0.7 0.1 pad_add_fusion.odd_ref
  0.8 0.5 copy-done.13
  1.3 0.1 copy-done.10
  1.3 0.0 copy-done.11
  1.4 0.1 copy-done.12
  1.5 0.9 %copy-done = f32[64,8,128]{2,1,0:T(8,128)S(1)} copy-done((f32[64,8,128]{2,1,0:T(8,128)S(1)}, f32[64,8,128]{2,1,0:T(8,128)}, u32[]{:S(2)}) %copy-start) | copy-done | bytes 262168
  2.4 1.4 %shard_map.149 = (bf16[512,128]{1,0:T(8,128)(2,1)S(1)}, bf16[144,128]{1,0:T(8,128)(2,1)S(1)}, bf16[32,512]{1,0:T(8,128)(2,1)S(1)}, bf16[32,512]{1,0:T(8,128)(2,1...) custom-call(s32[2]{0:T(128)S(1)} %pad_add_fusion.odd_ref, ...), custom_call_target="tpu_custom_call" | custom-call | flops 16777216 | bytes 262568 | tf_op jit(solution)/shard_map/pallas_call | solution.py:41
  3.8 1.9 %collective-permute-start = (bf16[32,512]{1,0:T(8,128)(2,1)S(1)}, bf16[32,512]{1,0:T(8,128)(2,1)S(1)}, u32[]{:S(2)}, u32[]{:S(2)}) collective-permute-start(bf16[32,512]{1,0:T(8,128)(2,1)S(1)} %get-tuple-element.33), channel_id=1, source_target_pairs={{0,4},{4,0},{8,12},{12,8},{16,20},{20,16},{24,28},{28,24},{32,36},... | collective-permute-start | bytes 98312 | tf_op jit(solution)/shard_map/ppermute | solution.py:30
  5.7 4.6 %collective-permute-start.1 = (bf16[32,512]{1,0:T(8,128)(2,1)S(1)}, bf16[32,512]{1,0:T(8,128)(2,1)S(1)}, u32[]{:S(2)}, u32[]{:S(2)}) collective-permute-start(bf16[32,512]{1,0:T(8,128)(2,1)S(1)} %get-tuple-element.34), channel_id=1, source_target_pairs={{4,8},{8,4},{12,16},{16,12},{20,24},{24,20},{28,32},{32,28},{36,40... | collective-permute-start | bytes 98312 | tf_op jit(solution)/shard_map/ppermute | solution.py:30
  10.3 4.8 %all-to-all-start = ((bf16[4,8,512]{2,1,0:T(8,128)(2,1)}), bf16[4,8,512]{2,1,0:T(8,128)(2,1)S(1)}, u32[]{:S(2)}, u32[]{:S(2)}) async-start(bf16[4,8,512]{2,1,0:T(8,128)(2,1)} %bitcast.5), calls=%async_computation | async-start | bytes 65536 | tf_op jit(solution)/shard_map/all_to_all | solution.py:238
  15.2 1.9 %collective-permute-start.2 = (bf16[16,512]{1,0:T(8,128)(2,1)S(1)}, bf16[16,512]{1,0:T(8,128)(2,1)S(1)}, u32[]{:S(2)}, u32[]{:S(2)}) collective-permute-start(bf16[16,512]{1,0:T(8,128)(2,1)S(1)} %get-tuple-element.35), channel_id=1, source_target_pairs={{0,8},{8,0},{4,12},{12,4},{16,24},{24,16},{20,28},{28,20},{32,40},... | collective-permute-start | bytes 49160 | tf_op jit(solution)/shard_map/ppermute | solution.py:30
  17.1 4.6 %collective-permute-start.3 = (bf16[16,512]{1,0:T(8,128)(2,1)S(1)}, bf16[16,512]{1,0:T(8,128)(2,1)S(1)}, u32[]{:S(2)}, u32[]{:S(2)}) collective-permute-start(bf16[16,512]{1,0:T(8,128)(2,1)S(1)} %get-tuple-element.36), channel_id=1, source_target_pairs={{8,16},{16,8},{12,20},{20,12},{24,32},{32,24},{28,36},{36,28},{40,... | collective-permute-start | bytes 49160 | tf_op jit(solution)/shard_map/ppermute | solution.py:30
  21.7 0.0 copy-done.9
  21.7 0.0 copy-done.6
  21.7 0.0 copy-done.8
  21.7 0.0 copy-done.5
  21.7 0.0 copy-start.4
  21.7 0.9 %copy-done.4 = bf16[6,2,64,64]{3,2,1,0:T(8,128)(2,1)S(1)} copy-done((bf16[6,2,64,64]{3,2,1,0:T(8,128)(2,1)S(1)}, bf16[6,2,64,64]{3,2,1,0:T(8,128)(2,1)}, u32[]{:S(2)}) %copy-start.4) | copy-done | bytes 98328
  22.6 0.7 copy-done.14
  23.3 0.7 copy-done.15
  24.0 0.7 shard_map.150
  24.7 0.0 collective-permute-done.2.f1
  24.7 1.3 %collective-permute-done.3.f2 = bf16[16,512]{1,0:T(8,128)(2,1)S(1)} collective-permute-done((bf16[16,512]{1,0:T(8,128)(2,1)S(1)}, bf16[16,512]{1,0:T(8,128)(2,1)S(1)}, u32[]{:S(2)}, u32[]{:S(2)}) %collective-permute-start.3) | collective-permute-done | bytes 16416 | tf_op jit(solution)/shard_map/ppermute | solution.py:30
  26.0 0.0 all-to-all-done
  26.0 0.0 collective-permute-done.n1
  26.0 0.0 collective-permute-done.1.n2
  26.0 0.0 copy-done.1
  26.1 0.0 copy-done.2
  26.1 2.3 %shard_map.151 = (f32[512,128]{1,0:T(8,128)S(1)}, bf16[512,128]{1,0:T(8,128)(2,1)S(1)}, bf16[32,512]{1,0:T(8,128)(2,1)S(1)}, bf16[32,512]{1,0:T(8,128)(2,1)S(1)}...) custom-call(bf16[512,128]{1,0:T(8,128)(2,1)S(1)} %get-tuple-element.32.field_ref, ...), custom_call_target="tpu_custom_call" | custom-call | flops 318767104 | bytes 1404928 | tf_op jit(solution)/shard_map/pallas_call | solution.py:41
  28.4 1.9 %collective-permute-start.4 = (bf16[32,512]{1,0:T(8,128)(2,1)S(1)}, bf16[32,512]{1,0:T(8,128)(2,1)S(1)}, u32[]{:S(2)}, u32[]{:S(2)}) collective-permute-start(bf16[32,512]{1,0:T(8,128)(2,1)S(1)} %get-tuple-element.44), channel_id=1, source_target_pairs={{0,4},{4,0},{8,12},{12,8},{16,20},{20,16},{24,28},{28,24},{32,36},... | collective-permute-start | bytes 98312 | tf_op jit(solution)/shard_map/ppermute | solution.py:30
  30.3 4.7 %collective-permute-start.5 = (bf16[32,512]{1,0:T(8,128)(2,1)S(1)}, bf16[32,512]{1,0:T(8,128)(2,1)S(1)}, u32[]{:S(2)}, u32[]{:S(2)}) collective-permute-start(bf16[32,512]{1,0:T(8,128)(2,1)S(1)} %get-tuple-element.45), channel_id=1, source_target_pairs={{4,8},{8,4},{12,16},{16,12},{20,24},{24,20},{28,32},{32,28},{36,40... | collective-permute-start | bytes 98312 | tf_op jit(solution)/shard_map/ppermute | solution.py:30
  35.0 4.8 %all-to-all-start.1 = ((bf16[4,8,512]{2,1,0:T(8,128)(2,1)}), bf16[4,8,512]{2,1,0:T(8,128)(2,1)S(1)}, u32[]{:S(2)}, u32[]{:S(2)}) async-start(bf16[4,8,512]{2,1,0:T(8,128)(2,1)} %bitcast.10), calls=%async_computation.1 | async-start | bytes 65536 | tf_op jit(solution)/shard_map/all_to_all | solution.py:238
  39.8 1.9 %collective-permute-start.6 = (bf16[16,512]{1,0:T(8,128)(2,1)S(1)}, bf16[16,512]{1,0:T(8,128)(2,1)S(1)}, u32[]{:S(2)}, u32[]{:S(2)}) collective-permute-start(bf16[16,512]{1,0:T(8,128)(2,1)S(1)} %get-tuple-element.46), channel_id=1, source_target_pairs={{0,8},{8,0},{4,12},{12,4},{16,24},{24,16},{20,28},{28,20},{32,40},... | collective-permute-start | bytes 49160 | tf_op jit(solution)/shard_map/ppermute | solution.py:30
  41.7 1.9 %collective-permute-start.7 = (bf16[16,512]{1,0:T(8,128)(2,1)S(1)}, bf16[16,512]{1,0:T(8,128)(2,1)S(1)}, u32[]{:S(2)}, u32[]{:S(2)}) collective-permute-start(bf16[16,512]{1,0:T(8,128)(2,1)S(1)} %get-tuple-element.47), channel_id=1, source_target_pairs={{8,16},{16,8},{12,20},{20,12},{24,32},{32,24},{28,36},{36,28},{40,... | collective-permute-start | bytes 49160 | tf_op jit(solution)/shard_map/ppermute | solution.py:30
  43.6 1.8 %collective-permute-done.6.f1 = bf16[16,512]{1,0:T(8,128)(2,1)S(1)} collective-permute-done((bf16[16,512]{1,0:T(8,128)(2,1)S(1)}, bf16[16,512]{1,0:T(8,128)(2,1)S(1)}, u32[]{:S(2)}, u32[]{:S(2)}) %collective-permute-start.6) | collective-permute-done | bytes 16416 | tf_op jit(solution)/shard_map/ppermute | solution.py:30
  45.4 5.2 %collective-permute-done.7.f2 = bf16[16,512]{1,0:T(8,128)(2,1)S(1)} collective-permute-done((bf16[16,512]{1,0:T(8,128)(2,1)S(1)}, bf16[16,512]{1,0:T(8,128)(2,1)S(1)}, u32[]{:S(2)}, u32[]{:S(2)}) %collective-permute-start.7) | collective-permute-done | bytes 16416 | tf_op jit(solution)/shard_map/ppermute | solution.py:30
  50.7 0.0 all-to-all-done.1
  50.7 0.0 collective-permute-done.4.n1
  50.7 0.0 collective-permute-done.5.n2
  50.7 2.3 %shard_map.152 = (f32[512,128]{1,0:T(8,128)S(1)}, bf16[512,128]{1,0:T(8,128)(2,1)S(1)}, bf16[32,512]{1,0:T(8,128)(2,1)S(1)}, bf16[32,512]{1,0:T(8,128)(2,1)S(1)}...) custom-call(bf16[512,128]{1,0:T(8,128)(2,1)S(1)} %get-tuple-element.43.field_ref, ...), custom_call_target="tpu_custom_call" | custom-call | flops 318767104 | bytes 1404928 | tf_op jit(solution)/shard_map/pallas_call | solution.py:41
  53.0 1.9 %collective-permute-start.8 = (bf16[32,512]{1,0:T(8,128)(2,1)S(1)}, bf16[32,512]{1,0:T(8,128)(2,1)S(1)}, u32[]{:S(2)}, u32[]{:S(2)}) collective-permute-start(bf16[32,512]{1,0:T(8,128)(2,1)S(1)} %get-tuple-element.51), channel_id=1, source_target_pairs={{0,4},{4,0},{8,12},{12,8},{16,20},{20,16},{24,28},{28,24},{32,36},... | collective-permute-start | bytes 98312 | tf_op jit(solution)/shard_map/ppermute | solution.py:30
  54.9 2.5 %collective-permute-start.9 = (bf16[32,512]{1,0:T(8,128)(2,1)S(1)}, bf16[32,512]{1,0:T(8,128)(2,1)S(1)}, u32[]{:S(2)}, u32[]{:S(2)}) collective-permute-start(bf16[32,512]{1,0:T(8,128)(2,1)S(1)} %get-tuple-element.52), channel_id=1, source_target_pairs={{4,8},{8,4},{12,16},{16,12},{20,24},{24,20},{28,32},{32,28},{36,40... | collective-permute-start | bytes 98312 | tf_op jit(solution)/shard_map/ppermute | solution.py:30
  57.4 4.8 %all-to-all-start.2 = ((bf16[4,8,512]{2,1,0:T(8,128)(2,1)}), bf16[4,8,512]{2,1,0:T(8,128)(2,1)S(1)}, u32[]{:S(2)}, u32[]{:S(2)}) async-start(bf16[4,8,512]{2,1,0:T(8,128)(2,1)} %bitcast.12), calls=%async_computation.2 | async-start | bytes 65536 | tf_op jit(solution)/shard_map/all_to_all | solution.py:238
  62.2 3.5 %collective-permute-start.10 = (bf16[16,512]{1,0:T(8,128)(2,1)S(1)}, bf16[16,512]{1,0:T(8,128)(2,1)S(1)}, u32[]{:S(2)}, u32[]{:S(2)}) collective-permute-start(bf16[16,512]{1,0:T(8,128)(2,1)S(1)} %get-tuple-element.53), channel_id=1, source_target_pairs={{0,8},{8,0},{4,12},{12,4},{16,24},{24,16},{20,28},{28,20},{32,40},... | collective-permute-start | bytes 49160 | tf_op jit(solution)/shard_map/ppermute | solution.py:30
  65.7 1.9 %collective-permute-start.11 = (bf16[16,512]{1,0:T(8,128)(2,1)S(1)}, bf16[16,512]{1,0:T(8,128)(2,1)S(1)}, u32[]{:S(2)}, u32[]{:S(2)}) collective-permute-start(bf16[16,512]{1,0:T(8,128)(2,1)S(1)} %get-tuple-element.54), channel_id=1, source_target_pairs={{8,16},{16,8},{12,20},{20,12},{24,32},{32,24},{28,36},{36,28},{40,... | collective-permute-start | bytes 49160 | tf_op jit(solution)/shard_map/ppermute | solution.py:30
  67.6 0.2 collective-permute-done.10.f1
  67.8 6.8 %collective-permute-done.11.f2 = bf16[16,512]{1,0:T(8,128)(2,1)S(1)} collective-permute-done((bf16[16,512]{1,0:T(8,128)(2,1)S(1)}, bf16[16,512]{1,0:T(8,128)(2,1)S(1)}, u32[]{:S(2)}, u32[]{:S(2)}) %collective-permute-start.11) | collective-permute-done | bytes 16416 | tf_op jit(solution)/shard_map/ppermute | solution.py:30
  74.6 0.0 all-to-all-done.2
  74.6 0.0 collective-permute-done.8.n1
  74.6 0.0 collective-permute-done.9.n2
  74.6 0.0 copy-start.7
  74.7 1.8 %shard_map.153 = (f32[512,128]{1,0:T(8,128)}, bf16[512,128]{1,0:T(8,128)(2,1)S(1)}, bf16[512,128]{1,0:T(8,128)(2,1)S(1)}, bf16[16,512]{1,0:T(8,128)(2,1)S(1)}) custom-call(bf16[512,128]{1,0:T(8,128)(2,1)S(1)} %get-tuple-element.50.field_ref, bf16[32,512]{1,0:T(8,128)(2,1)S(1)} %collective-permute-done.8.n1, bf16[32,512]{1,0:T(8,128)(2,1)S(1)} %collective-permute-done.9.n2, ...), custom_call_target="tpu_custom_call" | custom-call | flops 318767104 | bytes 1126400 | tf_op jit(solution)/shard_map/pallas_call | solution.py:41
  76.4 1.9 %collective-permute-start.12 = (bf16[16,512]{1,0:T(8,128)(2,1)S(1)}, bf16[16,512]{1,0:T(8,128)(2,1)S(1)}, u32[]{:S(2)}, u32[]{:S(2)}) collective-permute-start(bf16[16,512]{1,0:T(8,128)(2,1)S(1)} %get-tuple-element.59), channel_id=1, source_target_pairs={{0,1},{1,0},{2,3},{3,2},{4,5},{5,4},{6,7},{7,6},{8,9},{9,8},{10,11... | collective-permute-start | bytes 49160 | tf_op jit(solution)/shard_map/ppermute | solution.py:30
  78.3 3.7 %collective-permute-done.12.incoming = bf16[16,512]{1,0:T(8,128)(2,1)S(1)} collective-permute-done((bf16[16,512]{1,0:T(8,128)(2,1)S(1)}, bf16[16,512]{1,0:T(8,128)(2,1)S(1)}, u32[]{:S(2)}, u32[]{:S(2)}) %collective-permute-start.12) | collective-permute-done | bytes 16416 | tf_op jit(solution)/shard_map/ppermute | solution.py:30
  82.0 0.0 copy-done.7
  82.0 0.9 %copy-done.3 = f32[512,128]{1,0:T(8,128)S(1)} copy-done((f32[512,128]{1,0:T(8,128)S(1)}, f32[512,128]{1,0:T(8,128)}, u32[]{:S(2)}) %copy-start.3) | copy-done | bytes 262168
  83.0 1.1 %shard_map.154 = f32[512,128]{1,0:T(8,128)} custom-call(f32[512,128]{1,0:T(8,128)S(1)} %copy-done.3, bf16[512,128]{1,0:T(8,128)(2,1)S(1)} %get-tuple-element.57.rounded_ref, bf16[512,128]{1,0:T(8,128)(2,1)S(1)} %get-tuple-element.58.rest_ref, bf16[16,512]{1,0:T(8,128)(2,1)S(1)} %collective-permute-done.12.incoming, ...), custom_call_target="tpu_custom_call" | custom-call | flops 79691776 | bytes 847872 | tf_op jit(solution)/shard_map/pallas_call | solution.py:41
  (7 shorter events, 0.0 us)
Async XLA Ops:
  0.6 0.7 copy-start.13
  0.6 21.0 %copy-start.9 = (s32[6,128]{1,0:T(8,128)S(1)}, s32[6,128]{1,0:T(8,128)}, u32[]{:S(2)}) copy-start(s32[6,128]{1,0:T(8,128)} %neighbours.1) | copy-start | bytes 9220
  0.7 0.7 copy-start.10
  0.7 0.7 copy-start.11
  0.7 21.0 %copy-start.6 = (bf16[2,64,64]{2,1,0:T(8,128)(2,1)S(1)}, bf16[2,64,64]{2,1,0:T(8,128)(2,1)}, u32[]{:S(2)}) copy-start(bf16[2,64,64]{2,1,0:T(8,128)(2,1)} %smooth.1) | copy-start | bytes 49156
  0.7 21.0 %copy-start.8 = (s32[6,128]{1,0:T(8,128)S(1)}, s32[6,128]{1,0:T(8,128)}, u32[]{:S(2)}) copy-start(s32[6,128]{1,0:T(8,128)} %face_type.1) | copy-start | bytes 9220
  0.7 21.0 %copy-start.5 = (bf16[2,64,64]{2,1,0:T(8,128)(2,1)S(1)}, bf16[2,64,64]{2,1,0:T(8,128)(2,1)}, u32[]{:S(2)}) copy-start(bf16[2,64,64]{2,1,0:T(8,128)(2,1)} %diag.1) | copy-start | bytes 49156
  0.8 0.7 copy-start.12
  1.5 0.9 %copy-start = (f32[64,8,128]{2,1,0:T(8,128)S(1)}, f32[64,8,128]{2,1,0:T(8,128)}, u32[]{:S(2)}) copy-start(f32[64,8,128]{2,1,0:T(8,128)} %param.15) | copy-start | bytes 786436
  2.4 23.6 %copy-start.1 = (f32[64,8,128]{2,1,0:T(8,128)S(1)}, f32[64,8,128]{2,1,0:T(8,128)}, u32[]{:S(2)}) copy-start(f32[64,8,128]{2,1,0:T(8,128)} %param.15) | copy-start | bytes 786436
  2.4 23.6 %copy-start.2 = (f32[64,8,128]{2,1,0:T(8,128)S(1)}, f32[64,8,128]{2,1,0:T(8,128)}, u32[]{:S(2)}) copy-start(f32[64,8,128]{2,1,0:T(8,128)} %param.14) | copy-start | bytes 786436
  3.8 22.2 %collective-permute-start = (bf16[32,512]{1,0:T(8,128)(2,1)S(1)}, bf16[32,512]{1,0:T(8,128)(2,1)S(1)}, u32[]{:S(2)}, u32[]{:S(2)}) collective-permute-start(bf16[32,512]{1,0:T(8,128)(2,1)S(1)} %get-tuple-element.33), channel_id=1, source_target_pairs={{0,4},{4,0},{8,12},{12,8},{16,20},{20,16},{24,28},{28,24},{32,36},... | collective-permute-start | bytes 98312 | tf_op jit(solution)/shard_map/ppermute | solution.py:30
  5.7 20.3 %collective-permute-start.1 = (bf16[32,512]{1,0:T(8,128)(2,1)S(1)}, bf16[32,512]{1,0:T(8,128)(2,1)S(1)}, u32[]{:S(2)}, u32[]{:S(2)}) collective-permute-start(bf16[32,512]{1,0:T(8,128)(2,1)S(1)} %get-tuple-element.34), channel_id=1, source_target_pairs={{4,8},{8,4},{12,16},{16,12},{20,24},{24,20},{28,32},{32,28},{36,40... | collective-permute-start | bytes 98312 | tf_op jit(solution)/shard_map/ppermute | solution.py:30
  10.3 15.7 %all-to-all-start = ((bf16[4,8,512]{2,1,0:T(8,128)(2,1)}), bf16[4,8,512]{2,1,0:T(8,128)(2,1)S(1)}, u32[]{:S(2)}, u32[]{:S(2)}) async-start(bf16[4,8,512]{2,1,0:T(8,128)(2,1)} %bitcast.5), calls=%async_computation | async-start | bytes 65536 | tf_op jit(solution)/shard_map/all_to_all | solution.py:238
  15.2 9.5 %collective-permute-start.2 = (bf16[16,512]{1,0:T(8,128)(2,1)S(1)}, bf16[16,512]{1,0:T(8,128)(2,1)S(1)}, u32[]{:S(2)}, u32[]{:S(2)}) collective-permute-start(bf16[16,512]{1,0:T(8,128)(2,1)S(1)} %get-tuple-element.35), channel_id=1, source_target_pairs={{0,8},{8,0},{4,12},{12,4},{16,24},{24,16},{20,28},{28,20},{32,40},... | collective-permute-start | bytes 49160 | tf_op jit(solution)/shard_map/ppermute | solution.py:30
  17.1 9.0 %collective-permute-start.3 = (bf16[16,512]{1,0:T(8,128)(2,1)S(1)}, bf16[16,512]{1,0:T(8,128)(2,1)S(1)}, u32[]{:S(2)}, u32[]{:S(2)}) collective-permute-start(bf16[16,512]{1,0:T(8,128)(2,1)S(1)} %get-tuple-element.36), channel_id=1, source_target_pairs={{8,16},{16,8},{12,20},{20,12},{24,32},{32,24},{28,36},{36,28},{40,... | collective-permute-start | bytes 49160 | tf_op jit(solution)/shard_map/ppermute | solution.py:30
  21.7 0.9 %copy-start.4 = (bf16[6,2,64,64]{3,2,1,0:T(8,128)(2,1)S(1)}, bf16[6,2,64,64]{3,2,1,0:T(8,128)(2,1)}, u32[]{:S(2)}) copy-start(bf16[6,2,64,64]{3,2,1,0:T(8,128)(2,1)} %face.1) | copy-start | bytes 294916
  22.6 0.7 copy-start.14
  23.3 0.7 copy-start.15
  28.4 22.3 %collective-permute-start.4 = (bf16[32,512]{1,0:T(8,128)(2,1)S(1)}, bf16[32,512]{1,0:T(8,128)(2,1)S(1)}, u32[]{:S(2)}, u32[]{:S(2)}) collective-permute-start(bf16[32,512]{1,0:T(8,128)(2,1)S(1)} %get-tuple-element.44), channel_id=1, source_target_pairs={{0,4},{4,0},{8,12},{12,8},{16,20},{20,16},{24,28},{28,24},{32,36},... | collective-permute-start | bytes 98312 | tf_op jit(solution)/shard_map/ppermute | solution.py:30
  30.3 20.4 %collective-permute-start.5 = (bf16[32,512]{1,0:T(8,128)(2,1)S(1)}, bf16[32,512]{1,0:T(8,128)(2,1)S(1)}, u32[]{:S(2)}, u32[]{:S(2)}) collective-permute-start(bf16[32,512]{1,0:T(8,128)(2,1)S(1)} %get-tuple-element.45), channel_id=1, source_target_pairs={{4,8},{8,4},{12,16},{16,12},{20,24},{24,20},{28,32},{32,28},{36,40... | collective-permute-start | bytes 98312 | tf_op jit(solution)/shard_map/ppermute | solution.py:30
  35.0 15.7 %all-to-all-start.1 = ((bf16[4,8,512]{2,1,0:T(8,128)(2,1)}), bf16[4,8,512]{2,1,0:T(8,128)(2,1)S(1)}, u32[]{:S(2)}, u32[]{:S(2)}) async-start(bf16[4,8,512]{2,1,0:T(8,128)(2,1)} %bitcast.10), calls=%async_computation.1 | async-start | bytes 65536 | tf_op jit(solution)/shard_map/all_to_all | solution.py:238
  39.8 5.6 %collective-permute-start.6 = (bf16[16,512]{1,0:T(8,128)(2,1)S(1)}, bf16[16,512]{1,0:T(8,128)(2,1)S(1)}, u32[]{:S(2)}, u32[]{:S(2)}) collective-permute-start(bf16[16,512]{1,0:T(8,128)(2,1)S(1)} %get-tuple-element.46), channel_id=1, source_target_pairs={{0,8},{8,0},{4,12},{12,4},{16,24},{24,16},{20,28},{28,20},{32,40},... | collective-permute-start | bytes 49160 | tf_op jit(solution)/shard_map/ppermute | solution.py:30
  41.7 9.0 %collective-permute-start.7 = (bf16[16,512]{1,0:T(8,128)(2,1)S(1)}, bf16[16,512]{1,0:T(8,128)(2,1)S(1)}, u32[]{:S(2)}, u32[]{:S(2)}) collective-permute-start(bf16[16,512]{1,0:T(8,128)(2,1)S(1)} %get-tuple-element.47), channel_id=1, source_target_pairs={{8,16},{16,8},{12,20},{20,12},{24,32},{32,24},{28,36},{36,28},{40,... | collective-permute-start | bytes 49160 | tf_op jit(solution)/shard_map/ppermute | solution.py:30
  53.0 21.6 %collective-permute-start.8 = (bf16[32,512]{1,0:T(8,128)(2,1)S(1)}, bf16[32,512]{1,0:T(8,128)(2,1)S(1)}, u32[]{:S(2)}, u32[]{:S(2)}) collective-permute-start(bf16[32,512]{1,0:T(8,128)(2,1)S(1)} %get-tuple-element.51), channel_id=1, source_target_pairs={{0,4},{4,0},{8,12},{12,8},{16,20},{20,16},{24,28},{28,24},{32,36},... | collective-permute-start | bytes 98312 | tf_op jit(solution)/shard_map/ppermute | solution.py:30
  54.9 19.7 %collective-permute-start.9 = (bf16[32,512]{1,0:T(8,128)(2,1)S(1)}, bf16[32,512]{1,0:T(8,128)(2,1)S(1)}, u32[]{:S(2)}, u32[]{:S(2)}) collective-permute-start(bf16[32,512]{1,0:T(8,128)(2,1)S(1)} %get-tuple-element.52), channel_id=1, source_target_pairs={{4,8},{8,4},{12,16},{16,12},{20,24},{24,20},{28,32},{32,28},{36,40... | collective-permute-start | bytes 98312 | tf_op jit(solution)/shard_map/ppermute | solution.py:30
  57.4 17.2 %all-to-all-start.2 = ((bf16[4,8,512]{2,1,0:T(8,128)(2,1)}), bf16[4,8,512]{2,1,0:T(8,128)(2,1)S(1)}, u32[]{:S(2)}, u32[]{:S(2)}) async-start(bf16[4,8,512]{2,1,0:T(8,128)(2,1)} %bitcast.12), calls=%async_computation.2 | async-start | bytes 65536 | tf_op jit(solution)/shard_map/all_to_all | solution.py:238
  62.2 5.6 %collective-permute-start.10 = (bf16[16,512]{1,0:T(8,128)(2,1)S(1)}, bf16[16,512]{1,0:T(8,128)(2,1)S(1)}, u32[]{:S(2)}, u32[]{:S(2)}) collective-permute-start(bf16[16,512]{1,0:T(8,128)(2,1)S(1)} %get-tuple-element.53), channel_id=1, source_target_pairs={{0,8},{8,0},{4,12},{12,4},{16,24},{24,16},{20,28},{28,20},{32,40},... | collective-permute-start | bytes 49160 | tf_op jit(solution)/shard_map/ppermute | solution.py:30
  65.7 9.0 %collective-permute-start.11 = (bf16[16,512]{1,0:T(8,128)(2,1)S(1)}, bf16[16,512]{1,0:T(8,128)(2,1)S(1)}, u32[]{:S(2)}, u32[]{:S(2)}) collective-permute-start(bf16[16,512]{1,0:T(8,128)(2,1)S(1)} %get-tuple-element.54), channel_id=1, source_target_pairs={{8,16},{16,8},{12,20},{20,12},{24,32},{32,24},{28,36},{36,28},{40,... | collective-permute-start | bytes 49160 | tf_op jit(solution)/shard_map/ppermute | solution.py:30
  74.6 7.4 %copy-start.7 = (bf16[64,64]{1,0:T(8,128)(2,1)S(1)}, bf16[64,64]{1,0:T(8,128)(2,1)}, u32[]{:S(2)}) copy-start(bf16[64,64]{1,0:T(8,128)(2,1)} %inverse.1) | copy-start | bytes 24580
  76.4 5.6 %collective-permute-start.12 = (bf16[16,512]{1,0:T(8,128)(2,1)S(1)}, bf16[16,512]{1,0:T(8,128)(2,1)S(1)}, u32[]{:S(2)}, u32[]{:S(2)}) collective-permute-start(bf16[16,512]{1,0:T(8,128)(2,1)S(1)} %get-tuple-element.59), channel_id=1, source_target_pairs={{0,1},{1,0},{2,3},{3,2},{4,5},{5,4},{6,7},{7,6},{8,9},{9,8},{10,11... | collective-permute-start | bytes 49160 | tf_op jit(solution)/shard_map/ppermute | solution.py:30
  82.0 1.0 %copy-start.3 = (f32[512,128]{1,0:T(8,128)S(1)}, f32[512,128]{1,0:T(8,128)}, u32[]{:S(2)}) copy-start(f32[512,128]{1,0:T(8,128)} %get-tuple-element.56.residual_ref) | copy-start | bytes 786436

commit v2 on v1

--- a/solution.py
+++ b/solution.py
@@ -17,6 +17,7 @@
 F32 = jnp.float32
 
 SPLIT = (32, 32, 16, 16, 32)
+SENT = (32, 48, 16, 48, 32)
 HALO = sum(SPLIT)
 PAIRS = 16
 
@@ -67,16 +68,16 @@
 def send(choice, field, refs):
     rows = lax.dot_general(choice, field, (((1,), (1,)), ((), ())), preferred_element_type=F32).astype(BF)
     start = 0
-    for ref in refs:
-        ref[...] = rows[start : start + ref.shape[0]]
-        start += ref.shape[0]
-
-
-def pack_kernel(odd_ref, guess, near, far, sub, pair, field_ref, choice_ref, *messages):
+    for ref, used in refs:
+        ref[:used] = rows[start : start + used]
+        if ref.shape[0] > used:
+            ref[used:] = jnp.zeros((ref.shape[0] - used, ROWS), BF)
+        start += used
+
+
+def pack_kernel(odd_ref, guess, near, far, sub, field_ref, choice_ref, *messages):
     odd_core = odd_ref[0] == 1
     odd_chip = odd_ref[1] == 1
-    for r in range(RHS):
-        field_ref[r * DOF : (r + 1) * DOF, :] = guess[pl.ds(r, DOF, stride=RHS), :].astype(BF)
     lower, higher = near[0:1, :], near[1:2, :]
     far_lower, far_higher = far[0:1, :], far[1:2, :]
     blank = jnp.zeros((8, E), BF)
@@ -93,15 +94,16 @@
             side,
             side,
             side,
-            picker(pair[...]),
         ],
         axis=0,
     )
     choice_ref[...] = choice
-    send(choice[:HALO], field_ref[...], messages)
-
-
-def prep_kernel(odd_ref, diag, face, smooth, elem_type, face_type, neighbours, partner, pick_ref, mask_ref, wide_ref, smooth_ref, mate_ref):
+    for r in range(RHS):
+        field_ref[r * DOF : (r + 1) * DOF, :] = guess[pl.ds(r, DOF, stride=RHS), :].astype(BF)
+    send(choice, field_ref[...], zip(messages, SPLIT))
+
+
+def prep_kernel(odd_ref, diag, face, smooth, neighbours, face_type, elem_type, pick_ref, mask_ref, wide_ref, smooth_ref):
     odd_core = odd_ref[0]
     odd_chip = odd_ref[1]
     for d in range(FACES):
@@ -122,10 +124,9 @@
         for t in range(2):
             mask = jnp.where(jnp.broadcast_to(kinds, (16, E)) == t, 1.0, 0.0)
             mask_ref[2 * d + t] = mask.astype(BF)
-        pair = (diag[0], diag[1]) if d == 0 else (face[d - 1, 0], face[d - 1, 1])
-        wide_ref[:, d * 2 * DOF : (d + 1) * 2 * DOF] = jnp.concatenate(pair, axis=1)
+        both = (diag[0], diag[1]) if d == 0 else (face[d - 1, 0], face[d - 1, 1])
+        wide_ref[:, d * 2 * DOF : (d + 1) * 2 * DOF] = jnp.concatenate(both, axis=1)
     smooth_ref[...] = jnp.concatenate([smooth[0], smooth[1]], axis=1)
-    mate_ref[...] = jnp.where(iota((E + PAIRS, E), 0) == partner[...], 1.0, 0.0).astype(BF)
 
 
 def masked(block, mask):
@@ -134,11 +135,10 @@
 
 
 def residual_of(field_ref, halo, pick, masks, wide, rhs, take):
-    near = jnp.concatenate([ref[...] for ref in halo], axis=0)
+    near = jnp.concatenate([ref[:used] for ref, used in zip(halo, SPLIT)], axis=0)
     field = field_ref[...]
-    beside = jnp.dot(field, pick[:E, :], preferred_element_type=F32)
-    beside = beside + lax.dot_general(near, pick[E:, :], (((0,), (0,)), ((), ())), preferred_element_type=F32)
-    beside = beside.astype(BF)
+    extended = jnp.concatenate([field, near.T], axis=1)
+    beside = jnp.dot(extended, pick[...], preferred_element_type=F32).astype(BF)
     for r in range(0, RHS, 2):
         halves = []
         for s in (r, r + 1):
@@ -152,7 +152,7 @@
         take(r, right - product)
 
 
-def sweep_kernel(first, field_ref, n1, n2, f1, f2, side, pick, masks, wide, smooth, rhs, before, choice, after, next_field, *messages):
+def sweep_kernel(first, field_ref, f2, n2, f1, n1, side, pick, masks, wide, smooth, rhs, before, choice, after, next_field, *messages):
     def take(r, residual):
         rounded = residual.astype(BF)
         halves = []
@@ -169,34 +169,41 @@
             next_field[rows, :] = new.astype(BF)
 
     residual_of(field_ref, (n1, n2, f1, f2, side), pick, masks, wide, rhs, take)
-    send(choice[:HALO, :], next_field[...], messages)
-
-
-def residual_kernel(field_ref, n1, n2, f1, f2, side, pick, masks, wide, rhs, choice, residual_ref, rounded_ref, rest_ref, message):
+    send(choice[...], next_field[...], zip(messages, SPLIT))
+
+
+def residual_kernel(field_ref, f2, n2, f1, n1, side, pick, masks, wide, rhs, pair, residual_ref, rounded_ref, message):
     def take(r, residual):
         for i in range(2):
-            s = r + i
+            rows = slice((r + i) * DOF, (r + i + 1) * DOF)
             part = residual[:, i * E : (i + 1) * E]
-            residual_ref[pl.ds(s, DOF, stride=RHS), :] = part
-            rounded = part.astype(BF)
-            rounded_ref[s * DOF : (s + 1) * DOF, :] = rounded
-            rest_ref[s * DOF : (s + 1) * DOF, :] = (part - rounded.astype(F32)).astype(BF)
+            residual_ref[rows, :] = part
+            rounded_ref[rows, :] = part.astype(BF)
 
     residual_of(field_ref, (n1, n2, f1, f2, side), pick, masks, wide, rhs, take)
-    send(choice[HALO:, :], rounded_ref[...], (message,))
-
-
-def coarse_kernel(residual_ref, rounded_ref, rest_ref, incoming, mate, inverse, iterate, solution_ref):
-    local = mate[:E, :]
+    send(picker(pair[...]), rounded_ref[...], [(message, PAIRS)])
+
+
+def mate_picker(partner, first, count):
+    return jnp.where(iota((count, E), 0) + first == partner, 1.0, 0.0).astype(BF)
+
+
+def local_kernel(residual_ref, rounded_ref, partner, out_ref, half_ref):
+    rest = (residual_ref[...] - rounded_ref[...].astype(F32)).astype(BF)
+    local = mate_picker(partner[...], 0, E)
     mates = jnp.dot(rounded_ref[...], local, preferred_element_type=F32)
-    mates = mates + jnp.dot(rest_ref[...], local, preferred_element_type=F32)
-    mates = mates + lax.dot_general(incoming[...], mate[E:, :], (((0,), (0,)), ((), ())), preferred_element_type=F32)
+    mates = mates + jnp.dot(rest, local, preferred_element_type=F32)
+    half_ref[...] = residual_ref[...] + mates
+    for r in range(RHS):
+        out_ref[pl.ds(r, DOF, stride=RHS), :] = residual_ref[r * DOF : (r + 1) * DOF, :]
+
+
+def coarse_kernel(half_ref, incoming, partner, inverse, iterate, solution_ref):
+    mates = lax.dot_general(incoming[...], mate_picker(partner[...], E, PAIRS), (((0,), (0,)), ((), ())), preferred_element_type=F32)
+    coarse = (half_ref[...] + mates).astype(BF)
     for r in range(0, RHS, 2):
-        halves = []
-        for s in (r, r + 1):
-            coarse = residual_ref[pl.ds(s, DOF, stride=RHS), :] + mates[s * DOF : (s + 1) * DOF, :]
-            halves.append(coarse.astype(BF))
-        update = jnp.dot(inverse[...], jnp.concatenate(halves, axis=1), preferred_element_type=F32)
+        pair = jnp.concatenate([coarse[s * DOF : (s + 1) * DOF, :] for s in (r, r + 1)], axis=1)
+        update = jnp.dot(inverse[...], pair, preferred_element_type=F32)
         for i in range(2):
             s = r + i
             solution_ref[pl.ds(s, DOF, stride=RHS), :] = iterate[s * DOF : (s + 1) * DOF, :] + update[:, i * E : (i + 1) * E]
@@ -230,45 +237,41 @@
 
     def exchange(messages):
         n1, n2, f1, f2, side = messages
-        return (
-            swap(n1, "dom", inside),
-            swap(n2, "dom", across),
-            swap(f1, "dom", far_one),
-            swap(f2, "dom", far_two),
-            lax.all_to_all(side, "sub", 0, 0, tiled=True),
-        )
-
-    message_outs = [((n, ROWS), BF) for n in SPLIT]
+        f2 = swap(f2, "dom", far_two)
+        n2 = swap(n2, "dom", across)
+        f1 = swap(f1, "dom", far_one)
+        n1 = swap(n1, "dom", inside)
+        side = lax.all_to_all(side, "sub", 0, 0, tiled=True)
+        return f2, n2, f1, n1, side
+
+    message_outs = [((n, ROWS), BF) for n in SENT]
     field, choice, *messages = call(
         pack_kernel,
-        [((ROWS, E), BF), ((HALO + PAIRS, E), BF)] + message_outs,
+        [((ROWS, E), BF), ((HALO, E), BF)] + message_outs,
         odd,
         guess,
         send_near,
         send_far,
         sub_send.reshape(1, -1),
-        pair_send.reshape(1, -1),
         flops=2 * HALO * E * ROWS,
         scalars=1,
     )
     halo = exchange(messages)
-    pick, masks, wide, smooth, mate = call(
+    pick, masks, wide, smooth = call(
         prep_kernel,
         [
             ((E + HALO, FACES * E), BF),
             ((2 * FACES + 2, 16, E), BF),
             ((DOF, 2 * DOF * (FACES + 1)), BF),
             ((DOF, 2 * DOF), BF),
-            ((E + PAIRS, E), BF),
         ],
         odd,
         diag_blocks,
         face_blocks,
         smoother,
+        neighbours,
+        face_type,
         elem_type.reshape(1, -1),
-        face_type,
-        neighbours,
-        partner.reshape(1, -1),
         flops=1000000,
         scalars=1,
     )
@@ -290,28 +293,34 @@
             flops=work,
         )
         halo = exchange(messages)
-    residual, rounded, rest, message = call(
+    residual, rounded, message = call(
         residual_kernel,
-        [((ROWS, E), F32), ((ROWS, E), BF), ((ROWS, E), BF), ((PAIRS, ROWS), BF)],
+        [((ROWS, E), F32), ((ROWS, E), BF), ((PAIRS, ROWS), BF)],
         field,
         *halo,
         pick,
         masks,
         wide,
         rhs,
-        choice,
+        pair_send.reshape(1, -1),
         flops=work,
     )
     subs = lax.axis_size("sub")
     incoming = swap(message, "sub", [(i, i + 1) for i in range(0, subs, 2)])
+    residual, half = call(
+        local_kernel,
+        [((ROWS, E), F32), ((ROWS, E), F32)],
+        residual,
+        rounded,
+        partner.reshape(1, -1),
+        flops=work // 4,
+    )
     (solved,) = call(
         coarse_kernel,
         [((ROWS, E), F32)],
-        residual,
-        rounded,
-        rest,
+        half,
         incoming,
-        mate,
+        partner.reshape(1, -1),
         coarse_inverse,
         iterate,
         flops=work // 4,

time: 84.9 us -> 82 us (0.966)
  the two profiles are of different devices: /device:TPU:258 before, /device:TPU:250 now
where the time goes in v2:
time: 82 us; the launch traced here: 81.2 us
  starting transfers between devices  55.6 us (68%)
  waiting for transfers between devices  11 us (13%)
  Pallas kernels  9.06 us (11%)
  local copies, waits for them, and re-layouts  4.51 us (6%)
  between operations  0.95 us (1%)
    ppermute x13, starting transfers between devices, swap(): return lax.ppermute(array, axis, route)  41.2 us
    all_to_all x3, starting transfers between devices, exchange(): side = lax.all_to_all(side, 'sub', 0, 0, tiled=True)  14.5 us
    ppermute x13, waiting for transfers between devices, swap(): return lax.ppermute(array, axis, route)  11 us
    pallas_call x7, Pallas kernels, call(): pl.pallas_call(kernel, out_shape=[jax.ShapeDtypeStruct(s, d) for s, d in...  9.06 us
    unnamed x30, local copies, waits for them, and re-layouts  4.51 us
  transfers between devices with their start and end apart: 16, of which 4 were waited for; matrix products, arithmetic and copies ran while one was open for 0% of the time, Pallas kernels for 2%

profile of v2, /device:TPU:250, one launch (start us, length us, event | category | flops | bytes accessed | tf_op | source)
XLA Modules:
  0.0 81.2 jit_solution(7757922873002873377)
XLA Ops:
  0.6 0.0 copy-start.8
  0.6 0.0 copy-start.10
  0.7 0.0 copy-start.11
  0.7 0.0 copy-start.5
  0.7 0.0 copy-start.7
  0.7 0.0 copy-start.4
  0.7 0.1 pad_add_fusion.odd_ref
  0.8 0.5 copy-done.10
  1.3 0.0 copy-done.11
  1.3 0.1 copy-done.12
  1.5 0.9 %copy-done = f32[64,8,128]{2,1,0:T(8,128)S(1)} copy-done((f32[64,8,128]{2,1,0:T(8,128)S(1)}, f32[64,8,128]{2,1,0:T(8,128)}, u32[]{:S(2)}) %copy-start) | copy-done | bytes 262168
  2.4 1.4 %shard_map.149 = (bf16[512,128]{1,0:T(8,128)(2,1)S(1)}, bf16[128,128]{1,0:T(8,128)(2,1)S(1)}, bf16[32,512]{1,0:T(8,128)(2,1)S(1)}, bf16[48,512]{1,0:T(8,128)(2,1...) custom-call(s32[2]{0:T(128)S(1)} %pad_add_fusion.odd_ref, ...), custom_call_target="tpu_custom_call" | custom-call | flops 16777216 | bytes 262504 | tf_op jit(solution)/shard_map/pallas_call | solution.py:42
  3.8 4.7 %collective-permute-start = (bf16[48,512]{1,0:T(8,128)(2,1)S(1)}, bf16[48,512]{1,0:T(8,128)(2,1)S(1)}, u32[]{:S(2)}, u32[]{:S(2)}) collective-permute-start(bf16[48,512]{1,0:T(8,128)(2,1)S(1)} %get-tuple-element.33), channel_id=1, source_target_pairs={{8,16},{16,8},{12,20},{20,12},{24,32},{32,24},{28,36},{36,28},{40,... | collective-permute-start | bytes 147464 | tf_op jit(solution)/shard_map/ppermute | solution.py:31
  8.5 1.9 %collective-permute-start.1 = (bf16[48,512]{1,0:T(8,128)(2,1)S(1)}, bf16[48,512]{1,0:T(8,128)(2,1)S(1)}, u32[]{:S(2)}, u32[]{:S(2)}) collective-permute-start(bf16[48,512]{1,0:T(8,128)(2,1)S(1)} %get-tuple-element.34), channel_id=1, source_target_pairs={{4,8},{8,4},{12,16},{16,12},{20,24},{24,20},{28,32},{32,28},{36,40... | collective-permute-start | bytes 147464 | tf_op jit(solution)/shard_map/ppermute | solution.py:31
  10.4 4.6 %collective-permute-start.3 = (bf16[32,512]{1,0:T(8,128)(2,1)S(1)}, bf16[32,512]{1,0:T(8,128)(2,1)S(1)}, u32[]{:S(2)}, u32[]{:S(2)}) collective-permute-start(bf16[32,512]{1,0:T(8,128)(2,1)S(1)} %get-tuple-element.36), channel_id=1, source_target_pairs={{0,4},{4,0},{8,12},{12,8},{16,20},{20,16},{24,28},{28,24},{32,36},... | collective-permute-start | bytes 98312 | tf_op jit(solution)/shard_map/ppermute | solution.py:31
  15.0 4.8 %all-to-all-start = ((bf16[4,8,512]{2,1,0:T(8,128)(2,1)}), bf16[4,8,512]{2,1,0:T(8,128)(2,1)S(1)}, u32[]{:S(2)}, u32[]{:S(2)}) async-start(bf16[4,8,512]{2,1,0:T(8,128)(2,1)} %bitcast.4), calls=%async_computation | async-start | bytes 65536 | tf_op jit(solution)/shard_map/all_to_all | solution.py:244
  19.9 1.9 %collective-permute-start.2 = (bf16[16,512]{1,0:T(8,128)(2,1)S(1)}, bf16[16,512]{1,0:T(8,128)(2,1)S(1)}, u32[]{:S(2)}, u32[]{:S(2)}) collective-permute-start(bf16[16,512]{1,0:T(8,128)(2,1)S(1)} %get-tuple-element.35), channel_id=1, source_target_pairs={{0,8},{8,0},{4,12},{12,4},{16,24},{24,16},{20,28},{28,20},{32,40},... | collective-permute-start | bytes 49160 | tf_op jit(solution)/shard_map/ppermute | solution.py:31
  21.8 0.0 copy-done.8
  21.8 0.0 copy-done.5
  21.8 0.0 copy-done.7
  21.8 0.0 copy-done.4
  21.8 0.0 copy-start.3
  21.8 0.9 %copy-done.3 = bf16[6,2,64,64]{3,2,1,0:T(8,128)(2,1)S(1)} copy-done((bf16[6,2,64,64]{3,2,1,0:T(8,128)(2,1)S(1)}, bf16[6,2,64,64]{3,2,1,0:T(8,128)(2,1)}, u32[]{:S(2)}) %copy-start.3) | copy-done | bytes 98328
  22.7 0.7 copy-done.13
  23.4 0.7 shard_map.150
  24.1 1.3 %collective-permute-done.2.f1 = bf16[16,512]{1,0:T(8,128)(2,1)S(1)} collective-permute-done((bf16[16,512]{1,0:T(8,128)(2,1)S(1)}, bf16[16,512]{1,0:T(8,128)(2,1)S(1)}, u32[]{:S(2)}, u32[]{:S(2)}) %collective-permute-start.2) | collective-permute-done | bytes 16416 | tf_op jit(solution)/shard_map/ppermute | solution.py:31
  25.5 0.0 all-to-all-done
  25.5 0.0 collective-permute-done.3.n1
  25.5 0.0 collective-permute-done.f2
  25.5 0.0 collective-permute-done.1.n2
  25.5 0.0 copy-done.1
  25.5 0.0 copy-done.2
  25.5 2.1 %shard_map.151 = (f32[512,128]{1,0:T(8,128)S(1)}, bf16[512,128]{1,0:T(8,128)(2,1)S(1)}, bf16[32,512]{1,0:T(8,128)(2,1)S(1)}, bf16[48,512]{1,0:T(8,128)(2,1)S(1)}...) custom-call(bf16[512,128]{1,0:T(8,128)(2,1)S(1)} %get-tuple-element.32.field_ref, ...), custom_call_target="tpu_custom_call" | custom-call | flops 318767104 | bytes 1449984 | tf_op jit(solution)/shard_map/pallas_call | solution.py:42
  27.6 3.7 %collective-permute-start.4 = (bf16[48,512]{1,0:T(8,128)(2,1)S(1)}, bf16[48,512]{1,0:T(8,128)(2,1)S(1)}, u32[]{:S(2)}, u32[]{:S(2)}) collective-permute-start(bf16[48,512]{1,0:T(8,128)(2,1)S(1)} %get-tuple-element.44), channel_id=1, source_target_pairs={{8,16},{16,8},{12,20},{20,12},{24,32},{32,24},{28,36},{36,28},{40,... | collective-permute-start | bytes 147464 | tf_op jit(solution)/shard_map/ppermute | solution.py:31
  31.3 1.9 %collective-permute-start.5 = (bf16[48,512]{1,0:T(8,128)(2,1)S(1)}, bf16[48,512]{1,0:T(8,128)(2,1)S(1)}, u32[]{:S(2)}, u32[]{:S(2)}) collective-permute-start(bf16[48,512]{1,0:T(8,128)(2,1)S(1)} %get-tuple-element.45), channel_id=1, source_target_pairs={{4,8},{8,4},{12,16},{16,12},{20,24},{24,20},{28,32},{32,28},{36,40... | collective-permute-start | bytes 147464 | tf_op jit(solution)/shard_map/ppermute | solution.py:31
  33.3 5.5 %collective-permute-start.7 = (bf16[32,512]{1,0:T(8,128)(2,1)S(1)}, bf16[32,512]{1,0:T(8,128)(2,1)S(1)}, u32[]{:S(2)}, u32[]{:S(2)}) collective-permute-start(bf16[32,512]{1,0:T(8,128)(2,1)S(1)} %get-tuple-element.47), channel_id=1, source_target_pairs={{0,4},{4,0},{8,12},{12,8},{16,20},{20,16},{24,28},{28,24},{32,36},... | collective-permute-start | bytes 98312 | tf_op jit(solution)/shard_map/ppermute | solution.py:31
  38.8 4.8 %all-to-all-start.1 = ((bf16[4,8,512]{2,1,0:T(8,128)(2,1)}), bf16[4,8,512]{2,1,0:T(8,128)(2,1)S(1)}, u32[]{:S(2)}, u32[]{:S(2)}) async-start(bf16[4,8,512]{2,1,0:T(8,128)(2,1)} %bitcast.8), calls=%async_computation.1 | async-start | bytes 65536 | tf_op jit(solution)/shard_map/all_to_all | solution.py:244
  43.6 1.9 %collective-permute-start.6 = (bf16[16,512]{1,0:T(8,128)(2,1)S(1)}, bf16[16,512]{1,0:T(8,128)(2,1)S(1)}, u32[]{:S(2)}, u32[]{:S(2)}) collective-permute-start(bf16[16,512]{1,0:T(8,128)(2,1)S(1)} %get-tuple-element.46), channel_id=1, source_target_pairs={{0,8},{8,0},{4,12},{12,4},{16,24},{24,16},{20,28},{28,20},{32,40},... | collective-permute-start | bytes 49160 | tf_op jit(solution)/shard_map/ppermute | solution.py:31
  45.5 3.7 %collective-permute-done.6.f1 = bf16[16,512]{1,0:T(8,128)(2,1)S(1)} collective-permute-done((bf16[16,512]{1,0:T(8,128)(2,1)S(1)}, bf16[16,512]{1,0:T(8,128)(2,1)S(1)}, u32[]{:S(2)}, u32[]{:S(2)}) %collective-permute-start.6) | collective-permute-done | bytes 16416 | tf_op jit(solution)/shard_map/ppermute | solution.py:31
  49.2 0.0 all-to-all-done.1
  49.2 0.0 collective-permute-done.7.n1
  49.2 0.0 collective-permute-done.4.f2
  49.2 0.0 collective-permute-done.5.n2
  49.2 2.1 %shard_map.152 = (f32[512,128]{1,0:T(8,128)S(1)}, bf16[512,128]{1,0:T(8,128)(2,1)S(1)}, bf16[32,512]{1,0:T(8,128)(2,1)S(1)}, bf16[48,512]{1,0:T(8,128)(2,1)S(1)}...) custom-call(bf16[512,128]{1,0:T(8,128)(2,1)S(1)} %get-tuple-element.43.field_ref, ...), custom_call_target="tpu_custom_call" | custom-call | flops 318767104 | bytes 1449984 | tf_op jit(solution)/shard_map/pallas_call | solution.py:42
  51.3 1.9 %collective-permute-start.8 = (bf16[48,512]{1,0:T(8,128)(2,1)S(1)}, bf16[48,512]{1,0:T(8,128)(2,1)S(1)}, u32[]{:S(2)}, u32[]{:S(2)}) collective-permute-start(bf16[48,512]{1,0:T(8,128)(2,1)S(1)} %get-tuple-element.51), channel_id=1, source_target_pairs={{8,16},{16,8},{12,20},{20,12},{24,32},{32,24},{28,36},{36,28},{40,... | collective-permute-start | bytes 147464 | tf_op jit(solution)/shard_map/ppermute | solution.py:31
  53.2 1.9 %collective-permute-start.9 = (bf16[48,512]{1,0:T(8,128)(2,1)S(1)}, bf16[48,512]{1,0:T(8,128)(2,1)S(1)}, u32[]{:S(2)}, u32[]{:S(2)}) collective-permute-start(bf16[48,512]{1,0:T(8,128)(2,1)S(1)} %get-tuple-element.52), channel_id=1, source_target_pairs={{4,8},{8,4},{12,16},{16,12},{20,24},{24,20},{28,32},{32,28},{36,40... | collective-permute-start | bytes 147464 | tf_op jit(solution)/shard_map/ppermute | solution.py:31
  55.1 7.3 %collective-permute-start.11 = (bf16[32,512]{1,0:T(8,128)(2,1)S(1)}, bf16[32,512]{1,0:T(8,128)(2,1)S(1)}, u32[]{:S(2)}, u32[]{:S(2)}) collective-permute-start(bf16[32,512]{1,0:T(8,128)(2,1)S(1)} %get-tuple-element.54), channel_id=1, source_target_pairs={{0,4},{4,0},{8,12},{12,8},{16,20},{20,16},{24,28},{28,24},{32,36},... | collective-permute-start | bytes 98312 | tf_op jit(solution)/shard_map/ppermute | solution.py:31
  62.5 4.8 %all-to-all-start.2 = ((bf16[4,8,512]{2,1,0:T(8,128)(2,1)}), bf16[4,8,512]{2,1,0:T(8,128)(2,1)S(1)}, u32[]{:S(2)}, u32[]{:S(2)}) async-start(bf16[4,8,512]{2,1,0:T(8,128)(2,1)} %bitcast.10), calls=%async_computation.2 | async-start | bytes 65536 | tf_op jit(solution)/shard_map/all_to_all | solution.py:244
  67.3 1.9 %collective-permute-start.10 = (bf16[16,512]{1,0:T(8,128)(2,1)S(1)}, bf16[16,512]{1,0:T(8,128)(2,1)S(1)}, u32[]{:S(2)}, u32[]{:S(2)}) collective-permute-start(bf16[16,512]{1,0:T(8,128)(2,1)S(1)} %get-tuple-element.53), channel_id=1, source_target_pairs={{0,8},{8,0},{4,12},{12,4},{16,24},{24,16},{20,28},{28,20},{32,40},... | collective-permute-start | bytes 49160 | tf_op jit(solution)/shard_map/ppermute | solution.py:31
  69.2 3.7 %collective-permute-done.10.f1 = bf16[16,512]{1,0:T(8,128)(2,1)S(1)} collective-permute-done((bf16[16,512]{1,0:T(8,128)(2,1)S(1)}, bf16[16,512]{1,0:T(8,128)(2,1)S(1)}, u32[]{:S(2)}, u32[]{:S(2)}) %collective-permute-start.10) | collective-permute-done | bytes 16416 | tf_op jit(solution)/shard_map/ppermute | solution.py:31
  72.9 0.0 all-to-all-done.2
  72.9 0.0 collective-permute-done.11.n1
  72.9 0.0 collective-permute-done.8.f2
  72.9 0.0 collective-permute-done.9.n2
  73.0 0.0 copy-start.14
  73.0 0.6 copy-done.14
  73.6 0.9 %shard_map.153 = (f32[512,128]{1,0:T(8,128)S(1)}, bf16[512,128]{1,0:T(8,128)(2,1)S(1)}, bf16[16,512]{1,0:T(8,128)(2,1)S(1)}) custom-call(bf16[512,128]{1,0:T(8,128)(2,1)S(1)} %get-tuple-element.50.field_ref, bf16[48,512]{1,0:T(8,128)(2,1)S(1)} %collective-permute-done.8.f2, bf16[48,512]{1,0:T(8,128)(2,1)S(1)} %collective-permute-done.9.n2, ...), custom_call_target="tpu_custom_call" | custom-call | flops 318767104 | bytes 1138752 | tf_op jit(solution)/shard_map/pallas_call | solution.py:42
  74.5 1.9 %collective-permute-start.12 = (bf16[16,512]{1,0:T(8,128)(2,1)S(1)}, bf16[16,512]{1,0:T(8,128)(2,1)S(1)}, u32[]{:S(2)}, u32[]{:S(2)}) collective-permute-start(bf16[16,512]{1,0:T(8,128)(2,1)S(1)} %get-tuple-element.59), channel_id=1, source_target_pairs={{0,1},{1,0},{2,3},{3,2},{4,5},{5,4},{6,7},{7,6},{8,9},{9,8},{10,11... | collective-permute-start | bytes 49160 | tf_op jit(solution)/shard_map/ppermute | solution.py:31
  76.4 0.0 copy-start.9
  76.4 0.6 copy-done.9
  77.1 0.8 %shard_map.154 = (f32[512,128]{1,0:T(8,128)}, f32[512,128]{1,0:T(8,128)S(1)}) custom-call(f32[512,128]{1,0:T(8,128)S(1)} %get-tuple-element.56.residual_ref, bf16[512,128]{1,0:T(8,128)(2,1)S(1)} %get-tuple-element.57.rounded_ref, s32[1,128]{1,0:T(1,128)S(1)} %bitcast.24), custom_call_target="tpu_custom_call" | custom-call | flops 79691776 | bytes 393728 | tf_op jit(solution)/shard_map/pallas_call | solution.py:42
  77.9 2.2 %collective-permute-done.12.incoming = bf16[16,512]{1,0:T(8,128)(2,1)S(1)} collective-permute-done((bf16[16,512]{1,0:T(8,128)(2,1)S(1)}, bf16[16,512]{1,0:T(8,128)(2,1)S(1)}, u32[]{:S(2)}, u32[]{:S(2)}) %collective-permute-start.12) | collective-permute-done | bytes 16416 | tf_op jit(solution)/shard_map/ppermute | solution.py:31
  80.1 0.0 copy-done.6
  80.1 1.1 %shard_map.155 = f32[512,128]{1,0:T(8,128)} custom-call(f32[512,128]{1,0:T(8,128)S(1)} %get-tuple-element.58.half_ref, bf16[16,512]{1,0:T(8,128)(2,1)S(1)} %collective-permute-done.12.incoming, s32[1,128]{1,0:T(1,128)S(1)} %bitcast.25, bf16[64,64]{1,0:T(8,128)(2,1)S(1)} %copy-done.6, f32[512,128]{1,0:T(8,128)S(1)} %get-tuple-element.60.iterate), custom_call_target="tpu_custom_call" | custom-call | flops 79691776 | bytes 549376 | tf_op jit(solution)/shard_map/pallas_call | solution.py:42
  (6 shorter events, 0.0 us)
Async XLA Ops:
  0.6 21.1 %copy-start.8 = (s32[6,128]{1,0:T(8,128)S(1)}, s32[6,128]{1,0:T(8,128)}, u32[]{:S(2)}) copy-start(s32[6,128]{1,0:T(8,128)} %face_type.1) | copy-start | bytes 9220
  0.6 0.7 copy-start.10
  0.7 0.7 copy-start.11
  0.7 21.1 %copy-start.5 = (bf16[2,64,64]{2,1,0:T(8,128)(2,1)S(1)}, bf16[2,64,64]{2,1,0:T(8,128)(2,1)}, u32[]{:S(2)}) copy-start(bf16[2,64,64]{2,1,0:T(8,128)(2,1)} %smooth.1) | copy-start | bytes 49156
  0.7 21.1 %copy-start.7 = (s32[6,128]{1,0:T(8,128)S(1)}, s32[6,128]{1,0:T(8,128)}, u32[]{:S(2)}) copy-start(s32[6,128]{1,0:T(8,128)} %neighbours.1) | copy-start | bytes 9220
  0.7 21.1 %copy-start.4 = (bf16[2,64,64]{2,1,0:T(8,128)(2,1)S(1)}, bf16[2,64,64]{2,1,0:T(8,128)(2,1)}, u32[]{:S(2)}) copy-start(bf16[2,64,64]{2,1,0:T(8,128)(2,1)} %diag.1) | copy-start | bytes 49156
  0.8 0.7 copy-start.12
  1.5 0.9 %copy-start = (f32[64,8,128]{2,1,0:T(8,128)S(1)}, f32[64,8,128]{2,1,0:T(8,128)}, u32[]{:S(2)}) copy-start(f32[64,8,128]{2,1,0:T(8,128)} %param.15) | copy-start | bytes 786436
  2.4 23.1 %copy-start.1 = (f32[64,8,128]{2,1,0:T(8,128)S(1)}, f32[64,8,128]{2,1,0:T(8,128)}, u32[]{:S(2)}) copy-start(f32[64,8,128]{2,1,0:T(8,128)} %param.15) | copy-start | bytes 786436
  2.4 23.1 %copy-start.2 = (f32[64,8,128]{2,1,0:T(8,128)S(1)}, f32[64,8,128]{2,1,0:T(8,128)}, u32[]{:S(2)}) copy-start(f32[64,8,128]{2,1,0:T(8,128)} %param.14) | copy-start | bytes 786436
  3.8 21.7 %collective-permute-start = (bf16[48,512]{1,0:T(8,128)(2,1)S(1)}, bf16[48,512]{1,0:T(8,128)(2,1)S(1)}, u32[]{:S(2)}, u32[]{:S(2)}) collective-permute-start(bf16[48,512]{1,0:T(8,128)(2,1)S(1)} %get-tuple-element.33), channel_id=1, source_target_pairs={{8,16},{16,8},{12,20},{20,12},{24,32},{32,24},{28,36},{36,28},{40,... | collective-permute-start | bytes 147464 | tf_op jit(solution)/shard_map/ppermute | solution.py:31
  8.5 17.0 %collective-permute-start.1 = (bf16[48,512]{1,0:T(8,128)(2,1)S(1)}, bf16[48,512]{1,0:T(8,128)(2,1)S(1)}, u32[]{:S(2)}, u32[]{:S(2)}) collective-permute-start(bf16[48,512]{1,0:T(8,128)(2,1)S(1)} %get-tuple-element.34), channel_id=1, source_target_pairs={{4,8},{8,4},{12,16},{16,12},{20,24},{24,20},{28,32},{32,28},{36,40... | collective-permute-start | bytes 147464 | tf_op jit(solution)/shard_map/ppermute | solution.py:31
  10.4 15.0 %collective-permute-start.3 = (bf16[32,512]{1,0:T(8,128)(2,1)S(1)}, bf16[32,512]{1,0:T(8,128)(2,1)S(1)}, u32[]{:S(2)}, u32[]{:S(2)}) collective-permute-start(bf16[32,512]{1,0:T(8,128)(2,1)S(1)} %get-tuple-element.36), channel_id=1, source_target_pairs={{0,4},{4,0},{8,12},{12,8},{16,20},{20,16},{24,28},{28,24},{32,36},... | collective-permute-start | bytes 98312 | tf_op jit(solution)/shard_map/ppermute | solution.py:31
  15.0 10.5 %all-to-all-start = ((bf16[4,8,512]{2,1,0:T(8,128)(2,1)}), bf16[4,8,512]{2,1,0:T(8,128)(2,1)S(1)}, u32[]{:S(2)}, u32[]{:S(2)}) async-start(bf16[4,8,512]{2,1,0:T(8,128)(2,1)} %bitcast.4), calls=%async_computation | async-start | bytes 65536 | tf_op jit(solution)/shard_map/all_to_all | solution.py:244
  19.9 5.6 %collective-permute-start.2 = (bf16[16,512]{1,0:T(8,128)(2,1)S(1)}, bf16[16,512]{1,0:T(8,128)(2,1)S(1)}, u32[]{:S(2)}, u32[]{:S(2)}) collective-permute-start(bf16[16,512]{1,0:T(8,128)(2,1)S(1)} %get-tuple-element.35), channel_id=1, source_target_pairs={{0,8},{8,0},{4,12},{12,4},{16,24},{24,16},{20,28},{28,20},{32,40},... | collective-permute-start | bytes 49160 | tf_op jit(solution)/shard_map/ppermute | solution.py:31
  21.8 0.9 %copy-start.3 = (bf16[6,2,64,64]{3,2,1,0:T(8,128)(2,1)S(1)}, bf16[6,2,64,64]{3,2,1,0:T(8,128)(2,1)}, u32[]{:S(2)}) copy-start(bf16[6,2,64,64]{3,2,1,0:T(8,128)(2,1)} %face.1) | copy-start | bytes 294916
  22.7 0.7 copy-start.13
  27.6 21.6 %collective-permute-start.4 = (bf16[48,512]{1,0:T(8,128)(2,1)S(1)}, bf16[48,512]{1,0:T(8,128)(2,1)S(1)}, u32[]{:S(2)}, u32[]{:S(2)}) collective-permute-start(bf16[48,512]{1,0:T(8,128)(2,1)S(1)} %get-tuple-element.44), channel_id=1, source_target_pairs={{8,16},{16,8},{12,20},{20,12},{24,32},{32,24},{28,36},{36,28},{40,... | collective-permute-start | bytes 147464 | tf_op jit(solution)/shard_map/ppermute | solution.py:31
  31.3 17.9 %collective-permute-start.5 = (bf16[48,512]{1,0:T(8,128)(2,1)S(1)}, bf16[48,512]{1,0:T(8,128)(2,1)S(1)}, u32[]{:S(2)}, u32[]{:S(2)}) collective-permute-start(bf16[48,512]{1,0:T(8,128)(2,1)S(1)} %get-tuple-element.45), channel_id=1, source_target_pairs={{4,8},{8,4},{12,16},{16,12},{20,24},{24,20},{28,32},{32,28},{36,40... | collective-permute-start | bytes 147464 | tf_op jit(solution)/shard_map/ppermute | solution.py:31
  33.3 16.0 %collective-permute-start.7 = (bf16[32,512]{1,0:T(8,128)(2,1)S(1)}, bf16[32,512]{1,0:T(8,128)(2,1)S(1)}, u32[]{:S(2)}, u32[]{:S(2)}) collective-permute-start(bf16[32,512]{1,0:T(8,128)(2,1)S(1)} %get-tuple-element.47), channel_id=1, source_target_pairs={{0,4},{4,0},{8,12},{12,8},{16,20},{20,16},{24,28},{28,24},{32,36},... | collective-permute-start | bytes 98312 | tf_op jit(solution)/shard_map/ppermute | solution.py:31
  38.8 10.4 %all-to-all-start.1 = ((bf16[4,8,512]{2,1,0:T(8,128)(2,1)}), bf16[4,8,512]{2,1,0:T(8,128)(2,1)S(1)}, u32[]{:S(2)}, u32[]{:S(2)}) async-start(bf16[4,8,512]{2,1,0:T(8,128)(2,1)} %bitcast.8), calls=%async_computation.1 | async-start | bytes 65536 | tf_op jit(solution)/shard_map/all_to_all | solution.py:244
  43.6 5.6 %collective-permute-start.6 = (bf16[16,512]{1,0:T(8,128)(2,1)S(1)}, bf16[16,512]{1,0:T(8,128)(2,1)S(1)}, u32[]{:S(2)}, u32[]{:S(2)}) collective-permute-start(bf16[16,512]{1,0:T(8,128)(2,1)S(1)} %get-tuple-element.46), channel_id=1, source_target_pairs={{0,8},{8,0},{4,12},{12,4},{16,24},{24,16},{20,28},{28,20},{32,40},... | collective-permute-start | bytes 49160 | tf_op jit(solution)/shard_map/ppermute | solution.py:31
  51.3 21.6 %collective-permute-start.8 = (bf16[48,512]{1,0:T(8,128)(2,1)S(1)}, bf16[48,512]{1,0:T(8,128)(2,1)S(1)}, u32[]{:S(2)}, u32[]{:S(2)}) collective-permute-start(bf16[48,512]{1,0:T(8,128)(2,1)S(1)} %get-tuple-element.51), channel_id=1, source_target_pairs={{8,16},{16,8},{12,20},{20,12},{24,32},{32,24},{28,36},{36,28},{40,... | collective-permute-start | bytes 147464 | tf_op jit(solution)/shard_map/ppermute | solution.py:31
  53.2 19.7 %collective-permute-start.9 = (bf16[48,512]{1,0:T(8,128)(2,1)S(1)}, bf16[48,512]{1,0:T(8,128)(2,1)S(1)}, u32[]{:S(2)}, u32[]{:S(2)}) collective-permute-start(bf16[48,512]{1,0:T(8,128)(2,1)S(1)} %get-tuple-element.52), channel_id=1, source_target_pairs={{4,8},{8,4},{12,16},{16,12},{20,24},{24,20},{28,32},{32,28},{36,40... | collective-permute-start | bytes 147464 | tf_op jit(solution)/shard_map/ppermute | solution.py:31
  55.1 17.8 %collective-permute-start.11 = (bf16[32,512]{1,0:T(8,128)(2,1)S(1)}, bf16[32,512]{1,0:T(8,128)(2,1)S(1)}, u32[]{:S(2)}, u32[]{:S(2)}) collective-permute-start(bf16[32,512]{1,0:T(8,128)(2,1)S(1)} %get-tuple-element.54), channel_id=1, source_target_pairs={{0,4},{4,0},{8,12},{12,8},{16,20},{20,16},{24,28},{28,24},{32,36},... | collective-permute-start | bytes 98312 | tf_op jit(solution)/shard_map/ppermute | solution.py:31
  62.5 10.4 %all-to-all-start.2 = ((bf16[4,8,512]{2,1,0:T(8,128)(2,1)}), bf16[4,8,512]{2,1,0:T(8,128)(2,1)S(1)}, u32[]{:S(2)}, u32[]{:S(2)}) async-start(bf16[4,8,512]{2,1,0:T(8,128)(2,1)} %bitcast.10), calls=%async_computation.2 | async-start | bytes 65536 | tf_op jit(solution)/shard_map/all_to_all | solution.py:244
  67.3 5.6 %collective-permute-start.10 = (bf16[16,512]{1,0:T(8,128)(2,1)S(1)}, bf16[16,512]{1,0:T(8,128)(2,1)S(1)}, u32[]{:S(2)}, u32[]{:S(2)}) collective-permute-start(bf16[16,512]{1,0:T(8,128)(2,1)S(1)} %get-tuple-element.53), channel_id=1, source_target_pairs={{0,8},{8,0},{4,12},{12,4},{16,24},{24,16},{20,28},{28,20},{32,40},... | collective-permute-start | bytes 49160 | tf_op jit(solution)/shard_map/ppermute | solution.py:31
  73.0 0.7 copy-start.14
  74.5 5.6 %collective-permute-start.12 = (bf16[16,512]{1,0:T(8,128)(2,1)S(1)}, bf16[16,512]{1,0:T(8,128)(2,1)S(1)}, u32[]{:S(2)}, u32[]{:S(2)}) collective-permute-start(bf16[16,512]{1,0:T(8,128)(2,1)S(1)} %get-tuple-element.59), channel_id=1, source_target_pairs={{0,1},{1,0},{2,3},{3,2},{4,5},{5,4},{6,7},{7,6},{8,9},{9,8},{10,11... | collective-permute-start | bytes 49160 | tf_op jit(solution)/shard_map/ppermute | solution.py:31
  76.4 0.7 copy-start.9
  77.1 3.0 %copy-start.6 = (bf16[64,64]{1,0:T(8,128)(2,1)S(1)}, bf16[64,64]{1,0:T(8,128)(2,1)}, u32[]{:S(2)}) copy-start(bf16[64,64]{1,0:T(8,128)(2,1)} %inverse.1) | copy-start | bytes 24580

commit v3 on v2

v3 whole, which is shorter than its diff:
```python
import jax
import jax.numpy as jnp
from jax import lax
from jax.experimental import pallas as pl
from jax.experimental.pallas import tpu as pltpu
from jax.sharding import PartitionSpec as P

SWEEPS = 2
DOF = 64
RHS = 8
E = 128
CHIP = 2 * E
FACES = 6
ROWS = DOF * RHS
NEAR = 32
FAR = 8
SUB = 8
PAIRS = 16
CROSS = NEAR + 2 * FAR
SIDE = 4 * 2 * SUB
KEPT = CHIP + 2 * CROSS + SIDE
INTS = 32
BF = jnp.bfloat16
F32 = jnp.float32


def swap(array, axis, pairs):
    count = lax.axis_size(axis)
    route = []
    for low, high in pairs:
        if high < count:
            route += [(low, high), (high, low)]
    return lax.ppermute(array, axis, route)


def spec():
    return pl.BlockSpec(memory_space=pltpu.VMEM)


def call(kernel, outs, *args, flops=0, scalars=0, remote=0, scratch=(), vmem=16):
    specs = [pl.BlockSpec(memory_space=pltpu.SMEM)] * scalars
    specs += [pl.BlockSpec(memory_space=pl.ANY)] * remote
    specs += [spec()] * (len(args) - scalars - remote)
    moved = sum(a.size * a.dtype.itemsize for a in args)
    return pl.pallas_call(
        kernel,
        out_shape=[jax.ShapeDtypeStruct(s, d) for s, d in outs],
        in_specs=specs,
        out_specs=[spec()] * len(outs),
        scratch_shapes=scratch,
        cost_estimate=pl.CostEstimate(flops=flops, bytes_accessed=moved, transcendentals=0),
        compiler_params=pltpu.CompilerParams(vmem_limit_bytes=vmem << 20),
    )(*args)


def iota(shape, dim):
    return lax.broadcasted_iota(jnp.int32, shape, dim)


def half(core):
    return pl.ds(pl.multiple_of(core * E, E), E)


def column(row):
    count = row.shape[1]
    wide = jnp.broadcast_to(row.astype(F32), (count, count))
    kept = jnp.where(iota((count, count), 0) == iota((count, count), 1), wide, 0.0)
    return jnp.sum(kept, axis=1, keepdims=True).astype(jnp.int32)


def picker(row, width):
    count = row.shape[1]
    return jnp.where(iota((count, width), 1) == column(row), 1.0, 0.0).astype(BF)


def send(choice, field, refs):
    rows = lax.dot_general(choice, field, (((1,), (1,)), ((), ())), preferred_element_type=F32).astype(BF)
    start = 0
    for ref, used in refs:
        ref[:used] = rows[start : start + used]
        if ref.shape[0] > used:
            ref[used:] = jnp.zeros((ref.shape[0] - used, ROWS), BF)
        start += used


def first_kernel(*refs):
    sources, message, targets, ints, arrived = refs[:8], refs[8], refs[9:17], refs[17], refs[18]
    copies = [pltpu.make_async_copy(a, b, arrived.at[i]) for i, (a, b) in enumerate(zip(sources, targets))]
    for copy in copies:
        copy.start()
    near, far, sub, elem_type, face_type, neighbours, guess, rhs = targets
    for copy in copies[:6]:
        copy.wait()
    ints[...] = jnp.zeros((INTS, E), F32)
    ints[0:6, :] = neighbours[...].astype(F32)
    ints[8:14, :] = face_type[...].astype(F32)
    ints[14:15, :] = elem_type[...].astype(F32)
    ints[16:18, :NEAR] = near[...].astype(F32)
    ints[18:20, :FAR] = far[...].astype(F32)
    ints[20:21, :SUB] = sub[...].astype(F32)
    message[2 * ROWS :, :] = ints[...].astype(BF)
    for i, field in enumerate((guess, rhs)):
        copies[6 + i].wait()
        for r in range(RHS):
            start = i * ROWS + r * DOF
            message[start : start + DOF, :] = field[pl.ds(r, DOF, stride=RHS), :].astype(BF)


def pack_kernel(place_ref, mine, other, field_ref, ints_ref, choice_ref, *messages):
    core = place_ref[0]
    odd = place_ref[1] == 1
    field_ref[:, half(core)] = mine[:ROWS, :]
    field_ref[:, half(1 - core)] = other[:ROWS, :]
    ints_ref[core] = mine[2 * ROWS :, :].astype(F32).astype(jnp.int32)
    ints_ref[1 - core] = other[2 * ROWS :, :].astype(F32).astype(jnp.int32)
    low, high = ints_ref[0], ints_ref[1]

    def chosen(near, one, two):
        return picker(near, CHIP), jnp.concatenate([picker(one, CHIP), picker(two + E, CHIP)], axis=0)

    up = (high[17:18, :NEAR] + E, low[19:20, :FAR], high[19:20, :FAR])
    down = (low[16:17, :NEAR], low[18:19, :FAR], high[18:19, :FAR])
    to_one = [jnp.where(odd, d, u) for u, d in zip(up, down)]
    to_two = [jnp.where(odd, u, d) for u, d in zip(up, down)]
    side = jnp.concatenate([picker(low[20:21, :SUB], CHIP), picker(high[20:21, :SUB] + E, CHIP)], axis=0)
    choice = jnp.concatenate([*chosen(*to_one), *chosen(*to_two), side, side, side, side], axis=0)
    choice_ref[...] = choice
    send(choice, field_ref[...], zip(messages, (CROSS, CROSS, SIDE)))


def prep_kernel(place_ref, diag, face, smooth, ints, other, rhs, pick_ref, mask_ref, wide_ref, smooth_ref, rhs_ref):
    core = place_ref[0]
    odd = place_ref[1] == 1
    below = jnp.where(odd, CHIP, CHIP + CROSS)
    above = jnp.where(odd, CHIP + CROSS, CHIP)
    for c in range(2):
        mine, near = ints[c], ints[1 - c]
        listed = near[16:17, :NEAR] if c == 0 else near[17:18, :NEAR]
        inner = jnp.where(iota((E, NEAR), 0) == listed, 1.0, 0.0).astype(BF)
        for d in range(FACES):
            k = mine[d : d + 1, :]
            m = k - 208
            place = CHIP + 2 * CROSS + (m >> 3) * 2 * SUB + c * SUB + (m & 7)
            place = jnp.where(k < 208, above + NEAR + c * FAR + k - 200, place)
            place = jnp.where(k < 200, below + NEAR + c * FAR + k - 192, place)
            place = jnp.where(k < 192, -1 if c == 0 else above + k - 160, place)
            place = jnp.where(k < 160, below + k - 128 if c == 0 else -1, place)
            place = jnp.where(k < E, k + c * E, place)
            lanes = slice(d * CHIP + c * E, d * CHIP + (c + 1) * E)
            hot = jnp.where(iota((KEPT, E), 0) == place, 1.0, 0.0)
            slot = jnp.where(iota((NEAR, E), 0) + (160 if c == 0 else 128) == k, 1.0, 0.0).astype(BF)
            within = jnp.dot(inner, slot, preferred_element_type=F32)
            start = (1 - c) * E
            if start:
                pick_ref[:start, lanes] = hot[:start].astype(BF)
            pick_ref[start : start + E, lanes] = (hot[start : start + E] + within).astype(BF)
            pick_ref[start + E :, lanes] = hot[start + E :].astype(BF)
        for d in range(FACES + 1):
            kinds = mine[14:15, :] if d == 0 else mine[7 + d : 8 + d, :]
            for t in range(2):
                mask = jnp.where(jnp.broadcast_to(kinds, (16, E)) == t, 1.0, 0.0)
                mask_ref[2 * d + t, :, c * E : (c + 1) * E] = mask.astype(BF)
    for d in range(FACES + 1):
        both = (diag[0], diag[1]) if d == 0 else (face[d - 1, 0], face[d - 1, 1])
        wide_ref[:, d * 2 * DOF : (d + 1) * 2 * DOF] = jnp.concatenate(both, axis=1)
    smooth_ref[...] = jnp.concatenate([smooth[0], smooth[1]], axis=1)
    for r in range(RHS):
        rows = slice(r * DOF, (r + 1) * DOF)
        rhs_ref[rows, half(core)] = rhs[pl.ds(r, DOF, stride=RHS), :]
    rhs_ref[:, half(1 - core)] = other[ROWS : 2 * ROWS, :].astype(F32)


def masked(block, mask):
    return block * jnp.concatenate([mask] * (DOF // 16), axis=0)


def extend(field_ref, halo):
    near = jnp.concatenate([ref[:used] for ref, used in zip(halo, (CROSS, CROSS, SIDE))], axis=0)
    return jnp.concatenate([field_ref[...], near.T], axis=1)


def sweep_kernel(place_ref, field_ref, two, one, side, pick, masks, wide, smooth, rhs, choice, *refs):
    core = place_ref[0]
    before, (after, next_field, *messages) = refs[:-5], refs[-5:]
    if len(before) == 2:
        guess, other = before
        for r in range(RHS):
            after[r * DOF : (r + 1) * DOF, half(core)] = guess[pl.ds(r, DOF, stride=RHS), :]
        after[:, half(1 - core)] = other[:ROWS, :].astype(F32)
        before = after
    else:
        (before,) = before
    beside = jnp.dot(extend(field_ref, (one, two, side)), pick[...], preferred_element_type=F32).astype(BF)
    for r in range(RHS):
        rows = slice(r * DOF, (r + 1) * DOF)
        stack = []
        for d in range(FACES + 1):
            block = field_ref[rows, :] if d == 0 else beside[rows, (d - 1) * CHIP : d * CHIP]
            stack += [masked(block, masks[2 * d]), masked(block, masks[2 * d + 1])]
        product = jnp.dot(wide[...], jnp.concatenate(stack, axis=0), preferred_element_type=F32)
        rounded = (rhs[rows, :] - product).astype(BF)
        both = jnp.concatenate([masked(rounded, masks[0]), masked(rounded, masks[1])], axis=0)
        new = before[rows, :] + jnp.dot(smooth[...], both, preferred_element_type=F32)
        after[rows, :] = new
        next_field[rows, :] = new.astype(BF)
    send(choice[...], next_field[...], zip(messages, (CROSS, CROSS, SIDE)))


def residual_kernel(place_ref, field_ref, two, one, side, pick, masks, wide, rhs, pair, residual_ref, rounded_ref, message):
    core = place_ref[0]
    own = half(core)
    extended = extend(field_ref, (one, two, side))
    beside = []
    for d in range(FACES):
        columns = pick[:, pl.ds(pl.multiple_of(d * CHIP + core * E, E), E)]
        beside.append(columns)
    beside = jnp.dot(extended, jnp.concatenate(beside, axis=1), preferred_element_type=F32).astype(BF)
    field = field_ref[:, own]
    kinds = [masks[i, :, own] for i in range(2 * FACES + 2)]
    for r in range(0, RHS, 2):
        halves = []
        for s in (r, r + 1):
            rows = slice(s * DOF, (s + 1) * DOF)
            stack = []
            for d in range(FACES + 1):
                block = field[rows, :] if d == 0 else beside[rows, (d - 1) * E : d * E]
                stack += [masked(block, kinds[2 * d]), masked(block, kinds[2 * d + 1])]
            halves.append(jnp.concatenate(stack, axis=0))
        product = jnp.dot(wide[...], jnp.concatenate(halves, axis=1), preferred_element_type=F32)
        for i in range(2):
            rows = slice((r + i) * DOF, (r + i + 1) * DOF)
            part = rhs[rows, own] - product[:, i * E : (i + 1) * E]
            residual_ref[rows, :] = part
            rounded_ref[rows, :] = part.astype(BF)
    send(picker(pair[...], E), rounded_ref[...], [(message, PAIRS)])


def mate_picker(partner, first, count):
    return jnp.where(iota((count, E), 0) + first == partner, 1.0, 0.0).astype(BF)


def local_kernel(residual_ref, rounded_ref, partner, out_ref, half_ref):
    rest = (residual_ref[...] - rounded_ref[...].astype(F32)).astype(BF)
    local = mate_picker(partner[...], 0, E)
    mates = jnp.dot(rounded_ref[...], local, preferred_element_type=F32)
    mates = mates + jnp.dot(rest, local, preferred_element_type=F32)
    half_ref[...] = residual_ref[...] + mates
    for r in range(RHS):
        out_ref[pl.ds(r, DOF, stride=RHS), :] = residual_ref[r * DOF : (r + 1) * DOF, :]


def coarse_kernel(place_ref, half_ref, incoming, partner, inverse, iterate, solution_ref):
    own = half(place_ref[0])
    mates = lax.dot_general(
        incoming[...], mate_picker(partner[...], E, PAIRS), (((0,), (0,)), ((), ())), preferred_element_type=F32
    )
    coarse = (half_ref[...] + mates).astype(BF)
    for r in range(0, RHS, 2):
        pair = jnp.concatenate([coarse[s * DOF : (s + 1) * DOF, :] for s in (r, r + 1)], axis=1)
        update = jnp.dot(inverse[...], pair, preferred_element_type=F32)
        for i in range(2):
            s = r + i
            solution_ref[pl.ds(s, DOF, stride=RHS), :] = iterate[s * DOF : (s + 1) * DOF, own] + update[:, i * E : (i + 1) * E]


def body(
    rhs,
    guess,
    diag_blocks,
    face_blocks,
    smoother,
    coarse_inverse,
    elem_type,
    face_type,
    neighbours,
    send_near,
    send_far,
    sub_send,
    partner,
    pair_send,
):
    a = lax.axis_index("dom")
    place = jnp.stack([a % 2, (a // 2) % 2]).astype(jnp.int32)
    doms = lax.axis_size("dom")
    rhs = rhs.reshape(ROWS, E)
    guess = guess.reshape(ROWS, E)
    inside = [(i, i + 1) for i in range(0, doms, 2)]
    cross_one = [(i + j, i + j + 2) for i in range(0, doms, 4) for j in range(2)]
    cross_two = [(i + j + 2, i + j + 4) for i in range(0, doms, 4) for j in range(2)]

    def exchange(messages):
        one, two, side = messages
        two = swap(two, "dom", cross_two)
        one = swap(one, "dom", cross_one)
        side = lax.all_to_all(side, "sub", 0, 0, tiled=True)
        return two, one, side

    message_outs = [((n, ROWS), BF) for n in SENT]
    taken = (send_near, send_far, sub_send.reshape(1, -1), elem_type.reshape(1, -1), face_type, neighbours, guess, rhs)
    (mine,) = call(
        first_kernel,
        [((2 * ROWS + INTS, E), BF)],
        *taken,
        remote=len(taken),
        scratch=[pltpu.VMEM(x.shape, x.dtype) for x in taken]
        + [pltpu.VMEM((INTS, E), F32), pltpu.SemaphoreType.DMA((len(taken),))],
        vmem=60,
    )
    other = swap(mine, "dom", inside)
    field, ints, choice, *messages = call(
        pack_kernel,
        [((ROWS, CHIP), BF), ((2, INTS, E), jnp.int32), ((2 * CROSS + SIDE, CHIP), BF)] + message_outs,
        place,
        mine,
        other,
        flops=2 * (2 * CROSS + SIDE) * CHIP * ROWS,
        scalars=1,
    )
    halo = exchange(messages)
    pick, masks, wide, smooth, rhs = call(
        prep_kernel,
        [
            ((KEPT, FACES * CHIP), BF),
            ((2 * FACES + 2, 16, CHIP), BF),
            ((DOF, 2 * DOF * (FACES + 1)), BF),
            ((DOF, 2 * DOF), BF),
            ((ROWS, CHIP), F32),
        ],
        place,
        diag_blocks,
        face_blocks,
        smoother,
        ints,
        other,
        rhs,
        flops=1000000,
        scalars=1,
    )
    work = 2 * ROWS * KEPT * FACES * CHIP + 2 * DOF * 14 * DOF * RHS * CHIP
    before = (guess, other)
    for _ in range(SWEEPS):
        iterate, field, *messages = call(
            sweep_kernel,
            [((ROWS, CHIP), F32), ((ROWS, CHIP), BF)] + message_outs,
            place,
            field,
            *halo,
            pick,
            masks,
            wide,
            smooth,
            rhs,
            choice,
            *before,
            flops=work,
            scalars=1,
        )
        before = (iterate,)
        halo = exchange(messages)
    residual, rounded, message = call(
        residual_kernel,
        [((ROWS, E), F32), ((ROWS, E), BF), ((PAIRS, ROWS), BF)],
        place,
        field,
        *halo,
        pick,
        masks,
        wide,
        rhs,
        pair_send.reshape(1, -1),
        flops=work // 2,
        scalars=1,
    )
    subs = lax.axis_size("sub")
    incoming = swap(message, "sub", [(i, i + 1) for i in range(0, subs, 2)])
    partner = partner.reshape(1, -1)
    residual, coarse = call(
        local_kernel,
        [((ROWS, E), F32), ((ROWS, E), F32)],
        residual,
        rounded,
        partner,
        flops=work // 8,
    )
    (solved,) = call(
        coarse_kernel,
        [((ROWS, E), F32)],
        place,
        coarse,
        incoming,
        partner,
        coarse_inverse,
        iterate,
        flops=work // 8,
        scalars=1,
    )
    shape = (DOF, RHS, E)
    return (solved.reshape(shape), residual.reshape(shape))


SENT = (SIDE + 16, SIDE + 16, SIDE)


def solution(mesh):
    block = P(None, None, ("dom", "sub"))
    flat = P(("dom", "sub"))
    listed = P(None, ("dom", "sub"))
    in_specs = (block, block, P(), P(), P(), P(), flat, listed, listed, listed, listed, flat, flat, flat)
    return jax.shard_map(body, mesh=mesh, in_specs=in_specs, out_specs=(block, block), check_vma=False)
```

time: 82 us -> 74.9 us (0.913)
  the two profiles are of different devices: /device:TPU:250 before, /device:TPU:240 now
where the time goes in v3:
time: 74.9 us; the launch traced here: 74.3 us
  starting transfers between devices  31.1 us (42%)
  Pallas kernels  16.8 us (22%)
  blocking collectives  16 us (21%)
  waiting for transfers between devices  8.46 us (11%)
  local copies, waits for them, and re-layouts  0.99 us (1%)
  between operations  0.86 us (1%)
    ppermute x8, starting transfers between devices, swap(): return lax.ppermute(array, axis, route)  26.8 us
    pallas_call x8, Pallas kernels, call(): pl.pallas_call(kernel, out_shape=[jax.ShapeDtypeStruct(s, d) for s, d in...  16.8 us
    all_to_all x2, blocking collectives, exchange(): side = lax.all_to_all(side, 'sub', 0, 0, tiled=True)  16 us
    all_to_all x1, waiting for transfers between devices, exchange(): side = lax.all_to_all(side, 'sub', 0, 0, tiled=True)  4.55 us
    all_to_all x1, starting transfers between devices, exchange(): side = lax.all_to_all(side, 'sub', 0, 0, tiled=True)  4.3 us
    ppermute x8, waiting for transfers between devices, swap(): return lax.ppermute(array, axis, route)  3.91 us
  transfers between devices with their start and end apart: 9, of which 3 were waited for; matrix products, arithmetic and copies ran while one was open for 0% of the time, Pallas kernels for 3%

profile of v3, /device:TPU:240, one launch (start us, length us, event | category | flops | bytes accessed | tf_op | source)
XLA Modules:
  0.0 74.3 jit_solution(8871654586408828111)
XLA Ops:
  0.6 0.0 copy-start.2
  0.6 0.0 copy-start.1
  0.7 0.0 copy-start.5
  0.7 0.0 copy-start.3
  0.7 0.0 copy-start.4
  0.7 2.0 %shard_map.149.mine = bf16[1056,128]{1,0:T(8,128)(2,1)} custom-call(s32[2,32]{1,0:T(2,128)} %refs_0_.1, s32[2,8]{1,0:T(2,128)} %refs_1_.1, s32[1,8]{1,0:T(1,128)} %bitcast.29, s32[1,128]{1,0:T(1,128)} %bitcast.30, s32[6,128]{1,0:T(8,128)} %refs_4_.1, s32[6,128]{1,0:T(8,128)} %refs_5_.1, f32[512,128]{1,0:T(8,128)} %bitcast.19, f32[512,128]{1,0:T(8,128)} %bitcast.16), custom_call_target="tpu_custom_call" | custom-call | bytes 531296 | tf_op jit(solution)/shard_map/pallas_call | solution.py:45
  2.7 1.9 %collective-permute-start = (bf16[1056,128]{1,0:T(8,128)(2,1)}, bf16[1056,128]{1,0:T(8,128)(2,1)S(1)}, u32[]{:S(2)}, u32[]{:S(2)}) collective-permute-start(bf16[1056,128]{1,0:T(8,128)(2,1)} %shard_map.149.mine), channel_id=1, source_target_pairs={{0,4},{4,0},{8,12},{12,8},{16,20},{20,16},{24,28},{28,24},{32,36},... | collective-permute-start | bytes 811016 | tf_op jit(solution)/shard_map/ppermute | solution.py:33
  4.6 0.1 pad_add_fusion.place_ref
  4.7 1.6 %collective-permute-done.other.refs_1_ = bf16[1056,128]{1,0:T(8,128)(2,1)S(1)} collective-permute-done((bf16[1056,128]{1,0:T(8,128)(2,1)}, bf16[1056,128]{1,0:T(8,128)(2,1)S(1)}, u32[]{:S(2)}, u32[]{:S(2)}) %collective-permute-start) | collective-permute-done | bytes 270368 | tf_op jit(solution)/shard_map/ppermute | solution.py:33
  6.3 0.0 copy-start
  6.3 1.0 %copy-done = bf16[1056,128]{1,0:T(8,128)(2,1)S(1)} copy-done((bf16[1056,128]{1,0:T(8,128)(2,1)S(1)}, bf16[1056,128]{1,0:T(8,128)(2,1)}, u32[]{:S(2)}) %copy-start) | copy-done | bytes 270360
  7.3 1.5 %shard_map.150 = (bf16[512,256]{1,0:T(8,128)(2,1)S(1)}, s32[2,32,128]{2,1,0:T(8,128)S(1)}, bf16[160,256]{1,0:T(8,128)(2,1)S(1)}, bf16[80,512]{1,0:T(8,128)(2,1)}...) custom-call(s32[2]{0:T(128)S(1)} %pad_add_fusion.place_ref, bf16[1056,128]{1,0:T(8,128)(2,1)S(1)} %copy-done, ...), custom_call_target="tpu_custom_call" | custom-call | flops 41943040 | bytes 540680 | tf_op jit(solution)/shard_map/pallas_call | solution.py:45
  8.7 3.2 %collective-permute-start.1 = (bf16[80,512]{1,0:T(8,128)(2,1)}, bf16[80,512]{1,0:T(8,128)(2,1)}, u32[]{:S(2)}, u32[]{:S(2)}) collective-permute-start(bf16[80,512]{1,0:T(8,128)(2,1)} %get-tuple-element.29), channel_id=1, source_target_pairs={{8,16},{16,8},{12,20},{20,12},{24,32},{32,24},{28,36},{36,28},{40,... | collective-permute-start | bytes 245768 | tf_op jit(solution)/shard_map/ppermute | solution.py:33
  12.0 4.0 %collective-permute-start.2 = (bf16[80,512]{1,0:T(8,128)(2,1)}, bf16[80,512]{1,0:T(8,128)(2,1)}, u32[]{:S(2)}, u32[]{:S(2)}) collective-permute-start(bf16[80,512]{1,0:T(8,128)(2,1)} %get-tuple-element.30), channel_id=1, source_target_pairs={{0,8},{8,0},{4,12},{12,4},{16,24},{24,16},{20,28},{28,20},{32,40},... | collective-permute-start | bytes 245768 | tf_op jit(solution)/shard_map/ppermute | solution.py:33
  16.0 4.3 %all-to-all-start = ((bf16[4,16,512]{2,1,0:T(8,128)(2,1)}), bf16[4,16,512]{2,1,0:T(8,128)(2,1)S(1)}, u32[]{:S(2)}, u32[]{:S(2)}) async-start(bf16[4,16,512]{2,1,0:T(8,128)(2,1)} %bitcast.6), calls=%async_computation | async-start | bytes 131072 | tf_op jit(solution)/shard_map/all_to_all | solution.py:295
  20.3 0.0 copy-done.1
  20.3 0.0 copy-done.5
  20.3 0.0 copy-done.3
  20.4 0.0 copy-done.4
  20.4 1.1 %shard_map.151 = (bf16[416,1536]{1,0:T(8,128)(2,1)S(1)}, bf16[14,16,256]{2,1,0:T(8,128)(2,1)S(1)}, bf16[64,896]{1,0:T(8,128)(2,1)S(1)}, bf16[64,128]{1,0:T(8,128)(2,1)S(1)}, f32[512,256]{1,0:T(8,128)S(1)}) custom-call(s32[2]{0:T(128)S(1)} %pad_add_fusion.place_ref, bf16[2,64,64]{2,1,0:T(8,128)(2,1)S(1)} %copy-done.4, bf16[6,2,64,64]{3,2,1,0:T(8,128)(2,1)S(1)} %copy-done.3, ...), custom_call_target="tpu_custom_call" | custom-call | flops 1000000 | bytes 696328 | tf_op jit(solution)/shard_map/pallas_call | solution.py:45
  21.4 4.5 %all-to-all-done = bf16[4,16,512]{2,1,0:T(8,128)(2,1)S(1)} async-done(((bf16[4,16,512]{2,1,0:T(8,128)(2,1)}), bf16[4,16,512]{2,1,0:T(8,128)(2,1)S(1)}, u32[]{:S(2)}, u32[]{:S(2)}) %all-to-all-start) | async-done | bytes 65568 | tf_op jit(solution)/shard_map/all_to_all | solution.py:295
  26.0 0.0 collective-permute-done.1.two
  26.0 0.0 collective-permute-done.2.one
  26.0 0.0 copy-done.2
  26.0 4.3 %shard_map.152 = (f32[512,256]{1,0:T(8,128)S(1)}, bf16[512,256]{1,0:T(8,128)(2,1)S(1)}, bf16[80,512]{1,0:T(8,128)(2,1)S(1)}, bf16[80,512]{1,0:T(8,128)(2,1)S(1)}, bf16[64,512]{1,0:T(8,128)(2,1)S(1)}) custom-call(s32[2]{0:T(128)S(1)} %pad_add_fusion.place_ref, bf16[512,256]{1,0:T(8,128)(2,1)S(1)} %get-tuple-element.28.field_ref, ...), custom_call_target="tpu_custom_call" | custom-call | flops 889192448 | bytes 3153928 | tf_op jit(solution)/shard_map/pallas_call | solution.py:45
  30.3 1.9 %collective-permute-start.3 = (bf16[80,512]{1,0:T(8,128)(2,1)S(1)}, bf16[80,512]{1,0:T(8,128)(2,1)S(1)}, u32[]{:S(2)}, u32[]{:S(2)}) collective-permute-start(bf16[80,512]{1,0:T(8,128)(2,1)S(1)} %get-tuple-element.40), channel_id=1, source_target_pairs={{8,16},{16,8},{12,20},{20,12},{24,32},{32,24},{28,36},{36,28},{40,... | collective-permute-start | bytes 245768 | tf_op jit(solution)/shard_map/ppermute | solution.py:33
  32.2 5.1 %collective-permute-start.4 = (bf16[80,512]{1,0:T(8,128)(2,1)S(1)}, bf16[80,512]{1,0:T(8,128)(2,1)S(1)}, u32[]{:S(2)}, u32[]{:S(2)}) collective-permute-start(bf16[80,512]{1,0:T(8,128)(2,1)S(1)} %get-tuple-element.41), channel_id=1, source_target_pairs={{0,8},{8,0},{4,12},{12,4},{16,24},{24,16},{20,28},{28,20},{32,40},... | collective-permute-start | bytes 245768 | tf_op jit(solution)/shard_map/ppermute | solution.py:33
  37.3 8.0 %all_to_all.33 = bf16[4,16,512]{2,1,0:T(8,128)(2,1)S(1)} all-to-all(bf16[4,16,512]{2,1,0:T(8,128)(2,1)S(1)} %bitcast.24), channel_id=1, replica_groups=mesh['dom'=128,'sub'=4] {'sub'}, dimensions={0} | all-to-all | bytes 131072 | tf_op jit(solution)/shard_map/all_to_all | solution.py:295
  45.2 0.0 collective-permute-done.3.two
  45.2 0.0 collective-permute-done.4.one
  45.3 0.0 copy-start.8
  45.3 3.9 %shard_map.153 = (f32[512,256]{1,0:T(8,128)S(1)}, bf16[512,256]{1,0:T(8,128)(2,1)S(1)}, bf16[80,512]{1,0:T(8,128)(2,1)S(1)}, bf16[80,512]{1,0:T(8,128)(2,1)S(1)}, bf16[64,512]{1,0:T(8,128)(2,1)S(1)}) custom-call(s32[2]{0:T(128)S(1)} %pad_add_fusion.place_ref, bf16[512,256]{1,0:T(8,128)(2,1)S(1)} %get-tuple-element.39.field_ref, ...), custom_call_target="tpu_custom_call" | custom-call | flops 889192448 | bytes 3145736 | tf_op jit(solution)/shard_map/pallas_call | solution.py:45
  49.1 1.9 %collective-permute-start.5 = (bf16[80,512]{1,0:T(8,128)(2,1)S(1)}, bf16[80,512]{1,0:T(8,128)(2,1)S(1)}, u32[]{:S(2)}, u32[]{:S(2)}) collective-permute-start(bf16[80,512]{1,0:T(8,128)(2,1)S(1)} %get-tuple-element.45), channel_id=1, source_target_pairs={{8,16},{16,8},{12,20},{20,12},{24,32},{32,24},{28,36},{36,28},{40,... | collective-permute-start | bytes 245768 | tf_op jit(solution)/shard_map/ppermute | solution.py:33
  51.0 6.3 %collective-permute-start.6 = (bf16[80,512]{1,0:T(8,128)(2,1)S(1)}, bf16[80,512]{1,0:T(8,128)(2,1)S(1)}, u32[]{:S(2)}, u32[]{:S(2)}) collective-permute-start(bf16[80,512]{1,0:T(8,128)(2,1)S(1)} %get-tuple-element.46), channel_id=1, source_target_pairs={{0,8},{8,0},{4,12},{12,4},{16,24},{24,16},{20,28},{28,20},{32,40},... | collective-permute-start | bytes 245768 | tf_op jit(solution)/shard_map/ppermute | solution.py:33
  57.3 8.0 %all_to_all.34 = bf16[4,16,512]{2,1,0:T(8,128)(2,1)S(1)} all-to-all(bf16[4,16,512]{2,1,0:T(8,128)(2,1)S(1)} %bitcast.23), channel_id=1, replica_groups=mesh['dom'=128,'sub'=4] {'sub'}, dimensions={0} | all-to-all | bytes 131072 | tf_op jit(solution)/shard_map/all_to_all | solution.py:295
  65.3 0.0 copy-start.7
  65.3 0.0 collective-permute-done.5.two
  65.3 0.0 collective-permute-done.6.one
  65.3 0.0 copy-done.8
  65.3 0.0 copy-start.6
  65.3 1.7 %shard_map.154 = (f32[512,128]{1,0:T(8,128)S(1)}, bf16[512,128]{1,0:T(8,128)(2,1)S(1)}, bf16[16,512]{1,0:T(8,128)(2,1)S(1)}) custom-call(s32[2]{0:T(128)S(1)} %pad_add_fusion.place_ref, bf16[512,256]{1,0:T(8,128)(2,1)S(1)} %get-tuple-element.44.field_ref, bf16[80,512]{1,0:T(8,128)(2,1)S(1)} %collective-permute-done.5.two, ...), custom_call_target="tpu_custom_call" | custom-call | flops 444596224 | bytes 2523208 | tf_op jit(solution)/shard_map/pallas_call | solution.py:45
  67.1 2.5 %collective-permute-start.7 = (bf16[16,512]{1,0:T(8,128)(2,1)S(1)}, bf16[16,512]{1,0:T(8,128)(2,1)S(1)}, u32[]{:S(2)}, u32[]{:S(2)}) collective-permute-start(bf16[16,512]{1,0:T(8,128)(2,1)S(1)} %get-tuple-element.51), channel_id=1, source_target_pairs={{0,1},{1,0},{2,3},{3,2},{4,5},{5,4},{6,7},{7,6},{8,9},{9,8},{10,11... | collective-permute-start | bytes 49160 | tf_op jit(solution)/shard_map/ppermute | solution.py:33
  69.6 0.0 copy-done.7
  69.6 0.8 %shard_map.155 = (f32[512,128]{1,0:T(8,128)}, f32[512,128]{1,0:T(8,128)S(1)}) custom-call(f32[512,128]{1,0:T(8,128)S(1)} %get-tuple-element.48.residual_ref, bf16[512,128]{1,0:T(8,128)(2,1)S(1)} %get-tuple-element.49.rounded_ref, s32[1,128]{1,0:T(1,128)S(1)} %bitcast.25), custom_call_target="tpu_custom_call" | custom-call | flops 111149056 | bytes 393728 | tf_op jit(solution)/shard_map/pallas_call | solution.py:45
  70.4 2.3 %collective-permute-done.7.incoming = bf16[16,512]{1,0:T(8,128)(2,1)S(1)} collective-permute-done((bf16[16,512]{1,0:T(8,128)(2,1)S(1)}, bf16[16,512]{1,0:T(8,128)(2,1)S(1)}, u32[]{:S(2)}, u32[]{:S(2)}) %collective-permute-start.7) | collective-permute-done | bytes 16416 | tf_op jit(solution)/shard_map/ppermute | solution.py:33
  72.7 0.0 copy-done.6
  72.7 1.6 %shard_map.156 = f32[512,128]{1,0:T(8,128)} custom-call(s32[2]{0:T(128)S(1)} %pad_add_fusion.place_ref, f32[512,128]{1,0:T(8,128)S(1)} %get-tuple-element.50.half_ref, bf16[16,512]{1,0:T(8,128)(2,1)S(1)} %collective-permute-done.7.incoming, s32[1,128]{1,0:T(1,128)S(1)} %bitcast.26, bf16[64,64]{1,0:T(8,128)(2,1)S(1)} %copy-done.6, ...), custom_call_target="tpu_custom_call" | custom-call | flops 111149056 | bytes 811528 | tf_op jit(solution)/shard_map/pallas_call | solution.py:45
Async XLA Ops:
  0.6 25.3 %copy-start.2 = (f32[64,8,128]{2,1,0:T(8,128)S(1)}, f32[64,8,128]{2,1,0:T(8,128)}, u32[]{:S(2)}) copy-start(f32[64,8,128]{2,1,0:T(8,128)} %param.15) | copy-start | bytes 786436
  0.6 19.7 %copy-start.1 = (f32[64,8,128]{2,1,0:T(8,128)S(1)}, f32[64,8,128]{2,1,0:T(8,128)}, u32[]{:S(2)}) copy-start(f32[64,8,128]{2,1,0:T(8,128)} %param.14) | copy-start | bytes 786436
  0.7 19.7 %copy-start.5 = (bf16[2,64,64]{2,1,0:T(8,128)(2,1)S(1)}, bf16[2,64,64]{2,1,0:T(8,128)(2,1)}, u32[]{:S(2)}) copy-start(bf16[2,64,64]{2,1,0:T(8,128)(2,1)} %smooth.1) | copy-start | bytes 49156
  0.7 19.7 %copy-start.3 = (bf16[6,2,64,64]{3,2,1,0:T(8,128)(2,1)S(1)}, bf16[6,2,64,64]{3,2,1,0:T(8,128)(2,1)}, u32[]{:S(2)}) copy-start(bf16[6,2,64,64]{3,2,1,0:T(8,128)(2,1)} %face.1) | copy-start | bytes 294916
  0.7 19.7 %copy-start.4 = (bf16[2,64,64]{2,1,0:T(8,128)(2,1)S(1)}, bf16[2,64,64]{2,1,0:T(8,128)(2,1)}, u32[]{:S(2)}) copy-start(bf16[2,64,64]{2,1,0:T(8,128)(2,1)} %diag.1) | copy-start | bytes 49156
  2.7 3.7 %collective-permute-start = (bf16[1056,128]{1,0:T(8,128)(2,1)}, bf16[1056,128]{1,0:T(8,128)(2,1)S(1)}, u32[]{:S(2)}, u32[]{:S(2)}) collective-permute-start(bf16[1056,128]{1,0:T(8,128)(2,1)} %shard_map.149.mine), channel_id=1, source_target_pairs={{0,4},{4,0},{8,12},{12,8},{16,20},{20,16},{24,28},{28,24},{32,36},... | collective-permute-start | bytes 811016 | tf_op jit(solution)/shard_map/ppermute | solution.py:33
  6.3 1.0 %copy-start = (bf16[1056,128]{1,0:T(8,128)(2,1)S(1)}, bf16[1056,128]{1,0:T(8,128)(2,1)}, u32[]{:S(2)}) copy-start(bf16[1056,128]{1,0:T(8,128)(2,1)} %shard_map.149.mine) | copy-start | bytes 811012
  8.7 17.2 %collective-permute-start.1 = (bf16[80,512]{1,0:T(8,128)(2,1)}, bf16[80,512]{1,0:T(8,128)(2,1)}, u32[]{:S(2)}, u32[]{:S(2)}) collective-permute-start(bf16[80,512]{1,0:T(8,128)(2,1)} %get-tuple-element.29), channel_id=1, source_target_pairs={{8,16},{16,8},{12,20},{20,12},{24,32},{32,24},{28,36},{36,28},{40,... | collective-permute-start | bytes 245768 | tf_op jit(solution)/shard_map/ppermute | solution.py:33
  12.0 14.0 %collective-permute-start.2 = (bf16[80,512]{1,0:T(8,128)(2,1)}, bf16[80,512]{1,0:T(8,128)(2,1)}, u32[]{:S(2)}, u32[]{:S(2)}) collective-permute-start(bf16[80,512]{1,0:T(8,128)(2,1)} %get-tuple-element.30), channel_id=1, source_target_pairs={{0,8},{8,0},{4,12},{12,4},{16,24},{24,16},{20,28},{28,20},{32,40},... | collective-permute-start | bytes 245768 | tf_op jit(solution)/shard_map/ppermute | solution.py:33
  16.0 9.9 %all-to-all-start = ((bf16[4,16,512]{2,1,0:T(8,128)(2,1)}), bf16[4,16,512]{2,1,0:T(8,128)(2,1)S(1)}, u32[]{:S(2)}, u32[]{:S(2)}) async-start(bf16[4,16,512]{2,1,0:T(8,128)(2,1)} %bitcast.6), calls=%async_computation | async-start | bytes 131072 | tf_op jit(solution)/shard_map/all_to_all | solution.py:295
  30.3 15.0 %collective-permute-start.3 = (bf16[80,512]{1,0:T(8,128)(2,1)S(1)}, bf16[80,512]{1,0:T(8,128)(2,1)S(1)}, u32[]{:S(2)}, u32[]{:S(2)}) collective-permute-start(bf16[80,512]{1,0:T(8,128)(2,1)S(1)} %get-tuple-element.40), channel_id=1, source_target_pairs={{8,16},{16,8},{12,20},{20,12},{24,32},{32,24},{28,36},{36,28},{40,... | collective-permute-start | bytes 245768 | tf_op jit(solution)/shard_map/ppermute | solution.py:33
  32.2 13.1 %collective-permute-start.4 = (bf16[80,512]{1,0:T(8,128)(2,1)S(1)}, bf16[80,512]{1,0:T(8,128)(2,1)S(1)}, u32[]{:S(2)}, u32[]{:S(2)}) collective-permute-start(bf16[80,512]{1,0:T(8,128)(2,1)S(1)} %get-tuple-element.41), channel_id=1, source_target_pairs={{0,8},{8,0},{4,12},{12,4},{16,24},{24,16},{20,28},{28,20},{32,40},... | collective-permute-start | bytes 245768 | tf_op jit(solution)/shard_map/ppermute | solution.py:33
  45.3 20.1 %copy-start.8 = (s32[16]{0:T(128)S(1)}, s32[16]{0:T(128)}, u32[]{:S(2)}) copy-start(s32[16]{0:T(128)} %param.27) | copy-start | bytes 196
  49.1 16.2 %collective-permute-start.5 = (bf16[80,512]{1,0:T(8,128)(2,1)S(1)}, bf16[80,512]{1,0:T(8,128)(2,1)S(1)}, u32[]{:S(2)}, u32[]{:S(2)}) collective-permute-start(bf16[80,512]{1,0:T(8,128)(2,1)S(1)} %get-tuple-element.45), channel_id=1, source_target_pairs={{8,16},{16,8},{12,20},{20,12},{24,32},{32,24},{28,36},{36,28},{40,... | collective-permute-start | bytes 245768 | tf_op jit(solution)/shard_map/ppermute | solution.py:33
  51.0 14.3 %collective-permute-start.6 = (bf16[80,512]{1,0:T(8,128)(2,1)S(1)}, bf16[80,512]{1,0:T(8,128)(2,1)S(1)}, u32[]{:S(2)}, u32[]{:S(2)}) collective-permute-start(bf16[80,512]{1,0:T(8,128)(2,1)S(1)} %get-tuple-element.46), channel_id=1, source_target_pairs={{0,8},{8,0},{4,12},{12,4},{16,24},{24,16},{20,28},{28,20},{32,40},... | collective-permute-start | bytes 245768 | tf_op jit(solution)/shard_map/ppermute | solution.py:33
  65.3 4.3 %copy-start.7 = (s32[128]{0:T(128)S(1)}, s32[128]{0:T(128)}, u32[]{:S(2)}) copy-start(s32[128]{0:T(128)} %param.26) | copy-start | bytes 1540
  65.3 7.4 %copy-start.6 = (bf16[64,64]{1,0:T(8,128)(2,1)S(1)}, bf16[64,64]{1,0:T(8,128)(2,1)}, u32[]{:S(2)}) copy-start(bf16[64,64]{1,0:T(8,128)(2,1)} %inverse.1) | copy-start | bytes 24580
  67.1 5.6 %collective-permute-start.7 = (bf16[16,512]{1,0:T(8,128)(2,1)S(1)}, bf16[16,512]{1,0:T(8,128)(2,1)S(1)}, u32[]{:S(2)}, u32[]{:S(2)}) collective-permute-start(bf16[16,512]{1,0:T(8,128)(2,1)S(1)} %get-tuple-element.51), channel_id=1, source_target_pairs={{0,1},{1,0},{2,3},{3,2},{4,5},{5,4},{6,7},{7,6},{8,9},{9,8},{10,11... | collective-permute-start | bytes 49160 | tf_op jit(solution)/shard_map/ppermute | solution.py:33

commit v4 on v3

--- a/solution.py
+++ b/solution.py
@@ -101,9 +101,8 @@
     message[2 * ROWS :, :] = ints[...].astype(BF)
     for i, field in enumerate((guess, rhs)):
         copies[6 + i].wait()
-        for r in range(RHS):
-            start = i * ROWS + r * DOF
-            message[start : start + DOF, :] = field[pl.ds(r, DOF, stride=RHS), :].astype(BF)
+        blocks = [field[pl.ds(r, DOF, stride=RHS), :].astype(BF) for r in range(RHS)]
+        message[i * ROWS : (i + 1) * ROWS, :] = jnp.concatenate(blocks, axis=0)
 
 
 def pack_kernel(place_ref, mine, other, field_ref, ints_ref, choice_ref, *messages):
@@ -191,6 +190,7 @@
     else:
         (before,) = before
     beside = jnp.dot(extend(field_ref, (one, two, side)), pick[...], preferred_element_type=F32).astype(BF)
+    parts = []
     for r in range(RHS):
         rows = slice(r * DOF, (r + 1) * DOF)
         stack = []
@@ -199,11 +199,13 @@
             stack += [masked(block, masks[2 * d]), masked(block, masks[2 * d + 1])]
         product = jnp.dot(wide[...], jnp.concatenate(stack, axis=0), preferred_element_type=F32)
         rounded = (rhs[rows, :] - product).astype(BF)
-        both = jnp.concatenate([masked(rounded, masks[0]), masked(rounded, masks[1])], axis=0)
-        new = before[rows, :] + jnp.dot(smooth[...], both, preferred_element_type=F32)
-        after[rows, :] = new
-        next_field[rows, :] = new.astype(BF)
-    send(choice[...], next_field[...], zip(messages, (CROSS, CROSS, SIDE)))
+        parts.append(jnp.concatenate([masked(rounded, masks[0]), masked(rounded, masks[1])], axis=0))
+    changes = [jnp.dot(smooth[...], part, preferred_element_type=F32) for part in parts]
+    new = before[...] + jnp.concatenate(changes, axis=0)
+    rounded = new.astype(BF)
+    send(choice[...], rounded, zip(messages, (CROSS, CROSS, SIDE)))
+    after[...] = new
+    next_field[...] = rounded
 
 
 def residual_kernel(place_ref, field_ref, two, one, side, pick, masks, wide, rhs, pair, residual_ref, rounded_ref, message):
@@ -217,6 +219,7 @@
     beside = jnp.dot(extended, jnp.concatenate(beside, axis=1), preferred_element_type=F32).astype(BF)
     field = field_ref[:, own]
     kinds = [masks[i, :, own] for i in range(2 * FACES + 2)]
+    parts = []
     for r in range(0, RHS, 2):
         halves = []
         for s in (r, r + 1):
@@ -227,12 +230,12 @@
                 stack += [masked(block, kinds[2 * d]), masked(block, kinds[2 * d + 1])]
             halves.append(jnp.concatenate(stack, axis=0))
         product = jnp.dot(wide[...], jnp.concatenate(halves, axis=1), preferred_element_type=F32)
-        for i in range(2):
-            rows = slice((r + i) * DOF, (r + i + 1) * DOF)
-            part = rhs[rows, own] - product[:, i * E : (i + 1) * E]
-            residual_ref[rows, :] = part
-            rounded_ref[rows, :] = part.astype(BF)
-    send(picker(pair[...], E), rounded_ref[...], [(message, PAIRS)])
+        parts += [rhs[(r + i) * DOF : (r + i + 1) * DOF, own] - product[:, i * E : (i + 1) * E] for i in range(2)]
+    residual = jnp.concatenate(parts, axis=0)
+    rounded = residual.astype(BF)
+    send(picker(pair[...], E), rounded, [(message, PAIRS)])
+    residual_ref[...] = residual
+    rounded_ref[...] = rounded
 
 
 def mate_picker(partner, first, count):
@@ -240,13 +243,15 @@
 
 
 def local_kernel(residual_ref, rounded_ref, partner, out_ref, half_ref):
-    rest = (residual_ref[...] - rounded_ref[...].astype(F32)).astype(BF)
+    residual = residual_ref[...]
+    rounded = rounded_ref[...]
+    rest = (residual - rounded.astype(F32)).astype(BF)
     local = mate_picker(partner[...], 0, E)
-    mates = jnp.dot(rounded_ref[...], local, preferred_element_type=F32)
+    mates = jnp.dot(rounded, local, preferred_element_type=F32)
     mates = mates + jnp.dot(rest, local, preferred_element_type=F32)
-    half_ref[...] = residual_ref[...] + mates
     for r in range(RHS):
-        out_ref[pl.ds(r, DOF, stride=RHS), :] = residual_ref[r * DOF : (r + 1) * DOF, :]
+        out_ref[pl.ds(r, DOF, stride=RHS), :] = residual[r * DOF : (r + 1) * DOF, :]
+    half_ref[...] = residual + mates
 
 
 def coarse_kernel(place_ref, half_ref, incoming, partner, inverse, iterate, solution_ref):
@@ -255,12 +260,13 @@
         incoming[...], mate_picker(partner[...], E, PAIRS), (((0,), (0,)), ((), ())), preferred_element_type=F32
     )
     coarse = (half_ref[...] + mates).astype(BF)
+    solved = []
     for r in range(0, RHS, 2):
         pair = jnp.concatenate([coarse[s * DOF : (s + 1) * DOF, :] for s in (r, r + 1)], axis=1)
         update = jnp.dot(inverse[...], pair, preferred_element_type=F32)
-        for i in range(2):
-            s = r + i
-            solution_ref[pl.ds(s, DOF, stride=RHS), :] = iterate[s * DOF : (s + 1) * DOF, own] + update[:, i * E : (i + 1) * E]
+        solved += [iterate[(r + i) * DOF : (r + i + 1) * DOF, own] + update[:, i * E : (i + 1) * E] for i in range(2)]
+    for r in range(RHS):
+        solution_ref[pl.ds(r, DOF, stride=RHS), :] = solved[r]
 
 
 def body(

time: 74.9 us -> 72.1 us (0.963)
  Pallas kernels: 16.8 us -> 14.1 us
    pallas_call x8, Pallas kernels: 16.8 us -> 14.1 us  [call(): pl.pallas_call(kernel, out_shape=[jax.ShapeDtypeStruct(s, d) for s, d in...]
where the time goes in v4:
time: 72.1 us; the launch traced here: 71.6 us
  starting transfers between devices  31.1 us (43%)
  blocking collectives  16 us (22%)
  Pallas kernels  14.1 us (20%)
  waiting for transfers between devices  8.48 us (12%)
  local copies, waits for them, and re-layouts  0.99 us (1%)
  between operations  0.86 us (1%)
    ppermute x8, starting transfers between devices, swap(): return lax.ppermute(array, axis, route)  26.8 us
    all_to_all x2, blocking collectives, exchange(): side = lax.all_to_all(side, 'sub', 0, 0, tiled=True)  16 us
    pallas_call x8, Pallas kernels, call(): pl.pallas_call(kernel, out_shape=[jax.ShapeDtypeStruct(s, d) for s, d in...  14.1 us
    all_to_all x1, waiting for transfers between devices, exchange(): side = lax.all_to_all(side, 'sub', 0, 0, tiled=True)  4.55 us
    all_to_all x1, starting transfers between devices, exchange(): side = lax.all_to_all(side, 'sub', 0, 0, tiled=True)  4.3 us
    ppermute x8, waiting for transfers between devices, swap(): return lax.ppermute(array, axis, route)  3.93 us
  transfers between devices with their start and end apart: 9, of which 3 were waited for; matrix products, arithmetic and copies ran while one was open for 0% of the time, Pallas kernels for 3%

profile of v4, /device:TPU:240, one launch (start us, length us, event | category | flops | bytes accessed | tf_op | source)
XLA Modules:
  0.0 71.6 jit_solution(441083667082144786)
XLA Ops:
  0.6 0.0 copy-start.2
  0.6 0.0 copy-start.1
  0.7 0.0 copy-start.5
  0.7 0.0 copy-start.3
  0.7 0.0 copy-start.4
  0.7 2.0 %shard_map.149.mine = bf16[1056,128]{1,0:T(8,128)(2,1)} custom-call(s32[2,32]{1,0:T(2,128)} %refs_0_.1, s32[2,8]{1,0:T(2,128)} %refs_1_.1, s32[1,8]{1,0:T(1,128)} %bitcast.29, s32[1,128]{1,0:T(1,128)} %bitcast.30, s32[6,128]{1,0:T(8,128)} %refs_4_.1, s32[6,128]{1,0:T(8,128)} %refs_5_.1, f32[512,128]{1,0:T(8,128)} %bitcast.19, f32[512,128]{1,0:T(8,128)} %bitcast.16), custom_call_target="tpu_custom_call" | custom-call | bytes 531296 | tf_op jit(solution)/shard_map/pallas_call | solution.py:45
  2.7 1.9 %collective-permute-start = (bf16[1056,128]{1,0:T(8,128)(2,1)}, bf16[1056,128]{1,0:T(8,128)(2,1)S(1)}, u32[]{:S(2)}, u32[]{:S(2)}) collective-permute-start(bf16[1056,128]{1,0:T(8,128)(2,1)} %shard_map.149.mine), channel_id=1, source_target_pairs={{0,4},{4,0},{8,12},{12,8},{16,20},{20,16},{24,28},{28,24},{32,36},... | collective-permute-start | bytes 811016 | tf_op jit(solution)/shard_map/ppermute | solution.py:33
  4.6 0.1 pad_add_fusion.place_ref
  4.7 1.6 %collective-permute-done.other.refs_1_ = bf16[1056,128]{1,0:T(8,128)(2,1)S(1)} collective-permute-done((bf16[1056,128]{1,0:T(8,128)(2,1)}, bf16[1056,128]{1,0:T(8,128)(2,1)S(1)}, u32[]{:S(2)}, u32[]{:S(2)}) %collective-permute-start) | collective-permute-done | bytes 270368 | tf_op jit(solution)/shard_map/ppermute | solution.py:33
  6.3 0.0 copy-start
  6.3 1.0 %copy-done = bf16[1056,128]{1,0:T(8,128)(2,1)S(1)} copy-done((bf16[1056,128]{1,0:T(8,128)(2,1)S(1)}, bf16[1056,128]{1,0:T(8,128)(2,1)}, u32[]{:S(2)}) %copy-start) | copy-done | bytes 270360
  7.3 1.5 %shard_map.150 = (bf16[512,256]{1,0:T(8,128)(2,1)S(1)}, s32[2,32,128]{2,1,0:T(8,128)S(1)}, bf16[160,256]{1,0:T(8,128)(2,1)S(1)}, bf16[80,512]{1,0:T(8,128)(2,1)}...) custom-call(s32[2]{0:T(128)S(1)} %pad_add_fusion.place_ref, bf16[1056,128]{1,0:T(8,128)(2,1)S(1)} %copy-done, ...), custom_call_target="tpu_custom_call" | custom-call | flops 41943040 | bytes 540680 | tf_op jit(solution)/shard_map/pallas_call | solution.py:45
  8.7 3.2 %collective-permute-start.1 = (bf16[80,512]{1,0:T(8,128)(2,1)}, bf16[80,512]{1,0:T(8,128)(2,1)}, u32[]{:S(2)}, u32[]{:S(2)}) collective-permute-start(bf16[80,512]{1,0:T(8,128)(2,1)} %get-tuple-element.29), channel_id=1, source_target_pairs={{8,16},{16,8},{12,20},{20,12},{24,32},{32,24},{28,36},{36,28},{40,... | collective-permute-start | bytes 245768 | tf_op jit(solution)/shard_map/ppermute | solution.py:33
  12.0 4.0 %collective-permute-start.2 = (bf16[80,512]{1,0:T(8,128)(2,1)}, bf16[80,512]{1,0:T(8,128)(2,1)}, u32[]{:S(2)}, u32[]{:S(2)}) collective-permute-start(bf16[80,512]{1,0:T(8,128)(2,1)} %get-tuple-element.30), channel_id=1, source_target_pairs={{0,8},{8,0},{4,12},{12,4},{16,24},{24,16},{20,28},{28,20},{32,40},... | collective-permute-start | bytes 245768 | tf_op jit(solution)/shard_map/ppermute | solution.py:33
  16.0 4.3 %all-to-all-start = ((bf16[4,16,512]{2,1,0:T(8,128)(2,1)}), bf16[4,16,512]{2,1,0:T(8,128)(2,1)S(1)}, u32[]{:S(2)}, u32[]{:S(2)}) async-start(bf16[4,16,512]{2,1,0:T(8,128)(2,1)} %bitcast.6), calls=%async_computation | async-start | bytes 131072 | tf_op jit(solution)/shard_map/all_to_all | solution.py:301
  20.3 0.0 copy-done.1
  20.3 0.0 copy-done.5
  20.3 0.0 copy-done.3
  20.4 0.0 copy-done.4
  20.4 1.1 %shard_map.151 = (bf16[416,1536]{1,0:T(8,128)(2,1)S(1)}, bf16[14,16,256]{2,1,0:T(8,128)(2,1)S(1)}, bf16[64,896]{1,0:T(8,128)(2,1)S(1)}, bf16[64,128]{1,0:T(8,128)(2,1)S(1)}, f32[512,256]{1,0:T(8,128)S(1)}) custom-call(s32[2]{0:T(128)S(1)} %pad_add_fusion.place_ref, bf16[2,64,64]{2,1,0:T(8,128)(2,1)S(1)} %copy-done.4, bf16[6,2,64,64]{3,2,1,0:T(8,128)(2,1)S(1)} %copy-done.3, ...), custom_call_target="tpu_custom_call" | custom-call | flops 1000000 | bytes 696328 | tf_op jit(solution)/shard_map/pallas_call | solution.py:45
  21.4 4.5 %all-to-all-done = bf16[4,16,512]{2,1,0:T(8,128)(2,1)S(1)} async-done(((bf16[4,16,512]{2,1,0:T(8,128)(2,1)}), bf16[4,16,512]{2,1,0:T(8,128)(2,1)S(1)}, u32[]{:S(2)}, u32[]{:S(2)}) %all-to-all-start) | async-done | bytes 65568 | tf_op jit(solution)/shard_map/all_to_all | solution.py:301
  26.0 0.0 collective-permute-done.1.two
  26.0 0.0 collective-permute-done.2.one
  26.0 0.0 copy-done.2
  26.0 2.9 %shard_map.152 = (f32[512,256]{1,0:T(8,128)S(1)}, bf16[512,256]{1,0:T(8,128)(2,1)S(1)}, bf16[80,512]{1,0:T(8,128)(2,1)S(1)}, bf16[80,512]{1,0:T(8,128)(2,1)S(1)}, bf16[64,512]{1,0:T(8,128)(2,1)S(1)}) custom-call(s32[2]{0:T(128)S(1)} %pad_add_fusion.place_ref, bf16[512,256]{1,0:T(8,128)(2,1)S(1)} %get-tuple-element.28.field_ref, ...), custom_call_target="tpu_custom_call" | custom-call | flops 889192448 | bytes 3153928 | tf_op jit(solution)/shard_map/pallas_call | solution.py:45
  28.9 1.9 %collective-permute-start.3 = (bf16[80,512]{1,0:T(8,128)(2,1)S(1)}, bf16[80,512]{1,0:T(8,128)(2,1)S(1)}, u32[]{:S(2)}, u32[]{:S(2)}) collective-permute-start(bf16[80,512]{1,0:T(8,128)(2,1)S(1)} %get-tuple-element.40), channel_id=1, source_target_pairs={{8,16},{16,8},{12,20},{20,12},{24,32},{32,24},{28,36},{36,28},{40,... | collective-permute-start | bytes 245768 | tf_op jit(solution)/shard_map/ppermute | solution.py:33
  30.8 5.0 %collective-permute-start.4 = (bf16[80,512]{1,0:T(8,128)(2,1)S(1)}, bf16[80,512]{1,0:T(8,128)(2,1)S(1)}, u32[]{:S(2)}, u32[]{:S(2)}) collective-permute-start(bf16[80,512]{1,0:T(8,128)(2,1)S(1)} %get-tuple-element.41), channel_id=1, source_target_pairs={{0,8},{8,0},{4,12},{12,4},{16,24},{24,16},{20,28},{28,20},{32,40},... | collective-permute-start | bytes 245768 | tf_op jit(solution)/shard_map/ppermute | solution.py:33
  35.9 8.0 %all_to_all.33 = bf16[4,16,512]{2,1,0:T(8,128)(2,1)S(1)} all-to-all(bf16[4,16,512]{2,1,0:T(8,128)(2,1)S(1)} %bitcast.24), channel_id=1, replica_groups=mesh['dom'=128,'sub'=4] {'sub'}, dimensions={0} | all-to-all | bytes 131072 | tf_op jit(solution)/shard_map/all_to_all | solution.py:301
  43.9 0.0 collective-permute-done.3.two
  43.9 0.0 collective-permute-done.4.one
  43.9 0.0 copy-start.8
  43.9 2.5 %shard_map.153 = (f32[512,256]{1,0:T(8,128)S(1)}, bf16[512,256]{1,0:T(8,128)(2,1)S(1)}, bf16[80,512]{1,0:T(8,128)(2,1)S(1)}, bf16[80,512]{1,0:T(8,128)(2,1)S(1)}, bf16[64,512]{1,0:T(8,128)(2,1)S(1)}) custom-call(s32[2]{0:T(128)S(1)} %pad_add_fusion.place_ref, bf16[512,256]{1,0:T(8,128)(2,1)S(1)} %get-tuple-element.39.field_ref, ...), custom_call_target="tpu_custom_call" | custom-call | flops 889192448 | bytes 3145736 | tf_op jit(solution)/shard_map/pallas_call | solution.py:45
  46.4 1.9 %collective-permute-start.5 = (bf16[80,512]{1,0:T(8,128)(2,1)S(1)}, bf16[80,512]{1,0:T(8,128)(2,1)S(1)}, u32[]{:S(2)}, u32[]{:S(2)}) collective-permute-start(bf16[80,512]{1,0:T(8,128)(2,1)S(1)} %get-tuple-element.45), channel_id=1, source_target_pairs={{8,16},{16,8},{12,20},{20,12},{24,32},{32,24},{28,36},{36,28},{40,... | collective-permute-start | bytes 245768 | tf_op jit(solution)/shard_map/ppermute | solution.py:33
  48.3 6.3 %collective-permute-start.6 = (bf16[80,512]{1,0:T(8,128)(2,1)S(1)}, bf16[80,512]{1,0:T(8,128)(2,1)S(1)}, u32[]{:S(2)}, u32[]{:S(2)}) collective-permute-start(bf16[80,512]{1,0:T(8,128)(2,1)S(1)} %get-tuple-element.46), channel_id=1, source_target_pairs={{0,8},{8,0},{4,12},{12,4},{16,24},{24,16},{20,28},{28,20},{32,40},... | collective-permute-start | bytes 245768 | tf_op jit(solution)/shard_map/ppermute | solution.py:33
  54.6 8.0 %all_to_all.34 = bf16[4,16,512]{2,1,0:T(8,128)(2,1)S(1)} all-to-all(bf16[4,16,512]{2,1,0:T(8,128)(2,1)S(1)} %bitcast.23), channel_id=1, replica_groups=mesh['dom'=128,'sub'=4] {'sub'}, dimensions={0} | all-to-all | bytes 131072 | tf_op jit(solution)/shard_map/all_to_all | solution.py:301
  62.5 0.0 copy-start.7
  62.6 0.0 collective-permute-done.5.two
  62.6 0.0 collective-permute-done.6.one
  62.6 0.0 copy-done.8
  62.6 0.0 copy-start.6
  62.6 1.7 %shard_map.154 = (f32[512,128]{1,0:T(8,128)S(1)}, bf16[512,128]{1,0:T(8,128)(2,1)S(1)}, bf16[16,512]{1,0:T(8,128)(2,1)S(1)}) custom-call(s32[2]{0:T(128)S(1)} %pad_add_fusion.place_ref, bf16[512,256]{1,0:T(8,128)(2,1)S(1)} %get-tuple-element.44.field_ref, bf16[80,512]{1,0:T(8,128)(2,1)S(1)} %collective-permute-done.5.two, ...), custom_call_target="tpu_custom_call" | custom-call | flops 444596224 | bytes 2523208 | tf_op jit(solution)/shard_map/pallas_call | solution.py:45
  64.3 2.5 %collective-permute-start.7 = (bf16[16,512]{1,0:T(8,128)(2,1)S(1)}, bf16[16,512]{1,0:T(8,128)(2,1)S(1)}, u32[]{:S(2)}, u32[]{:S(2)}) collective-permute-start(bf16[16,512]{1,0:T(8,128)(2,1)S(1)} %get-tuple-element.51), channel_id=1, source_target_pairs={{0,1},{1,0},{2,3},{3,2},{4,5},{5,4},{6,7},{7,6},{8,9},{9,8},{10,11... | collective-permute-start | bytes 49160 | tf_op jit(solution)/shard_map/ppermute | solution.py:33
  66.8 0.0 copy-done.7
  66.8 0.8 %shard_map.155 = (f32[512,128]{1,0:T(8,128)}, f32[512,128]{1,0:T(8,128)S(1)}) custom-call(f32[512,128]{1,0:T(8,128)S(1)} %get-tuple-element.48.residual_ref, bf16[512,128]{1,0:T(8,128)(2,1)S(1)} %get-tuple-element.49.rounded_ref, s32[1,128]{1,0:T(1,128)S(1)} %bitcast.25), custom_call_target="tpu_custom_call" | custom-call | flops 111149056 | bytes 393728 | tf_op jit(solution)/shard_map/pallas_call | solution.py:45
  67.7 2.3 %collective-permute-done.7.incoming = bf16[16,512]{1,0:T(8,128)(2,1)S(1)} collective-permute-done((bf16[16,512]{1,0:T(8,128)(2,1)S(1)}, bf16[16,512]{1,0:T(8,128)(2,1)S(1)}, u32[]{:S(2)}, u32[]{:S(2)}) %collective-permute-start.7) | collective-permute-done | bytes 16416 | tf_op jit(solution)/shard_map/ppermute | solution.py:33
  70.0 0.0 copy-done.6
  70.0 1.6 %shard_map.156 = f32[512,128]{1,0:T(8,128)} custom-call(s32[2]{0:T(128)S(1)} %pad_add_fusion.place_ref, f32[512,128]{1,0:T(8,128)S(1)} %get-tuple-element.50.half_ref, bf16[16,512]{1,0:T(8,128)(2,1)S(1)} %collective-permute-done.7.incoming, s32[1,128]{1,0:T(1,128)S(1)} %bitcast.26, bf16[64,64]{1,0:T(8,128)(2,1)S(1)} %copy-done.6, ...), custom_call_target="tpu_custom_call" | custom-call | flops 111149056 | bytes 811528 | tf_op jit(solution)/shard_map/pallas_call | solution.py:45
Async XLA Ops:
  0.6 25.3 %copy-start.2 = (f32[64,8,128]{2,1,0:T(8,128)S(1)}, f32[64,8,128]{2,1,0:T(8,128)}, u32[]{:S(2)}) copy-start(f32[64,8,128]{2,1,0:T(8,128)} %param.15) | copy-start | bytes 786436
  0.6 19.7 %copy-start.1 = (f32[64,8,128]{2,1,0:T(8,128)S(1)}, f32[64,8,128]{2,1,0:T(8,128)}, u32[]{:S(2)}) copy-start(f32[64,8,128]{2,1,0:T(8,128)} %param.14) | copy-start | bytes 786436
  0.7 19.7 %copy-start.5 = (bf16[2,64,64]{2,1,0:T(8,128)(2,1)S(1)}, bf16[2,64,64]{2,1,0:T(8,128)(2,1)}, u32[]{:S(2)}) copy-start(bf16[2,64,64]{2,1,0:T(8,128)(2,1)} %smooth.1) | copy-start | bytes 49156
  0.7 19.7 %copy-start.3 = (bf16[6,2,64,64]{3,2,1,0:T(8,128)(2,1)S(1)}, bf16[6,2,64,64]{3,2,1,0:T(8,128)(2,1)}, u32[]{:S(2)}) copy-start(bf16[6,2,64,64]{3,2,1,0:T(8,128)(2,1)} %face.1) | copy-start | bytes 294916
  0.7 19.7 %copy-start.4 = (bf16[2,64,64]{2,1,0:T(8,128)(2,1)S(1)}, bf16[2,64,64]{2,1,0:T(8,128)(2,1)}, u32[]{:S(2)}) copy-start(bf16[2,64,64]{2,1,0:T(8,128)(2,1)} %diag.1) | copy-start | bytes 49156
  2.7 3.7 %collective-permute-start = (bf16[1056,128]{1,0:T(8,128)(2,1)}, bf16[1056,128]{1,0:T(8,128)(2,1)S(1)}, u32[]{:S(2)}, u32[]{:S(2)}) collective-permute-start(bf16[1056,128]{1,0:T(8,128)(2,1)} %shard_map.149.mine), channel_id=1, source_target_pairs={{0,4},{4,0},{8,12},{12,8},{16,20},{20,16},{24,28},{28,24},{32,36},... | collective-permute-start | bytes 811016 | tf_op jit(solution)/shard_map/ppermute | solution.py:33
  6.3 1.0 %copy-start = (bf16[1056,128]{1,0:T(8,128)(2,1)S(1)}, bf16[1056,128]{1,0:T(8,128)(2,1)}, u32[]{:S(2)}) copy-start(bf16[1056,128]{1,0:T(8,128)(2,1)} %shard_map.149.mine) | copy-start | bytes 811012
  8.7 17.2 %collective-permute-start.1 = (bf16[80,512]{1,0:T(8,128)(2,1)}, bf16[80,512]{1,0:T(8,128)(2,1)}, u32[]{:S(2)}, u32[]{:S(2)}) collective-permute-start(bf16[80,512]{1,0:T(8,128)(2,1)} %get-tuple-element.29), channel_id=1, source_target_pairs={{8,16},{16,8},{12,20},{20,12},{24,32},{32,24},{28,36},{36,28},{40,... | collective-permute-start | bytes 245768 | tf_op jit(solution)/shard_map/ppermute | solution.py:33
  12.0 14.0 %collective-permute-start.2 = (bf16[80,512]{1,0:T(8,128)(2,1)}, bf16[80,512]{1,0:T(8,128)(2,1)}, u32[]{:S(2)}, u32[]{:S(2)}) collective-permute-start(bf16[80,512]{1,0:T(8,128)(2,1)} %get-tuple-element.30), channel_id=1, source_target_pairs={{0,8},{8,0},{4,12},{12,4},{16,24},{24,16},{20,28},{28,20},{32,40},... | collective-permute-start | bytes 245768 | tf_op jit(solution)/shard_map/ppermute | solution.py:33
  16.0 9.9 %all-to-all-start = ((bf16[4,16,512]{2,1,0:T(8,128)(2,1)}), bf16[4,16,512]{2,1,0:T(8,128)(2,1)S(1)}, u32[]{:S(2)}, u32[]{:S(2)}) async-start(bf16[4,16,512]{2,1,0:T(8,128)(2,1)} %bitcast.6), calls=%async_computation | async-start | bytes 131072 | tf_op jit(solution)/shard_map/all_to_all | solution.py:301
  28.9 15.0 %collective-permute-start.3 = (bf16[80,512]{1,0:T(8,128)(2,1)S(1)}, bf16[80,512]{1,0:T(8,128)(2,1)S(1)}, u32[]{:S(2)}, u32[]{:S(2)}) collective-permute-start(bf16[80,512]{1,0:T(8,128)(2,1)S(1)} %get-tuple-element.40), channel_id=1, source_target_pairs={{8,16},{16,8},{12,20},{20,12},{24,32},{32,24},{28,36},{36,28},{40,... | collective-permute-start | bytes 245768 | tf_op jit(solution)/shard_map/ppermute | solution.py:33
  30.8 13.1 %collective-permute-start.4 = (bf16[80,512]{1,0:T(8,128)(2,1)S(1)}, bf16[80,512]{1,0:T(8,128)(2,1)S(1)}, u32[]{:S(2)}, u32[]{:S(2)}) collective-permute-start(bf16[80,512]{1,0:T(8,128)(2,1)S(1)} %get-tuple-element.41), channel_id=1, source_target_pairs={{0,8},{8,0},{4,12},{12,4},{16,24},{24,16},{20,28},{28,20},{32,40},... | collective-permute-start | bytes 245768 | tf_op jit(solution)/shard_map/ppermute | solution.py:33
  43.9 18.7 %copy-start.8 = (s32[16]{0:T(128)S(1)}, s32[16]{0:T(128)}, u32[]{:S(2)}) copy-start(s32[16]{0:T(128)} %param.27) | copy-start | bytes 196
  46.4 16.2 %collective-permute-start.5 = (bf16[80,512]{1,0:T(8,128)(2,1)S(1)}, bf16[80,512]{1,0:T(8,128)(2,1)S(1)}, u32[]{:S(2)}, u32[]{:S(2)}) collective-permute-start(bf16[80,512]{1,0:T(8,128)(2,1)S(1)} %get-tuple-element.45), channel_id=1, source_target_pairs={{8,16},{16,8},{12,20},{20,12},{24,32},{32,24},{28,36},{36,28},{40,... | collective-permute-start | bytes 245768 | tf_op jit(solution)/shard_map/ppermute | solution.py:33
  48.3 14.3 %collective-permute-start.6 = (bf16[80,512]{1,0:T(8,128)(2,1)S(1)}, bf16[80,512]{1,0:T(8,128)(2,1)S(1)}, u32[]{:S(2)}, u32[]{:S(2)}) collective-permute-start(bf16[80,512]{1,0:T(8,128)(2,1)S(1)} %get-tuple-element.46), channel_id=1, source_target_pairs={{0,8},{8,0},{4,12},{12,4},{16,24},{24,16},{20,28},{28,20},{32,40},... | collective-permute-start | bytes 245768 | tf_op jit(solution)/shard_map/ppermute | solution.py:33
  62.5 4.3 %copy-start.7 = (s32[128]{0:T(128)S(1)}, s32[128]{0:T(128)}, u32[]{:S(2)}) copy-start(s32[128]{0:T(128)} %param.26) | copy-start | bytes 1540
  62.6 7.4 %copy-start.6 = (bf16[64,64]{1,0:T(8,128)(2,1)S(1)}, bf16[64,64]{1,0:T(8,128)(2,1)}, u32[]{:S(2)}) copy-start(bf16[64,64]{1,0:T(8,128)(2,1)} %inverse.1) | copy-start | bytes 24580
  64.3 5.6 %collective-permute-start.7 = (bf16[16,512]{1,0:T(8,128)(2,1)S(1)}, bf16[16,512]{1,0:T(8,128)(2,1)S(1)}, u32[]{:S(2)}, u32[]{:S(2)}) collective-permute-start(bf16[16,512]{1,0:T(8,128)(2,1)S(1)} %get-tuple-element.51), channel_id=1, source_target_pairs={{0,1},{1,0},{2,3},{3,2},{4,5},{5,4},{6,7},{7,6},{8,9},{9,8},{10,11... | collective-permute-start | bytes 49160 | tf_op jit(solution)/shard_map/ppermute | solution.py:33

commit v5 on v4

v5 whole, which is shorter than its diff:
```python
import jax
import jax.numpy as jnp
from jax import lax
from jax.experimental import pallas as pl
from jax.experimental.pallas import tpu as pltpu
from jax.sharding import PartitionSpec as P

SWEEPS = 2
DOF = 64
RHS = 8
E = 128
CHIP = 2 * E
FACES = 6
ROWS = DOF * RHS
NEAR = 32
FAR = 8
SUB = 8
PAIRS = 16
CROSS = NEAR + 2 * FAR
SIDE = 4 * 2 * SUB
HALO = 2 * CROSS + SIDE
INTS = 32
BF = jnp.bfloat16
F32 = jnp.float32


def swap(array, axis, pairs):
    count = lax.axis_size(axis)
    route = []
    for low, high in pairs:
        if high < count:
            route += [(low, high), (high, low)]
    return lax.ppermute(array, axis, route)


def spec():
    return pl.BlockSpec(memory_space=pltpu.VMEM)


def call(kernel, outs, *args, flops=0, scalars=0, remote=0, scratch=(), vmem=16):
    specs = [pl.BlockSpec(memory_space=pltpu.SMEM)] * scalars
    specs += [pl.BlockSpec(memory_space=pl.ANY)] * remote
    specs += [spec()] * (len(args) - scalars - remote)
    moved = sum(a.size * a.dtype.itemsize for a in args)
    return pl.pallas_call(
        kernel,
        out_shape=[jax.ShapeDtypeStruct(s, d) for s, d in outs],
        in_specs=specs,
        out_specs=[spec()] * len(outs),
        scratch_shapes=scratch,
        cost_estimate=pl.CostEstimate(flops=flops, bytes_accessed=moved, transcendentals=0),
        compiler_params=pltpu.CompilerParams(vmem_limit_bytes=vmem << 20),
    )(*args)


def iota(shape, dim):
    return lax.broadcasted_iota(jnp.int32, shape, dim)


def column(row):
    count = row.shape[1]
    wide = jnp.broadcast_to(row.astype(F32), (count, count))
    kept = jnp.where(iota((count, count), 0) == iota((count, count), 1), wide, 0.0)
    return jnp.sum(kept, axis=1, keepdims=True).astype(jnp.int32)


def picker(row, width):
    count = row.shape[1]
    return jnp.where(iota((count, width), 1) == column(row), 1.0, 0.0).astype(BF)


def send(choice, field, refs):
    rows = lax.dot_general(choice, field, (((1,), (1,)), ((), ())), preferred_element_type=F32).astype(BF)
    start = 0
    for ref, used in refs:
        ref[:used] = rows[start : start + used]
        if ref.shape[0] > used:
            ref[used:] = jnp.zeros((ref.shape[0] - used, ROWS), BF)
        start += used


def first_kernel(*refs):
    sources, message, targets, ints, arrived = refs[:10], refs[10], refs[11:21], refs[21], refs[22]
    copies = [pltpu.make_async_copy(a, b, arrived.at[i]) for i, (a, b) in enumerate(zip(sources, targets))]
    for copy in copies:
        copy.start()
    near, far, sub, elem_type, face_type, neighbours, pair, partner, guess, rhs = targets
    for copy in copies[:8]:
        copy.wait()
    ints[...] = jnp.zeros((INTS, E), F32)
    ints[0:6, :] = neighbours[...].astype(F32)
    ints[8:14, :] = face_type[...].astype(F32)
    ints[14:15, :] = elem_type[...].astype(F32)
    ints[16:18, :NEAR] = near[...].astype(F32)
    ints[18:20, :FAR] = far[...].astype(F32)
    ints[20:21, :SUB] = sub[...].astype(F32)
    ints[21:22, :PAIRS] = pair[...].astype(F32)
    ints[22:23, :] = partner[...].astype(F32)
    message[2 * ROWS :, :] = ints[...].astype(BF)
    for i, field in enumerate((guess, rhs)):
        copies[8 + i].wait()
        blocks = [field[pl.ds(r, DOF, stride=RHS), :].astype(BF) for r in range(RHS)]
        message[i * ROWS : (i + 1) * ROWS, :] = jnp.concatenate(blocks, axis=0)


def tables(lists, core, odd, local_ref, halo_ref, mask_ref):
    below = jnp.where(odd, 0, CROSS)
    above = jnp.where(odd, CROSS, 0)
    first = core == 0
    slots = []
    for d in range(FACES):
        k = lists[d : d + 1, :]
        m = k - 208
        place = 2 * CROSS + (m >> 3) * 2 * SUB + core * SUB + (m & 7)
        place = jnp.where(k < 208, above + NEAR + core * FAR + k - 200, place)
        place = jnp.where(k < 200, below + NEAR + core * FAR + k - 192, place)
        place = jnp.where(k < 192, jnp.where(first, -1, above + k - 160), place)
        place = jnp.where(k < 160, jnp.where(first, below + k - 128, -1), place)
        place = jnp.where(k < E, -1, place)
        lanes = slice(d * E, (d + 1) * E)
        local_ref[:, lanes] = jnp.where(iota((E, E), 0) == k, 1.0, 0.0).astype(BF)
        halo_ref[:, lanes] = jnp.where(iota((HALO, E), 0) == place, 1.0, 0.0).astype(BF)
        start = jnp.where(first, 160, 128)
        slots.append(jnp.where(iota((NEAR, E), 0) + start == k, 1.0, 0.0).astype(BF))
    for d in range(FACES + 1):
        kinds = lists[14:15, :] if d == 0 else lists[7 + d : 8 + d, :]
        for t in range(2):
            mask_ref[2 * d + t] = jnp.where(jnp.broadcast_to(kinds, (16, E)) == t, 1.0, 0.0).astype(BF)
    return jnp.concatenate(slots, axis=1)


def own_kernel(place_ref, mine, diag, face, smooth, field_ref, ints_ref, slot_ref, local_ref, halo_ref, mask_ref, wide_ref, smooth_ref):
    lists = mine[2 * ROWS :, :].astype(F32).astype(jnp.int32)
    ints_ref[...] = lists
    slot_ref[...] = tables(lists, place_ref[0], place_ref[1] == 1, local_ref, halo_ref, mask_ref)
    field_ref[...] = mine[:ROWS, :]
    for d in range(FACES + 1):
        both = (diag[0], diag[1]) if d == 0 else (face[d - 1, 0], face[d - 1, 1])
        wide_ref[:, d * 2 * DOF : (d + 1) * 2 * DOF] = jnp.concatenate(both, axis=1)
    smooth_ref[...] = jnp.concatenate([smooth[0], smooth[1]], axis=1)


def pack_kernel(place_ref, own_field, own_lists, own_slots, other, field_ref, choice_ref, inner_ref, outer_ref, local_ref, halo_ref, mask_ref, *messages):
    core = place_ref[0]
    first = core == 0
    odd = place_ref[1] == 1
    mine = own_lists[...]
    theirs = other[2 * ROWS :, :].astype(F32).astype(jnp.int32)
    low = jnp.where(first, mine, theirs)
    high = jnp.where(first, theirs, mine)
    low_at, high_at = core * E, (1 - core) * E
    field = jnp.concatenate([own_field[...], other[:ROWS, :]], axis=1)

    def chosen(near, one, two):
        return picker(near, CHIP), jnp.concatenate([picker(one + low_at, CHIP), picker(two + high_at, CHIP)], axis=0)

    up = (high[17:18, :NEAR] + high_at, low[19:20, :FAR], high[19:20, :FAR])
    down = (low[16:17, :NEAR] + low_at, low[18:19, :FAR], high[18:19, :FAR])
    to_one = [jnp.where(odd, d, u) for u, d in zip(up, down)]
    to_two = [jnp.where(odd, u, d) for u, d in zip(up, down)]
    side = jnp.concatenate([picker(low[20:21, :SUB] + low_at, CHIP), picker(high[20:21, :SUB] + high_at, CHIP)], axis=0)
    choice = jnp.concatenate([*chosen(*to_one), *chosen(*to_two), side, side, side, side], axis=0)
    send(choice, field, zip(messages, (CROSS, CROSS, SIDE)))
    choice_ref[...] = choice
    field_ref[...] = field
    their_slots = tables(theirs, 1 - core, odd, local_ref, halo_ref, mask_ref)
    listed = jnp.where(first, theirs[16:17, :NEAR], theirs[17:18, :NEAR])
    inner = jnp.where(iota((E, NEAR), 0) == listed, 1.0, 0.0).astype(BF)
    inner_ref[...] = jnp.dot(inner, own_slots[...], preferred_element_type=F32).astype(BF)
    listed = jnp.where(first, mine[17:18, :NEAR], mine[16:17, :NEAR])
    outer = jnp.where(iota((E, NEAR), 0) == listed, 1.0, 0.0).astype(BF)
    outer_ref[...] = jnp.dot(outer, their_slots, preferred_element_type=F32).astype(BF)


def masked(block, mask):
    return block * jnp.concatenate([mask] * (DOF // 16), axis=0)


def extend(field_ref, halo):
    near = jnp.concatenate([ref[:used] for ref, used in zip(halo, (CROSS, CROSS, SIDE))], axis=0)
    return jnp.concatenate([field_ref[...], near.T], axis=1)


def select(extended, *blocks):
    columns = jnp.concatenate([block[...] for block in blocks], axis=0)
    return jnp.dot(extended, columns, preferred_element_type=F32).astype(BF)


def sweep_kernel(field_ref, two, one, side, *refs):
    own_local, own_halo, own_masks, inner, outer, local, halo, masks, wide, smooth, rhs, other, choice, *refs = refs
    before, (after, next_field, *messages) = refs[:-5], refs[-5:]
    extended = extend(field_ref, (one, two, side))
    mine = select(extended, own_local, inner, own_halo)
    theirs = select(extended, outer, local, halo)
    kinds = [jnp.concatenate([own_masks[i], masks[i]], axis=1) for i in range(2 * FACES + 2)]
    parts = []
    for r in range(RHS):
        rows = slice(r * DOF, (r + 1) * DOF)
        stack = []
        for d in range(FACES + 1):
            lanes = slice((d - 1) * E, d * E)
            block = field_ref[rows, :] if d == 0 else jnp.concatenate([mine[rows, lanes], theirs[rows, lanes]], axis=1)
            stack += [masked(block, kinds[2 * d]), masked(block, kinds[2 * d + 1])]
        product = jnp.dot(wide[...], jnp.concatenate(stack, axis=0), preferred_element_type=F32)
        given = other[ROWS + r * DOF : ROWS + (r + 1) * DOF, :].astype(F32)
        given = jnp.concatenate([rhs[pl.ds(r, DOF, stride=RHS), :], given], axis=1)
        rounded = (given - product).astype(BF)
        parts.append(jnp.concatenate([masked(rounded, kinds[0]), masked(rounded, kinds[1])], axis=0))
    changes = jnp.concatenate([jnp.dot(smooth[...], part, preferred_element_type=F32) for part in parts], axis=0)
    if len(before) == 1 and before[0].shape[1] == CHIP:
        old = before[0][...]
    else:
        own = jnp.concatenate([before[0][pl.ds(r, DOF, stride=RHS), :] for r in range(RHS)], axis=0)
        old = jnp.concatenate([own, other[:ROWS, :].astype(F32)], axis=1)
    new = old + changes
    rounded = new.astype(BF)
    send(choice[...], rounded, zip(messages, (CROSS, CROSS, SIDE)))
    after[...] = new
    next_field[...] = rounded


def residual_kernel(field_ref, two, one, side, own_local, inner, own_halo, masks, wide, rhs, lists, residual_ref, rounded_ref, message):
    beside = select(extend(field_ref, (one, two, side)), own_local, inner, own_halo)
    parts = []
    for r in range(0, RHS, 2):
        halves = []
        for s in (r, r + 1):
            rows = slice(s * DOF, (s + 1) * DOF)
            stack = []
            for d in range(FACES + 1):
                block = field_ref[rows, :E] if d == 0 else beside[rows, (d - 1) * E : d * E]
                stack += [masked(block, masks[2 * d]), masked(block, masks[2 * d + 1])]
            halves.append(jnp.concatenate(stack, axis=0))
        product = jnp.dot(wide[...], jnp.concatenate(halves, axis=1), preferred_element_type=F32)
        parts += [rhs[pl.ds(r + i, DOF, stride=RHS), :] - product[:, i * E : (i + 1) * E] for i in range(2)]
    residual = jnp.concatenate(parts, axis=0)
    rounded = residual.astype(BF)
    send(picker(lists[21:22, :PAIRS], E), rounded, [(message, PAIRS)])
    residual_ref[...] = residual
    rounded_ref[...] = rounded


def mate_picker(partner, first, count):
    return jnp.where(iota((count, E), 0) + first == partner, 1.0, 0.0).astype(BF)


def local_kernel(residual_ref, rounded_ref, lists, out_ref, half_ref):
    residual = residual_ref[...]
    rounded = rounded_ref[...]
    rest = (residual - rounded.astype(F32)).astype(BF)
    local = mate_picker(lists[22:23, :], 0, E)
    mates = jnp.dot(rounded, local, preferred_element_type=F32)
    mates = mates + jnp.dot(rest, local, preferred_element_type=F32)
    for r in range(RHS):
        out_ref[pl.ds(r, DOF, stride=RHS), :] = residual[r * DOF : (r + 1) * DOF, :]
    half_ref[...] = residual + mates


def coarse_kernel(half_ref, incoming, lists, inverse, iterate, solution_ref):
    mates = lax.dot_general(
        incoming[...], mate_picker(lists[22:23, :], E, PAIRS), (((0,), (0,)), ((), ())), preferred_element_type=F32
    )
    coarse = (half_ref[...] + mates).astype(BF)
    solved = []
    for r in range(0, RHS, 2):
        pair = jnp.concatenate([coarse[s * DOF : (s + 1) * DOF, :] for s in (r, r + 1)], axis=1)
        update = jnp.dot(inverse[...], pair, preferred_element_type=F32)
        solved += [iterate[(r + i) * DOF : (r + i + 1) * DOF, :E] + update[:, i * E : (i + 1) * E] for i in range(2)]
    for r in range(RHS):
        solution_ref[pl.ds(r, DOF, stride=RHS), :] = solved[r]


def body(
    rhs,
    guess,
    diag_blocks,
    face_blocks,
    smoother,
    coarse_inverse,
    elem_type,
    face_type,
    neighbours,
    send_near,
    send_far,
    sub_send,
    partner,
    pair_send,
):
    a = lax.axis_index("dom")
    place = jnp.stack([a % 2, (a // 2) % 2]).astype(jnp.int32)
    doms = lax.axis_size("dom")
    rhs = rhs.reshape(ROWS, E)
    guess = guess.reshape(ROWS, E)
    inside = [(i, i + 1) for i in range(0, doms, 2)]
    cross_one = [(i + j, i + j + 2) for i in range(0, doms, 4) for j in range(2)]
    cross_two = [(i + j + 2, i + j + 4) for i in range(0, doms, 4) for j in range(2)]

    def exchange(messages):
        one, two, side = messages
        two = swap(two, "dom", cross_two)
        one = swap(one, "dom", cross_one)
        side = lax.all_to_all(side, "sub", 0, 0, tiled=True)
        return two, one, side

    message_outs = [((n, ROWS), BF) for n in SENT]
    taken = (send_near, send_far, sub_send.reshape(1, -1), elem_type.reshape(1, -1), face_type, neighbours)
    taken += (pair_send.reshape(1, -1), partner.reshape(1, -1), guess, rhs)
    (mine,) = call(
        first_kernel,
        [((2 * ROWS + INTS, E), BF)],
        *taken,
        remote=len(taken),
        scratch=[pltpu.VMEM(x.shape, x.dtype) for x in taken]
        + [pltpu.VMEM((INTS, E), F32), pltpu.SemaphoreType.DMA((len(taken),))],
        vmem=60,
    )
    other = swap(mine, "dom", inside)
    table_outs = [((E, FACES * E), BF), ((HALO, FACES * E), BF), ((2 * FACES + 2, 16, E), BF)]
    own_field, own_lists, own_slots, own_local, own_halo, own_masks, wide, smooth = call(
        own_kernel,
        [((ROWS, E), BF), ((INTS, E), jnp.int32), ((NEAR, FACES * E), BF)]
        + table_outs
        + [((DOF, 2 * DOF * (FACES + 1)), BF), ((DOF, 2 * DOF), BF)],
        place,
        mine,
        diag_blocks,
        face_blocks,
        smoother,
        flops=1000000,
        scalars=1,
    )
    field, choice, inner, outer, local, halo, masks, *messages = call(
        pack_kernel,
        [((ROWS, CHIP), BF), ((HALO, CHIP), BF), ((E, FACES * E), BF), ((E, FACES * E), BF)] + table_outs + message_outs,
        place,
        own_field,
        own_lists,
        own_slots,
        other,
        flops=2 * HALO * CHIP * ROWS,
        scalars=1,
    )
    brought = exchange(messages)
    work = 2 * ROWS * (CHIP + HALO) * FACES * CHIP + 2 * DOF * 14 * DOF * RHS * CHIP
    iterate = guess
    for _ in range(SWEEPS):
        iterate, field, *messages = call(
            sweep_kernel,
            [((ROWS, CHIP), F32), ((ROWS, CHIP), BF)] + message_outs,
            field,
            *brought,
            own_local,
            own_halo,
            own_masks,
            inner,
            outer,
            local,
            halo,
            masks,
            wide,
            smooth,
            rhs,
            other,
            choice,
            iterate,
            flops=work,
        )
        brought = exchange(messages)
    residual, rounded, message = call(
        residual_kernel,
        [((ROWS, E), F32), ((ROWS, E), BF), ((PAIRS, ROWS), BF)],
        field,
        *brought,
        own_local,
        inner,
        own_halo,
        own_masks,
        wide,
        rhs,
        own_lists,
        flops=work // 2,
    )
    subs = lax.axis_size("sub")
    incoming = swap(message, "sub", [(i, i + 1) for i in range(0, subs, 2)])
    residual, coarse = call(
        local_kernel,
        [((ROWS, E), F32), ((ROWS, E), F32)],
        residual,
        rounded,
        own_lists,
        flops=work // 8,
    )
    (solved,) = call(
        coarse_kernel,
        [((ROWS, E), F32)],
        coarse,
        incoming,
        own_lists,
        coarse_inverse,
        iterate,
        flops=work // 8,
    )
    shape = (DOF, RHS, E)
    return (solved.reshape(shape), residual.reshape(shape))


SENT = (SIDE + 16, SIDE + 16, SIDE)


def solution(mesh):
    block = P(None, None, ("dom", "sub"))
    flat = P(("dom", "sub"))
    listed = P(None, ("dom", "sub"))
    in_specs = (block, block, P(), P(), P(), P(), flat, listed, listed, listed, listed, flat, flat, flat)
    return jax.shard_map(body, mesh=mesh, in_specs=in_specs, out_specs=(block, block), check_vma=False)
```

time: 72.1 us -> 68.6 us (0.951)
  blocking collectives: 16 us -> 25.7 us
  waiting for transfers between devices: 8.48 us -> 2.31 us
  starting transfers between devices: 31.1 us -> 26.8 us
  Pallas kernels: 14.1 us -> 10.7 us
    all_to_all x2 -> x3, blocking collectives: 16 us -> 25.7 us  [exchange(): side = lax.all_to_all(side, 'sub', 0, 0, tiled=True)]
    all_to_all x1 -> x0, waiting for transfers between devices: 4.55 us -> none  [exchange(): side = lax.all_to_all(side, 'sub', 0, 0, tiled=True)]
    all_to_all x1 -> x0, starting transfers between devices: 4.3 us -> none  [exchange(): side = lax.all_to_all(side, 'sub', 0, 0, tiled=True)]
    pallas_call x8, Pallas kernels: 14.1 us -> 10.7 us  [call(): pl.pallas_call(kernel, out_shape=[jax.ShapeDtypeStruct(s, d) for s, d in...]
    ppermute x8, waiting for transfers between devices: 3.93 us -> 2.31 us  [swap(): return lax.ppermute(array, axis, route)]
    unnamed x18 -> x14, local copies, waits for them, and re-layouts: 0.99 us -> 1.63 us
  transfers between devices with their start and end apart: 9 -> 8, of which waited for: 3 -> 1; matrix products, arithmetic and copies ran while one was open for 0% -> 0% of each run, Pallas kernels for 3% -> 2%
where the time goes in v5:
time: 68.6 us; the launch traced here: 68.1 us
  starting transfers between devices  26.8 us (39%)
  blocking collectives  25.7 us (37%)
  Pallas kernels  10.7 us (16%)
  waiting for transfers between devices  2.31 us (3%)
  local copies, waits for them, and re-layouts  1.63 us (2%)
  between operations  0.85 us (1%)
    ppermute x8, starting transfers between devices, swap(): return lax.ppermute(array, axis, route)  26.8 us
    all_to_all x3, blocking collectives, exchange(): side = lax.all_to_all(side, 'sub', 0, 0, tiled=True)  25.7 us
    pallas_call x8, Pallas kernels, call(): pl.pallas_call(kernel, out_shape=[jax.ShapeDtypeStruct(s, d) for s, d in...  10.7 us
    ppermute x8, waiting for transfers between devices, swap(): return lax.ppermute(array, axis, route)  2.31 us
    unnamed x14, local copies, waits for them, and re-layouts  1.63 us
  transfers between devices with their start and end apart: 8, of which 1 were waited for; matrix products, arithmetic and copies ran while one was open for 0% of the time, Pallas kernels for 2%

profile of v5, /device:TPU:240, one launch (start us, length us, event | category | flops | bytes accessed | tf_op | source)
XLA Modules:
  0.0 68.1 jit_solution(12307054430701794735)
XLA Ops:
  0.6 0.0 copy-start.3
  0.6 2.0 %shard_map.149.mine = bf16[1056,128]{1,0:T(8,128)(2,1)} custom-call(s32[2,32]{1,0:T(2,128)} %refs_0_.1, s32[2,8]{1,0:T(2,128)} %refs_1_.1, s32[1,8]{1,0:T(1,128)} %bitcast.29, s32[1,128]{1,0:T(1,128)} %bitcast.30, s32[6,128]{1,0:T(8,128)} %refs_4_.1, s32[6,128]{1,0:T(8,128)} %refs_5_.1, s32[1,16]{1,0:T(1,128)} %bitcast.31, s32[1,128]{1,0:T(1,128)} %bitcast.32, ...), custom_call_target="tpu_custom_call" | custom-call | bytes 531872 | tf_op jit(solution)/shard_map/pallas_call | solution.py:45
  2.7 1.9 %collective-permute-start = (bf16[1056,128]{1,0:T(8,128)(2,1)}, bf16[1056,128]{1,0:T(8,128)(2,1)S(1)}, u32[]{:S(2)}, u32[]{:S(2)}) collective-permute-start(bf16[1056,128]{1,0:T(8,128)(2,1)} %shard_map.149.mine), channel_id=1, source_target_pairs={{0,4},{4,0},{8,12},{12,8},{16,20},{20,16},{24,28},{28,24},{32,36},... | collective-permute-start | bytes 811016 | tf_op jit(solution)/shard_map/ppermute | solution.py:33
  4.6 0.0 copy-start.5
  4.6 0.0 copy-start.4
  4.7 0.1 pad_add_fusion.place_ref
  4.7 0.0 copy-done.3
  4.7 0.6 copy-done.5
  5.4 0.0 copy-done.4
  5.4 0.0 copy-start
  5.4 1.0 %copy-done = bf16[1056,128]{1,0:T(8,128)(2,1)S(1)} copy-done((bf16[1056,128]{1,0:T(8,128)(2,1)S(1)}, bf16[1056,128]{1,0:T(8,128)(2,1)}, u32[]{:S(2)}) %copy-start) | copy-done | bytes 270360
  6.3 0.7 %shard_map.150 = (bf16[512,128]{1,0:T(8,128)(2,1)S(1)}, s32[32,128]{1,0:T(8,128)S(1)}, bf16[32,768]{1,0:T(8,128)(2,1)S(1)}, bf16[128,768]{1,0:T(8,128)(2,1)S(1)}...) custom-call(s32[2]{0:T(128)S(1)} %pad_add_fusion.place_ref, ...), custom_call_target="tpu_custom_call" | custom-call | flops 1000000 | bytes 401416 | tf_op jit(solution)/shard_map/pallas_call | solution.py:45
  7.1 0.0 collective-permute-done.other.refs_11_
  7.1 0.0 copy-start.1
  7.1 0.0 copy-start.2
  7.1 1.0 %shard_map.151 = (bf16[512,256]{1,0:T(8,128)(2,1)S(1)}, bf16[160,256]{1,0:T(8,128)(2,1)S(1)}, bf16[128,768]{1,0:T(8,128)(2,1)S(1)}, bf16[128,768]{1,0:T(8,128)(2...) custom-call(s32[2]{0:T(128)S(1)} %pad_add_fusion.place_ref, ...), custom_call_target="tpu_custom_call" | custom-call | flops 41943040 | bytes 466952 | tf_op jit(solution)/shard_map/pallas_call | solution.py:45
  8.1 3.3 %collective-permute-start.1 = (bf16[80,512]{1,0:T(8,128)(2,1)S(1)}, bf16[80,512]{1,0:T(8,128)(2,1)S(1)}, u32[]{:S(2)}, u32[]{:S(2)}) collective-permute-start(bf16[80,512]{1,0:T(8,128)(2,1)S(1)} %get-tuple-element.39), channel_id=1, source_target_pairs={{8,16},{16,8},{12,20},{20,12},{24,32},{32,24},{28,36},{36,28},{40,... | collective-permute-start | bytes 245768 | tf_op jit(solution)/shard_map/ppermute | solution.py:33
  11.3 4.0 %collective-permute-start.2 = (bf16[80,512]{1,0:T(8,128)(2,1)S(1)}, bf16[80,512]{1,0:T(8,128)(2,1)S(1)}, u32[]{:S(2)}, u32[]{:S(2)}) collective-permute-start(bf16[80,512]{1,0:T(8,128)(2,1)S(1)} %get-tuple-element.40), channel_id=1, source_target_pairs={{0,8},{8,0},{4,12},{12,4},{16,24},{24,16},{20,28},{28,20},{32,40},... | collective-permute-start | bytes 245768 | tf_op jit(solution)/shard_map/ppermute | solution.py:33
  15.4 9.7 %all_to_all.33 = bf16[4,16,512]{2,1,0:T(8,128)(2,1)S(1)} all-to-all(bf16[4,16,512]{2,1,0:T(8,128)(2,1)S(1)} %bitcast.24), channel_id=1, replica_groups=mesh['dom'=128,'sub'=4] {'sub'}, dimensions={0} | all-to-all | bytes 131072 | tf_op jit(solution)/shard_map/all_to_all | solution.py:302
  25.1 0.0 collective-permute-done.1.two
  25.1 0.0 collective-permute-done.2.one
  25.1 0.0 copy-done.1
  25.1 0.0 copy-done.2
  25.1 1.9 %shard_map.152 = (f32[512,256]{1,0:T(8,128)S(1)}, bf16[512,256]{1,0:T(8,128)(2,1)S(1)}, bf16[80,512]{1,0:T(8,128)(2,1)S(1)}, bf16[80,512]{1,0:T(8,128)(2,1)S(1)}, bf16[64,512]{1,0:T(8,128)(2,1)S(1)}) custom-call(bf16[512,256]{1,0:T(8,128)(2,1)S(1)} %get-tuple-element.38.field_ref, bf16[80,512]{1,0:T(8,128)(2,1)S(1)} %collective-permute-done.1.two, ...), custom_call_target="tpu_custom_call" | custom-call | flops 889192448 | bytes 2891776 | tf_op jit(solution)/shard_map/pallas_call | solution.py:45
  27.1 1.9 %collective-permute-start.3 = (bf16[80,512]{1,0:T(8,128)(2,1)S(1)}, bf16[80,512]{1,0:T(8,128)(2,1)S(1)}, u32[]{:S(2)}, u32[]{:S(2)}) collective-permute-start(bf16[80,512]{1,0:T(8,128)(2,1)S(1)} %get-tuple-element.54), channel_id=1, source_target_pairs={{8,16},{16,8},{12,20},{20,12},{24,32},{32,24},{28,36},{36,28},{40,... | collective-permute-start | bytes 245768 | tf_op jit(solution)/shard_map/ppermute | solution.py:33
  29.0 5.0 %collective-permute-start.4 = (bf16[80,512]{1,0:T(8,128)(2,1)S(1)}, bf16[80,512]{1,0:T(8,128)(2,1)S(1)}, u32[]{:S(2)}, u32[]{:S(2)}) collective-permute-start(bf16[80,512]{1,0:T(8,128)(2,1)S(1)} %get-tuple-element.55), channel_id=1, source_target_pairs={{0,8},{8,0},{4,12},{12,4},{16,24},{24,16},{20,28},{28,20},{32,40},... | collective-permute-start | bytes 245768 | tf_op jit(solution)/shard_map/ppermute | solution.py:33
  34.0 8.0 %all_to_all.34 = bf16[4,16,512]{2,1,0:T(8,128)(2,1)S(1)} all-to-all(bf16[4,16,512]{2,1,0:T(8,128)(2,1)S(1)} %bitcast.27), channel_id=1, replica_groups=mesh['dom'=128,'sub'=4] {'sub'}, dimensions={0} | all-to-all | bytes 131072 | tf_op jit(solution)/shard_map/all_to_all | solution.py:302
  42.0 0.0 collective-permute-done.3.two
  42.0 0.0 collective-permute-done.4.one
  42.0 1.9 %shard_map.153 = (f32[512,256]{1,0:T(8,128)S(1)}, bf16[512,256]{1,0:T(8,128)(2,1)S(1)}, bf16[80,512]{1,0:T(8,128)(2,1)S(1)}, bf16[80,512]{1,0:T(8,128)(2,1)S(1)}, bf16[64,512]{1,0:T(8,128)(2,1)S(1)}) custom-call(bf16[512,256]{1,0:T(8,128)(2,1)S(1)} %get-tuple-element.53.field_ref, bf16[80,512]{1,0:T(8,128)(2,1)S(1)} %collective-permute-done.3.two, ...), custom_call_target="tpu_custom_call" | custom-call | flops 889192448 | bytes 3153920 | tf_op jit(solution)/shard_map/pallas_call | solution.py:45
  44.0 1.9 %collective-permute-start.5 = (bf16[80,512]{1,0:T(8,128)(2,1)S(1)}, bf16[80,512]{1,0:T(8,128)(2,1)S(1)}, u32[]{:S(2)}, u32[]{:S(2)}) collective-permute-start(bf16[80,512]{1,0:T(8,128)(2,1)S(1)} %get-tuple-element.59), channel_id=1, source_target_pairs={{8,16},{16,8},{12,20},{20,12},{24,32},{32,24},{28,36},{36,28},{40,... | collective-permute-start | bytes 245768 | tf_op jit(solution)/shard_map/ppermute | solution.py:33
  45.9 6.3 %collective-permute-start.6 = (bf16[80,512]{1,0:T(8,128)(2,1)S(1)}, bf16[80,512]{1,0:T(8,128)(2,1)S(1)}, u32[]{:S(2)}, u32[]{:S(2)}) collective-permute-start(bf16[80,512]{1,0:T(8,128)(2,1)S(1)} %get-tuple-element.60), channel_id=1, source_target_pairs={{0,8},{8,0},{4,12},{12,4},{16,24},{24,16},{20,28},{28,20},{32,40},... | collective-permute-start | bytes 245768 | tf_op jit(solution)/shard_map/ppermute | solution.py:33
  52.2 8.0 %all_to_all.35 = bf16[4,16,512]{2,1,0:T(8,128)(2,1)S(1)} all-to-all(bf16[4,16,512]{2,1,0:T(8,128)(2,1)S(1)} %bitcast.23), channel_id=1, replica_groups=mesh['dom'=128,'sub'=4] {'sub'}, dimensions={0} | all-to-all | bytes 131072 | tf_op jit(solution)/shard_map/all_to_all | solution.py:302
  60.2 0.0 collective-permute-done.5.two
  60.2 0.0 collective-permute-done.6.one
  60.2 1.2 %shard_map.154 = (f32[512,128]{1,0:T(8,128)S(1)}, bf16[512,128]{1,0:T(8,128)(2,1)S(1)}, bf16[16,512]{1,0:T(8,128)(2,1)S(1)}) custom-call(bf16[512,256]{1,0:T(8,128)(2,1)S(1)} %get-tuple-element.58.field_ref, bf16[80,512]{1,0:T(8,128)(2,1)S(1)} %collective-permute-done.5.two, bf16[80,512]{1,0:T(8,128)(2,1)S(1)} %collective-permute-done.6.one, ...), custom_call_target="tpu_custom_call" | custom-call | flops 444596224 | bytes 1581056 | tf_op jit(solution)/shard_map/pallas_call | solution.py:45
  61.3 2.5 %collective-permute-start.7 = (bf16[16,512]{1,0:T(8,128)(2,1)S(1)}, bf16[16,512]{1,0:T(8,128)(2,1)S(1)}, u32[]{:S(2)}, u32[]{:S(2)}) collective-permute-start(bf16[16,512]{1,0:T(8,128)(2,1)S(1)} %get-tuple-element.65), channel_id=1, source_target_pairs={{0,1},{1,0},{2,3},{3,2},{4,5},{5,4},{6,7},{7,6},{8,9},{9,8},{10,11... | collective-permute-start | bytes 49160 | tf_op jit(solution)/shard_map/ppermute | solution.py:33
  63.8 0.0 copy-start.6
  63.8 0.8 %shard_map.155 = (f32[512,128]{1,0:T(8,128)}, f32[512,128]{1,0:T(8,128)S(1)}) custom-call(f32[512,128]{1,0:T(8,128)S(1)} %get-tuple-element.62.residual_ref, bf16[512,128]{1,0:T(8,128)(2,1)S(1)} %get-tuple-element.63.rounded_ref, s32[32,128]{1,0:T(8,128)S(1)} %get-tuple-element.36.own_lists.lists), custom_call_target="tpu_custom_call" | custom-call | flops 111149056 | bytes 409600 | tf_op jit(solution)/shard_map/pallas_call | solution.py:45
  64.7 2.3 %collective-permute-done.7.incoming = bf16[16,512]{1,0:T(8,128)(2,1)S(1)} collective-permute-done((bf16[16,512]{1,0:T(8,128)(2,1)S(1)}, bf16[16,512]{1,0:T(8,128)(2,1)S(1)}, u32[]{:S(2)}, u32[]{:S(2)}) %collective-permute-start.7) | collective-permute-done | bytes 16416 | tf_op jit(solution)/shard_map/ppermute | solution.py:33
  67.0 0.0 copy-done.6
  67.0 1.1 %shard_map.156 = f32[512,128]{1,0:T(8,128)} custom-call(f32[512,128]{1,0:T(8,128)S(1)} %get-tuple-element.64.half_ref, bf16[16,512]{1,0:T(8,128)(2,1)S(1)} %collective-permute-done.7.incoming, s32[32,128]{1,0:T(8,128)S(1)} %get-tuple-element.36.own_lists.lists, bf16[64,64]{1,0:T(8,128)(2,1)S(1)} %copy-done.6, f32[512,256]{1,0:T(8,128)S(1)} %get-tuple-element.66.iterate), custom_call_target="tpu_custom_call" | custom-call | flops 111149056 | bytes 827392 | tf_op jit(solution)/shard_map/pallas_call | solution.py:45
Async XLA Ops:
  0.6 4.1 %copy-start.3 = (bf16[6,2,64,64]{3,2,1,0:T(8,128)(2,1)S(1)}, bf16[6,2,64,64]{3,2,1,0:T(8,128)(2,1)}, u32[]{:S(2)}) copy-start(bf16[6,2,64,64]{3,2,1,0:T(8,128)(2,1)} %face.1) | copy-start | bytes 294916
  2.7 4.4 %collective-permute-start = (bf16[1056,128]{1,0:T(8,128)(2,1)}, bf16[1056,128]{1,0:T(8,128)(2,1)S(1)}, u32[]{:S(2)}, u32[]{:S(2)}) collective-permute-start(bf16[1056,128]{1,0:T(8,128)(2,1)} %shard_map.149.mine), channel_id=1, source_target_pairs={{0,4},{4,0},{8,12},{12,8},{16,20},{20,16},{24,28},{28,24},{32,36},... | collective-permute-start | bytes 811016 | tf_op jit(solution)/shard_map/ppermute | solution.py:33
  4.6 0.8 %copy-start.5 = (bf16[2,64,64]{2,1,0:T(8,128)(2,1)S(1)}, bf16[2,64,64]{2,1,0:T(8,128)(2,1)}, u32[]{:S(2)}) copy-start(bf16[2,64,64]{2,1,0:T(8,128)(2,1)} %smooth.1) | copy-start | bytes 49156
  4.6 0.8 %copy-start.4 = (bf16[2,64,64]{2,1,0:T(8,128)(2,1)S(1)}, bf16[2,64,64]{2,1,0:T(8,128)(2,1)}, u32[]{:S(2)}) copy-start(bf16[2,64,64]{2,1,0:T(8,128)(2,1)} %diag.1) | copy-start | bytes 49156
  5.4 1.0 %copy-start = (bf16[1056,128]{1,0:T(8,128)(2,1)S(1)}, bf16[1056,128]{1,0:T(8,128)(2,1)}, u32[]{:S(2)}) copy-start(bf16[1056,128]{1,0:T(8,128)(2,1)} %shard_map.149.mine) | copy-start | bytes 811012
  7.1 18.0 %copy-start.1 = (f32[64,8,128]{2,1,0:T(8,128)S(1)}, f32[64,8,128]{2,1,0:T(8,128)}, u32[]{:S(2)}) copy-start(f32[64,8,128]{2,1,0:T(8,128)} %param.15) | copy-start | bytes 786436
  7.1 18.0 %copy-start.2 = (f32[64,8,128]{2,1,0:T(8,128)S(1)}, f32[64,8,128]{2,1,0:T(8,128)}, u32[]{:S(2)}) copy-start(f32[64,8,128]{2,1,0:T(8,128)} %param.14) | copy-start | bytes 786436
  8.1 17.0 %collective-permute-start.1 = (bf16[80,512]{1,0:T(8,128)(2,1)S(1)}, bf16[80,512]{1,0:T(8,128)(2,1)S(1)}, u32[]{:S(2)}, u32[]{:S(2)}) collective-permute-start(bf16[80,512]{1,0:T(8,128)(2,1)S(1)} %get-tuple-element.39), channel_id=1, source_target_pairs={{8,16},{16,8},{12,20},{20,12},{24,32},{32,24},{28,36},{36,28},{40,... | collective-permute-start | bytes 245768 | tf_op jit(solution)/shard_map/ppermute | solution.py:33
  11.3 13.8 %collective-permute-start.2 = (bf16[80,512]{1,0:T(8,128)(2,1)S(1)}, bf16[80,512]{1,0:T(8,128)(2,1)S(1)}, u32[]{:S(2)}, u32[]{:S(2)}) collective-permute-start(bf16[80,512]{1,0:T(8,128)(2,1)S(1)} %get-tuple-element.40), channel_id=1, source_target_pairs={{0,8},{8,0},{4,12},{12,4},{16,24},{24,16},{20,28},{28,20},{32,40},... | collective-permute-start | bytes 245768 | tf_op jit(solution)/shard_map/ppermute | solution.py:33
  27.1 15.0 %collective-permute-start.3 = (bf16[80,512]{1,0:T(8,128)(2,1)S(1)}, bf16[80,512]{1,0:T(8,128)(2,1)S(1)}, u32[]{:S(2)}, u32[]{:S(2)}) collective-permute-start(bf16[80,512]{1,0:T(8,128)(2,1)S(1)} %get-tuple-element.54), channel_id=1, source_target_pairs={{8,16},{16,8},{12,20},{20,12},{24,32},{32,24},{28,36},{36,28},{40,... | collective-permute-start | bytes 245768 | tf_op jit(solution)/shard_map/ppermute | solution.py:33
  29.0 13.0 %collective-permute-start.4 = (bf16[80,512]{1,0:T(8,128)(2,1)S(1)}, bf16[80,512]{1,0:T(8,128)(2,1)S(1)}, u32[]{:S(2)}, u32[]{:S(2)}) collective-permute-start(bf16[80,512]{1,0:T(8,128)(2,1)S(1)} %get-tuple-element.55), channel_id=1, source_target_pairs={{0,8},{8,0},{4,12},{12,4},{16,24},{24,16},{20,28},{28,20},{32,40},... | collective-permute-start | bytes 245768 | tf_op jit(solution)/shard_map/ppermute | solution.py:33
  44.0 16.2 %collective-permute-start.5 = (bf16[80,512]{1,0:T(8,128)(2,1)S(1)}, bf16[80,512]{1,0:T(8,128)(2,1)S(1)}, u32[]{:S(2)}, u32[]{:S(2)}) collective-permute-start(bf16[80,512]{1,0:T(8,128)(2,1)S(1)} %get-tuple-element.59), channel_id=1, source_target_pairs={{8,16},{16,8},{12,20},{20,12},{24,32},{32,24},{28,36},{36,28},{40,... | collective-permute-start | bytes 245768 | tf_op jit(solution)/shard_map/ppermute | solution.py:33
  45.9 14.3 %collective-permute-start.6 = (bf16[80,512]{1,0:T(8,128)(2,1)S(1)}, bf16[80,512]{1,0:T(8,128)(2,1)S(1)}, u32[]{:S(2)}, u32[]{:S(2)}) collective-permute-start(bf16[80,512]{1,0:T(8,128)(2,1)S(1)} %get-tuple-element.60), channel_id=1, source_target_pairs={{0,8},{8,0},{4,12},{12,4},{16,24},{24,16},{20,28},{28,20},{32,40},... | collective-permute-start | bytes 245768 | tf_op jit(solution)/shard_map/ppermute | solution.py:33
  61.3 5.6 %collective-permute-start.7 = (bf16[16,512]{1,0:T(8,128)(2,1)S(1)}, bf16[16,512]{1,0:T(8,128)(2,1)S(1)}, u32[]{:S(2)}, u32[]{:S(2)}) collective-permute-start(bf16[16,512]{1,0:T(8,128)(2,1)S(1)} %get-tuple-element.65), channel_id=1, source_target_pairs={{0,1},{1,0},{2,3},{3,2},{4,5},{5,4},{6,7},{7,6},{8,9},{9,8},{10,11... | collective-permute-start | bytes 49160 | tf_op jit(solution)/shard_map/ppermute | solution.py:33
  63.8 3.2 %copy-start.6 = (bf16[64,64]{1,0:T(8,128)(2,1)S(1)}, bf16[64,64]{1,0:T(8,128)(2,1)}, u32[]{:S(2)}) copy-start(bf16[64,64]{1,0:T(8,128)(2,1)} %inverse.1) | copy-start | bytes 24580

commit v6 on v5

--- a/solution.py
+++ b/solution.py
@@ -19,6 +19,7 @@
 CROSS = NEAR + 2 * FAR
 SIDE = 4 * 2 * SUB
 HALO = 2 * CROSS + SIDE
+WIDE = 2 * DOF * (FACES + 1)
 INTS = 32
 BF = jnp.bfloat16
 F32 = jnp.float32
@@ -80,11 +81,11 @@
 
 
 def first_kernel(*refs):
-    sources, message, targets, ints, arrived = refs[:10], refs[10], refs[11:21], refs[21], refs[22]
+    sources, (message, wide_ref), targets, (ints, arrived) = refs[:13], refs[13:15], refs[15:28], refs[28:]
     copies = [pltpu.make_async_copy(a, b, arrived.at[i]) for i, (a, b) in enumerate(zip(sources, targets))]
     for copy in copies:
         copy.start()
-    near, far, sub, elem_type, face_type, neighbours, pair, partner, guess, rhs = targets
+    near, far, sub, elem_type, face_type, neighbours, pair, partner, guess, rhs, diag, face, smooth = targets
     for copy in copies[:8]:
         copy.wait()
     ints[...] = jnp.zeros((INTS, E), F32)
@@ -101,6 +102,12 @@
         copies[8 + i].wait()
         blocks = [field[pl.ds(r, DOF, stride=RHS), :].astype(BF) for r in range(RHS)]
         message[i * ROWS : (i + 1) * ROWS, :] = jnp.concatenate(blocks, axis=0)
+    for copy in copies[10:]:
+        copy.wait()
+    for d in range(FACES + 1):
+        both = (diag[0], diag[1]) if d == 0 else (face[d - 1, 0], face[d - 1, 1])
+        wide_ref[:, d * 2 * DOF : (d + 1) * 2 * DOF] = jnp.concatenate(both, axis=1)
+    wide_ref[:, WIDE:] = jnp.concatenate([smooth[0], smooth[1]], axis=1)
 
 
 def tables(lists, core, odd, local_ref, halo_ref, mask_ref):
@@ -129,15 +136,11 @@
     return jnp.concatenate(slots, axis=1)
 
 
-def own_kernel(place_ref, mine, diag, face, smooth, field_ref, ints_ref, slot_ref, local_ref, halo_ref, mask_ref, wide_ref, smooth_ref):
+def own_kernel(place_ref, mine, field_ref, ints_ref, slot_ref, local_ref, halo_ref, mask_ref):
     lists = mine[2 * ROWS :, :].astype(F32).astype(jnp.int32)
     ints_ref[...] = lists
     slot_ref[...] = tables(lists, place_ref[0], place_ref[1] == 1, local_ref, halo_ref, mask_ref)
     field_ref[...] = mine[:ROWS, :]
-    for d in range(FACES + 1):
-        both = (diag[0], diag[1]) if d == 0 else (face[d - 1, 0], face[d - 1, 1])
-        wide_ref[:, d * 2 * DOF : (d + 1) * 2 * DOF] = jnp.concatenate(both, axis=1)
-    smooth_ref[...] = jnp.concatenate([smooth[0], smooth[1]], axis=1)
 
 
 def pack_kernel(place_ref, own_field, own_lists, own_slots, other, field_ref, choice_ref, inner_ref, outer_ref, local_ref, halo_ref, mask_ref, *messages):
@@ -187,7 +190,7 @@
 
 
 def sweep_kernel(field_ref, two, one, side, *refs):
-    own_local, own_halo, own_masks, inner, outer, local, halo, masks, wide, smooth, rhs, other, choice, *refs = refs
+    own_local, own_halo, own_masks, inner, outer, local, halo, masks, wide, rhs, other, choice, *refs = refs
     before, (after, next_field, *messages) = refs[:-5], refs[-5:]
     extended = extend(field_ref, (one, two, side))
     mine = select(extended, own_local, inner, own_halo)
@@ -201,12 +204,12 @@
             lanes = slice((d - 1) * E, d * E)
             block = field_ref[rows, :] if d == 0 else jnp.concatenate([mine[rows, lanes], theirs[rows, lanes]], axis=1)
             stack += [masked(block, kinds[2 * d]), masked(block, kinds[2 * d + 1])]
-        product = jnp.dot(wide[...], jnp.concatenate(stack, axis=0), preferred_element_type=F32)
+        product = jnp.dot(wide[:, :WIDE], jnp.concatenate(stack, axis=0), preferred_element_type=F32)
         given = other[ROWS + r * DOF : ROWS + (r + 1) * DOF, :].astype(F32)
         given = jnp.concatenate([rhs[pl.ds(r, DOF, stride=RHS), :], given], axis=1)
         rounded = (given - product).astype(BF)
         parts.append(jnp.concatenate([masked(rounded, kinds[0]), masked(rounded, kinds[1])], axis=0))
-    changes = jnp.concatenate([jnp.dot(smooth[...], part, preferred_element_type=F32) for part in parts], axis=0)
+    changes = jnp.concatenate([jnp.dot(wide[:, WIDE:], part, preferred_element_type=F32) for part in parts], axis=0)
     if len(before) == 1 and before[0].shape[1] == CHIP:
         old = before[0][...]
     else:
@@ -231,7 +234,7 @@
                 block = field_ref[rows, :E] if d == 0 else beside[rows, (d - 1) * E : d * E]
                 stack += [masked(block, masks[2 * d]), masked(block, masks[2 * d + 1])]
             halves.append(jnp.concatenate(stack, axis=0))
-        product = jnp.dot(wide[...], jnp.concatenate(halves, axis=1), preferred_element_type=F32)
+        product = jnp.dot(wide[:, :WIDE], jnp.concatenate(halves, axis=1), preferred_element_type=F32)
         parts += [rhs[pl.ds(r + i, DOF, stride=RHS), :] - product[:, i * E : (i + 1) * E] for i in range(2)]
     residual = jnp.concatenate(parts, axis=0)
     rounded = residual.astype(BF)
@@ -305,9 +308,10 @@
     message_outs = [((n, ROWS), BF) for n in SENT]
     taken = (send_near, send_far, sub_send.reshape(1, -1), elem_type.reshape(1, -1), face_type, neighbours)
     taken += (pair_send.reshape(1, -1), partner.reshape(1, -1), guess, rhs)
-    (mine,) = call(
+    taken += (diag_blocks, face_blocks, smoother)
+    mine, wide = call(
         first_kernel,
-        [((2 * ROWS + INTS, E), BF)],
+        [((2 * ROWS + INTS, E), BF), ((DOF, WIDE + 2 * DOF), BF)],
         *taken,
         remote=len(taken),
         scratch=[pltpu.VMEM(x.shape, x.dtype) for x in taken]
@@ -316,16 +320,11 @@
     )
     other = swap(mine, "dom", inside)
     table_outs = [((E, FACES * E), BF), ((HALO, FACES * E), BF), ((2 * FACES + 2, 16, E), BF)]
-    own_field, own_lists, own_slots, own_local, own_halo, own_masks, wide, smooth = call(
+    own_field, own_lists, own_slots, own_local, own_halo, own_masks = call(
         own_kernel,
-        [((ROWS, E), BF), ((INTS, E), jnp.int32), ((NEAR, FACES * E), BF)]
-        + table_outs
-        + [((DOF, 2 * DOF * (FACES + 1)), BF), ((DOF, 2 * DOF), BF)],
+        [((ROWS, E), BF), ((INTS, E), jnp.int32), ((NEAR, FACES * E), BF)] + table_outs,
         place,
         mine,
-        diag_blocks,
-        face_blocks,
-        smoother,
         flops=1000000,
         scalars=1,
     )
@@ -358,7 +357,6 @@
             halo,
             masks,
             wide,
-            smooth,
             rhs,
             other,
             choice,

time: 68.6 us -> 67.9 us (0.990)
    unnamed x14 -> x10, local copies, waits for them, and re-layouts: 1.63 us -> 0.98 us
where the time goes in v6:
time: 67.9 us; the launch traced here: 67.4 us
  starting transfers between devices  26.8 us (39%)
  blocking collectives  25.7 us (38%)
  Pallas kernels  10.7 us (16%)
  waiting for transfers between devices  2.31 us (3%)
  local copies, waits for them, and re-layouts  0.98 us (1%)
  between operations  0.83 us (1%)
    ppermute x8, starting transfers between devices, swap(): return lax.ppermute(array, axis, route)  26.8 us
    all_to_all x3, blocking collectives, exchange(): side = lax.all_to_all(side, 'sub', 0, 0, tiled=True)  25.7 us
    pallas_call x8, Pallas kernels, call(): pl.pallas_call(kernel, out_shape=[jax.ShapeDtypeStruct(s, d) for s, d in...  10.7 us
    ppermute x8, waiting for transfers between devices, swap(): return lax.ppermute(array, axis, route)  2.31 us
  transfers between devices with their start and end apart: 8, of which 1 were waited for; matrix products, arithmetic and copies ran while one was open for 0% of the time, Pallas kernels for 2%

profile of v6, /device:TPU:240, one launch (start us, length us, event | category | flops | bytes accessed | tf_op | source)
XLA Modules:
  0.0 67.4 jit_solution(11310913779395193642)
XLA Ops:
  0.6 2.1 %shard_map.149 = (bf16[1056,128]{1,0:T(8,128)(2,1)}, bf16[64,1024]{1,0:T(8,128)(2,1)}) custom-call(s32[2,32]{1,0:T(2,128)} %refs_0_.1, s32[2,8]{1,0:T(2,128)} %refs_1_.1, s32[1,8]{1,0:T(1,128)} %bitcast.29, s32[1,128]{1,0:T(1,128)} %bitcast.30, s32[6,128]{1,0:T(8,128)} %refs_4_.1, s32[6,128]{1,0:T(8,128)} %refs_5_.1, s32[1,16]{1,0:T(1,128)} %bitcast.31, ...), custom_call_target="tpu_custom_call" | custom-call | bytes 662944 | tf_op jit(solution)/shard_map/pallas_call | solution.py:46
  2.7 1.9 %collective-permute-start = (bf16[1056,128]{1,0:T(8,128)(2,1)}, bf16[1056,128]{1,0:T(8,128)(2,1)S(1)}, u32[]{:S(2)}, u32[]{:S(2)}) collective-permute-start(bf16[1056,128]{1,0:T(8,128)(2,1)} %get-tuple-element.35.mine), channel_id=1, source_target_pairs={{0,4},{4,0},{8,12},{12,8},{16,20},{20,16},{24,28},{28,24},{32,36},... | collective-permute-start | bytes 811016 | tf_op jit(solution)/shard_map/ppermute | solution.py:34
  4.7 0.1 pad_add_fusion.place_ref
  4.8 0.0 copy-start
  4.8 1.0 %copy-done = bf16[1056,128]{1,0:T(8,128)(2,1)S(1)} copy-done((bf16[1056,128]{1,0:T(8,128)(2,1)S(1)}, bf16[1056,128]{1,0:T(8,128)(2,1)}, u32[]{:S(2)}) %copy-start) | copy-done | bytes 270360
  5.7 0.0 copy-start.4
  5.7 0.7 shard_map.150
  6.4 0.0 collective-permute-done.other.refs_10_
  6.4 0.0 copy-start.1
  6.4 0.0 copy-start.2
  6.4 1.0 %shard_map.151 = (bf16[512,256]{1,0:T(8,128)(2,1)S(1)}, bf16[160,256]{1,0:T(8,128)(2,1)S(1)}, bf16[128,768]{1,0:T(8,128)(2,1)S(1)}, bf16[128,768]{1,0:T(8,128)(2...) custom-call(s32[2]{0:T(128)S(1)} %pad_add_fusion.place_ref, ...), custom_call_target="tpu_custom_call" | custom-call | flops 41943040 | bytes 466952 | tf_op jit(solution)/shard_map/pallas_call | solution.py:46
  7.4 3.3 %collective-permute-start.1 = (bf16[80,512]{1,0:T(8,128)(2,1)S(1)}, bf16[80,512]{1,0:T(8,128)(2,1)S(1)}, u32[]{:S(2)}, u32[]{:S(2)}) collective-permute-start(bf16[80,512]{1,0:T(8,128)(2,1)S(1)} %get-tuple-element.40), channel_id=1, source_target_pairs={{8,16},{16,8},{12,20},{20,12},{24,32},{32,24},{28,36},{36,28},{40,... | collective-permute-start | bytes 245768 | tf_op jit(solution)/shard_map/ppermute | solution.py:34
  10.7 4.0 %collective-permute-start.2 = (bf16[80,512]{1,0:T(8,128)(2,1)S(1)}, bf16[80,512]{1,0:T(8,128)(2,1)S(1)}, u32[]{:S(2)}, u32[]{:S(2)}) collective-permute-start(bf16[80,512]{1,0:T(8,128)(2,1)S(1)} %get-tuple-element.41), channel_id=1, source_target_pairs={{0,8},{8,0},{4,12},{12,4},{16,24},{24,16},{20,28},{28,20},{32,40},... | collective-permute-start | bytes 245768 | tf_op jit(solution)/shard_map/ppermute | solution.py:34
  14.7 9.7 %all_to_all.33 = bf16[4,16,512]{2,1,0:T(8,128)(2,1)S(1)} all-to-all(bf16[4,16,512]{2,1,0:T(8,128)(2,1)S(1)} %bitcast.24), channel_id=1, replica_groups=mesh['dom'=128,'sub'=4] {'sub'}, dimensions={0} | all-to-all | bytes 131072 | tf_op jit(solution)/shard_map/all_to_all | solution.py:305
  24.4 0.0 collective-permute-done.1.two
  24.4 0.0 collective-permute-done.2.one
  24.4 0.0 copy-done.4
  24.4 0.0 copy-done.1
  24.4 0.0 copy-done.2
  24.4 1.9 %shard_map.152 = (f32[512,256]{1,0:T(8,128)S(1)}, bf16[512,256]{1,0:T(8,128)(2,1)S(1)}, bf16[80,512]{1,0:T(8,128)(2,1)S(1)}, bf16[80,512]{1,0:T(8,128)(2,1)S(1)}, bf16[64,512]{1,0:T(8,128)(2,1)S(1)}) custom-call(bf16[512,256]{1,0:T(8,128)(2,1)S(1)} %get-tuple-element.39.field_ref, bf16[80,512]{1,0:T(8,128)(2,1)S(1)} %collective-permute-done.1.two, ...), custom_call_target="tpu_custom_call" | custom-call | flops 889192448 | bytes 2891776 | tf_op jit(solution)/shard_map/pallas_call | solution.py:46
  26.4 1.9 %collective-permute-start.3 = (bf16[80,512]{1,0:T(8,128)(2,1)S(1)}, bf16[80,512]{1,0:T(8,128)(2,1)S(1)}, u32[]{:S(2)}, u32[]{:S(2)}) collective-permute-start(bf16[80,512]{1,0:T(8,128)(2,1)S(1)} %get-tuple-element.54), channel_id=1, source_target_pairs={{8,16},{16,8},{12,20},{20,12},{24,32},{32,24},{28,36},{36,28},{40,... | collective-permute-start | bytes 245768 | tf_op jit(solution)/shard_map/ppermute | solution.py:34
  28.3 5.1 %collective-permute-start.4 = (bf16[80,512]{1,0:T(8,128)(2,1)S(1)}, bf16[80,512]{1,0:T(8,128)(2,1)S(1)}, u32[]{:S(2)}, u32[]{:S(2)}) collective-permute-start(bf16[80,512]{1,0:T(8,128)(2,1)S(1)} %get-tuple-element.55), channel_id=1, source_target_pairs={{0,8},{8,0},{4,12},{12,4},{16,24},{24,16},{20,28},{28,20},{32,40},... | collective-permute-start | bytes 245768 | tf_op jit(solution)/shard_map/ppermute | solution.py:34
  33.4 8.0 %all_to_all.34 = bf16[4,16,512]{2,1,0:T(8,128)(2,1)S(1)} all-to-all(bf16[4,16,512]{2,1,0:T(8,128)(2,1)S(1)} %bitcast.27), channel_id=1, replica_groups=mesh['dom'=128,'sub'=4] {'sub'}, dimensions={0} | all-to-all | bytes 131072 | tf_op jit(solution)/shard_map/all_to_all | solution.py:305
  41.4 0.0 collective-permute-done.3.two
  41.4 0.0 collective-permute-done.4.one
  41.4 1.9 %shard_map.153 = (f32[512,256]{1,0:T(8,128)S(1)}, bf16[512,256]{1,0:T(8,128)(2,1)S(1)}, bf16[80,512]{1,0:T(8,128)(2,1)S(1)}, bf16[80,512]{1,0:T(8,128)(2,1)S(1)}, bf16[64,512]{1,0:T(8,128)(2,1)S(1)}) custom-call(bf16[512,256]{1,0:T(8,128)(2,1)S(1)} %get-tuple-element.53.field_ref, bf16[80,512]{1,0:T(8,128)(2,1)S(1)} %collective-permute-done.3.two, ...), custom_call_target="tpu_custom_call" | custom-call | flops 889192448 | bytes 3153920 | tf_op jit(solution)/shard_map/pallas_call | solution.py:46
  43.3 1.9 %collective-permute-start.5 = (bf16[80,512]{1,0:T(8,128)(2,1)S(1)}, bf16[80,512]{1,0:T(8,128)(2,1)S(1)}, u32[]{:S(2)}, u32[]{:S(2)}) collective-permute-start(bf16[80,512]{1,0:T(8,128)(2,1)S(1)} %get-tuple-element.59), channel_id=1, source_target_pairs={{8,16},{16,8},{12,20},{20,12},{24,32},{32,24},{28,36},{36,28},{40,... | collective-permute-start | bytes 245768 | tf_op jit(solution)/shard_map/ppermute | solution.py:34
  45.3 6.3 %collective-permute-start.6 = (bf16[80,512]{1,0:T(8,128)(2,1)S(1)}, bf16[80,512]{1,0:T(8,128)(2,1)S(1)}, u32[]{:S(2)}, u32[]{:S(2)}) collective-permute-start(bf16[80,512]{1,0:T(8,128)(2,1)S(1)} %get-tuple-element.60), channel_id=1, source_target_pairs={{0,8},{8,0},{4,12},{12,4},{16,24},{24,16},{20,28},{28,20},{32,40},... | collective-permute-start | bytes 245768 | tf_op jit(solution)/shard_map/ppermute | solution.py:34
  51.5 8.0 %all_to_all.35 = bf16[4,16,512]{2,1,0:T(8,128)(2,1)S(1)} all-to-all(bf16[4,16,512]{2,1,0:T(8,128)(2,1)S(1)} %bitcast.23), channel_id=1, replica_groups=mesh['dom'=128,'sub'=4] {'sub'}, dimensions={0} | all-to-all | bytes 131072 | tf_op jit(solution)/shard_map/all_to_all | solution.py:305
  59.5 0.0 collective-permute-done.5.two
  59.5 0.0 collective-permute-done.6.one
  59.5 1.2 %shard_map.154 = (f32[512,128]{1,0:T(8,128)S(1)}, bf16[512,128]{1,0:T(8,128)(2,1)S(1)}, bf16[16,512]{1,0:T(8,128)(2,1)S(1)}) custom-call(bf16[512,256]{1,0:T(8,128)(2,1)S(1)} %get-tuple-element.58.field_ref, bf16[80,512]{1,0:T(8,128)(2,1)S(1)} %collective-permute-done.5.two, bf16[80,512]{1,0:T(8,128)(2,1)S(1)} %collective-permute-done.6.one, ...), custom_call_target="tpu_custom_call" | custom-call | flops 444596224 | bytes 1597440 | tf_op jit(solution)/shard_map/pallas_call | solution.py:46
  60.7 2.5 %collective-permute-start.7 = (bf16[16,512]{1,0:T(8,128)(2,1)S(1)}, bf16[16,512]{1,0:T(8,128)(2,1)S(1)}, u32[]{:S(2)}, u32[]{:S(2)}) collective-permute-start(bf16[16,512]{1,0:T(8,128)(2,1)S(1)} %get-tuple-element.65), channel_id=1, source_target_pairs={{0,1},{1,0},{2,3},{3,2},{4,5},{5,4},{6,7},{7,6},{8,9},{9,8},{10,11... | collective-permute-start | bytes 49160 | tf_op jit(solution)/shard_map/ppermute | solution.py:34
  63.2 0.0 copy-start.3
  63.2 0.8 %shard_map.155 = (f32[512,128]{1,0:T(8,128)}, f32[512,128]{1,0:T(8,128)S(1)}) custom-call(f32[512,128]{1,0:T(8,128)S(1)} %get-tuple-element.62.residual_ref, bf16[512,128]{1,0:T(8,128)(2,1)S(1)} %get-tuple-element.63.rounded_ref, s32[32,128]{1,0:T(8,128)S(1)} %get-tuple-element.37.own_lists.lists), custom_call_target="tpu_custom_call" | custom-call | flops 111149056 | bytes 409600 | tf_op jit(solution)/shard_map/pallas_call | solution.py:46
  64.0 2.3 %collective-permute-done.7.incoming = bf16[16,512]{1,0:T(8,128)(2,1)S(1)} collective-permute-done((bf16[16,512]{1,0:T(8,128)(2,1)S(1)}, bf16[16,512]{1,0:T(8,128)(2,1)S(1)}, u32[]{:S(2)}, u32[]{:S(2)}) %collective-permute-start.7) | collective-permute-done | bytes 16416 | tf_op jit(solution)/shard_map/ppermute | solution.py:34
  66.3 0.0 copy-done.3
  66.3 1.1 %shard_map.156 = f32[512,128]{1,0:T(8,128)} custom-call(f32[512,128]{1,0:T(8,128)S(1)} %get-tuple-element.64.half_ref, bf16[16,512]{1,0:T(8,128)(2,1)S(1)} %collective-permute-done.7.incoming, s32[32,128]{1,0:T(8,128)S(1)} %get-tuple-element.37.own_lists.lists, bf16[64,64]{1,0:T(8,128)(2,1)S(1)} %copy-done.3, f32[512,256]{1,0:T(8,128)S(1)} %get-tuple-element.66.iterate), custom_call_target="tpu_custom_call" | custom-call | flops 111149056 | bytes 827392 | tf_op jit(solution)/shard_map/pallas_call | solution.py:46
Async XLA Ops:
  2.7 3.7 %collective-permute-start = (bf16[1056,128]{1,0:T(8,128)(2,1)}, bf16[1056,128]{1,0:T(8,128)(2,1)S(1)}, u32[]{:S(2)}, u32[]{:S(2)}) collective-permute-start(bf16[1056,128]{1,0:T(8,128)(2,1)} %get-tuple-element.35.mine), channel_id=1, source_target_pairs={{0,4},{4,0},{8,12},{12,8},{16,20},{20,16},{24,28},{28,24},{32,36},... | collective-permute-start | bytes 811016 | tf_op jit(solution)/shard_map/ppermute | solution.py:34
  4.8 1.0 %copy-start = (bf16[1056,128]{1,0:T(8,128)(2,1)S(1)}, bf16[1056,128]{1,0:T(8,128)(2,1)}, u32[]{:S(2)}) copy-start(bf16[1056,128]{1,0:T(8,128)(2,1)} %get-tuple-element.35.mine) | copy-start | bytes 811012
  5.7 18.7 %copy-start.4 = (bf16[64,1024]{1,0:T(8,128)(2,1)S(1)}, bf16[64,1024]{1,0:T(8,128)(2,1)}, u32[]{:S(2)}) copy-start(bf16[64,1024]{1,0:T(8,128)(2,1)} %get-tuple-element.51.refs_8_.wide) | copy-start | bytes 393220
  6.4 18.0 %copy-start.1 = (f32[64,8,128]{2,1,0:T(8,128)S(1)}, f32[64,8,128]{2,1,0:T(8,128)}, u32[]{:S(2)}) copy-start(f32[64,8,128]{2,1,0:T(8,128)} %param.15) | copy-start | bytes 786436
  6.4 18.0 %copy-start.2 = (f32[64,8,128]{2,1,0:T(8,128)S(1)}, f32[64,8,128]{2,1,0:T(8,128)}, u32[]{:S(2)}) copy-start(f32[64,8,128]{2,1,0:T(8,128)} %param.14) | copy-start | bytes 786436
  7.4 17.0 %collective-permute-start.1 = (bf16[80,512]{1,0:T(8,128)(2,1)S(1)}, bf16[80,512]{1,0:T(8,128)(2,1)S(1)}, u32[]{:S(2)}, u32[]{:S(2)}) collective-permute-start(bf16[80,512]{1,0:T(8,128)(2,1)S(1)} %get-tuple-element.40), channel_id=1, source_target_pairs={{8,16},{16,8},{12,20},{20,12},{24,32},{32,24},{28,36},{36,28},{40,... | collective-permute-start | bytes 245768 | tf_op jit(solution)/shard_map/ppermute | solution.py:34
  10.7 13.8 %collective-permute-start.2 = (bf16[80,512]{1,0:T(8,128)(2,1)S(1)}, bf16[80,512]{1,0:T(8,128)(2,1)S(1)}, u32[]{:S(2)}, u32[]{:S(2)}) collective-permute-start(bf16[80,512]{1,0:T(8,128)(2,1)S(1)} %get-tuple-element.41), channel_id=1, source_target_pairs={{0,8},{8,0},{4,12},{12,4},{16,24},{24,16},{20,28},{28,20},{32,40},... | collective-permute-start | bytes 245768 | tf_op jit(solution)/shard_map/ppermute | solution.py:34
  26.4 15.0 %collective-permute-start.3 = (bf16[80,512]{1,0:T(8,128)(2,1)S(1)}, bf16[80,512]{1,0:T(8,128)(2,1)S(1)}, u32[]{:S(2)}, u32[]{:S(2)}) collective-permute-start(bf16[80,512]{1,0:T(8,128)(2,1)S(1)} %get-tuple-element.54), channel_id=1, source_target_pairs={{8,16},{16,8},{12,20},{20,12},{24,32},{32,24},{28,36},{36,28},{40,... | collective-permute-start | bytes 245768 | tf_op jit(solution)/shard_map/ppermute | solution.py:34
  28.3 13.1 %collective-permute-start.4 = (bf16[80,512]{1,0:T(8,128)(2,1)S(1)}, bf16[80,512]{1,0:T(8,128)(2,1)S(1)}, u32[]{:S(2)}, u32[]{:S(2)}) collective-permute-start(bf16[80,512]{1,0:T(8,128)(2,1)S(1)} %get-tuple-element.55), channel_id=1, source_target_pairs={{0,8},{8,0},{4,12},{12,4},{16,24},{24,16},{20,28},{28,20},{32,40},... | collective-permute-start | bytes 245768 | tf_op jit(solution)/shard_map/ppermute | solution.py:34
  43.3 16.2 %collective-permute-start.5 = (bf16[80,512]{1,0:T(8,128)(2,1)S(1)}, bf16[80,512]{1,0:T(8,128)(2,1)S(1)}, u32[]{:S(2)}, u32[]{:S(2)}) collective-permute-start(bf16[80,512]{1,0:T(8,128)(2,1)S(1)} %get-tuple-element.59), channel_id=1, source_target_pairs={{8,16},{16,8},{12,20},{20,12},{24,32},{32,24},{28,36},{36,28},{40,... | collective-permute-start | bytes 245768 | tf_op jit(solution)/shard_map/ppermute | solution.py:34
  45.3 14.3 %collective-permute-start.6 = (bf16[80,512]{1,0:T(8,128)(2,1)S(1)}, bf16[80,512]{1,0:T(8,128)(2,1)S(1)}, u32[]{:S(2)}, u32[]{:S(2)}) collective-permute-start(bf16[80,512]{1,0:T(8,128)(2,1)S(1)} %get-tuple-element.60), channel_id=1, source_target_pairs={{0,8},{8,0},{4,12},{12,4},{16,24},{24,16},{20,28},{28,20},{32,40},... | collective-permute-start | bytes 245768 | tf_op jit(solution)/shard_map/ppermute | solution.py:34
  60.7 5.6 %collective-permute-start.7 = (bf16[16,512]{1,0:T(8,128)(2,1)S(1)}, bf16[16,512]{1,0:T(8,128)(2,1)S(1)}, u32[]{:S(2)}, u32[]{:S(2)}) collective-permute-start(bf16[16,512]{1,0:T(8,128)(2,1)S(1)} %get-tuple-element.65), channel_id=1, source_target_pairs={{0,1},{1,0},{2,3},{3,2},{4,5},{5,4},{6,7},{7,6},{8,9},{9,8},{10,11... | collective-permute-start | bytes 49160 | tf_op jit(solution)/shard_map/ppermute | solution.py:34
  63.2 3.2 %copy-start.3 = (bf16[64,64]{1,0:T(8,128)(2,1)S(1)}, bf16[64,64]{1,0:T(8,128)(2,1)}, u32[]{:S(2)}) copy-start(bf16[64,64]{1,0:T(8,128)(2,1)} %inverse.1) | copy-start | bytes 24580

commit v7 on v6

--- a/solution.py
+++ b/solution.py
@@ -211,14 +211,14 @@
         parts.append(jnp.concatenate([masked(rounded, kinds[0]), masked(rounded, kinds[1])], axis=0))
     changes = jnp.concatenate([jnp.dot(wide[:, WIDE:], part, preferred_element_type=F32) for part in parts], axis=0)
     if len(before) == 1 and before[0].shape[1] == CHIP:
-        old = before[0][...]
+        old = field_ref[...].astype(F32) + before[0][...].astype(F32)
     else:
         own = jnp.concatenate([before[0][pl.ds(r, DOF, stride=RHS), :] for r in range(RHS)], axis=0)
         old = jnp.concatenate([own, other[:ROWS, :].astype(F32)], axis=1)
     new = old + changes
     rounded = new.astype(BF)
     send(choice[...], rounded, zip(messages, (CROSS, CROSS, SIDE)))
-    after[...] = new
+    after[...] = (new - rounded.astype(F32)).astype(BF)
     next_field[...] = rounded
 
 
@@ -259,7 +259,7 @@
     half_ref[...] = residual + mates
 
 
-def coarse_kernel(half_ref, incoming, lists, inverse, iterate, solution_ref):
+def coarse_kernel(half_ref, incoming, lists, inverse, field_ref, rest, solution_ref):
     mates = lax.dot_general(
         incoming[...], mate_picker(lists[22:23, :], E, PAIRS), (((0,), (0,)), ((), ())), preferred_element_type=F32
     )
@@ -268,7 +268,10 @@
     for r in range(0, RHS, 2):
         pair = jnp.concatenate([coarse[s * DOF : (s + 1) * DOF, :] for s in (r, r + 1)], axis=1)
         update = jnp.dot(inverse[...], pair, preferred_element_type=F32)
-        solved += [iterate[(r + i) * DOF : (r + i + 1) * DOF, :E] + update[:, i * E : (i + 1) * E] for i in range(2)]
+        for i in range(2):
+            rows = slice((r + i) * DOF, (r + i + 1) * DOF)
+            iterate = field_ref[rows, :E].astype(F32) + rest[rows, :E].astype(F32)
+            solved.append(iterate + update[:, i * E : (i + 1) * E])
     for r in range(RHS):
         solution_ref[pl.ds(r, DOF, stride=RHS), :] = solved[r]
 
@@ -345,7 +348,7 @@
     for _ in range(SWEEPS):
         iterate, field, *messages = call(
             sweep_kernel,
-            [((ROWS, CHIP), F32), ((ROWS, CHIP), BF)] + message_outs,
+            [((ROWS, CHIP), BF), ((ROWS, CHIP), BF)] + message_outs,
             field,
             *brought,
             own_local,
@@ -395,6 +398,7 @@
         incoming,
         own_lists,
         coarse_inverse,
+        field,
         iterate,
         flops=work // 8,
     )
@@ -402,7 +406,7 @@
     return (solved.reshape(shape), residual.reshape(shape))
 
 
-SENT = (SIDE + 16, SIDE + 16, SIDE)
+SENT = (CROSS, CROSS, SIDE)
 
 
 def solution(mesh):

time: 67.9 us -> 67.9 us (level)
  the two profiles are of different devices: /device:TPU:240 before, /device:TPU:250 now
where the time goes in v7:
time: 67.9 us; the launch traced here: 67.2 us
  starting transfers between devices  37.8 us (56%)
  waiting for transfers between devices  15 us (22%)
  Pallas kernels  12.5 us (18%)
  local copies, waits for them, and re-layouts  0.98 us (1%)
  between operations  0.82 us (1%)
    ppermute x8, starting transfers between devices, swap(): return lax.ppermute(array, axis, route)  23.4 us
    ppermute x8, waiting for transfers between devices, swap(): return lax.ppermute(array, axis, route)  15 us
    all_to_all x3, starting transfers between devices, exchange(): side = lax.all_to_all(side, 'sub', 0, 0, tiled=True)  14.4 us
    pallas_call x8, Pallas kernels, call(): pl.pallas_call(kernel, out_shape=[jax.ShapeDtypeStruct(s, d) for s, d in...  12.5 us
  transfers between devices with their start and end apart: 11, of which 7 were waited for; matrix products, arithmetic and copies ran while one was open for 0% of the time, Pallas kernels for 2%

profile of v7, /device:TPU:250, one launch (start us, length us, event | category | flops | bytes accessed | tf_op | source)
XLA Modules:
  0.0 67.2 jit_solution(3602305310856241419)
XLA Ops:
  0.6 2.1 %shard_map.149 = (bf16[1056,128]{1,0:T(8,128)(2,1)}, bf16[64,1024]{1,0:T(8,128)(2,1)}) custom-call(s32[2,32]{1,0:T(2,128)} %refs_0_.1, s32[2,8]{1,0:T(2,128)} %refs_1_.1, s32[1,8]{1,0:T(1,128)} %bitcast.26, s32[1,128]{1,0:T(1,128)} %bitcast.27, s32[6,128]{1,0:T(8,128)} %refs_4_.1, s32[6,128]{1,0:T(8,128)} %refs_5_.1, s32[1,16]{1,0:T(1,128)} %bitcast.28, ...), custom_call_target="tpu_custom_call" | custom-call | bytes 662944 | tf_op jit(solution)/shard_map/pallas_call | solution.py:46
  2.7 1.9 %collective-permute-start = (bf16[1056,128]{1,0:T(8,128)(2,1)}, bf16[1056,128]{1,0:T(8,128)(2,1)S(1)}, u32[]{:S(2)}, u32[]{:S(2)}) collective-permute-start(bf16[1056,128]{1,0:T(8,128)(2,1)} %get-tuple-element.35.mine), channel_id=1, source_target_pairs={{0,4},{4,0},{8,12},{12,8},{16,20},{20,16},{24,28},{28,24},{32,36},... | collective-permute-start | bytes 811016 | tf_op jit(solution)/shard_map/ppermute | solution.py:34
  4.7 0.1 pad_add_fusion.place_ref
  4.8 0.0 copy-start
  4.8 1.0 %copy-done = bf16[1056,128]{1,0:T(8,128)(2,1)S(1)} copy-done((bf16[1056,128]{1,0:T(8,128)(2,1)S(1)}, bf16[1056,128]{1,0:T(8,128)(2,1)}, u32[]{:S(2)}) %copy-start) | copy-done | bytes 270360
  5.7 0.0 copy-start.4
  5.7 0.7 shard_map.150
  6.4 0.0 collective-permute-done.other.refs_10_
  6.4 0.0 copy-start.1
  6.4 0.0 copy-start.2
  6.4 1.5 %shard_map.151 = (bf16[512,256]{1,0:T(8,128)(2,1)S(1)}, bf16[160,256]{1,0:T(8,128)(2,1)S(1)}, bf16[128,768]{1,0:T(8,128)(2,1)S(1)}, bf16[128,768]{1,0:T(8,128)(2...) custom-call(s32[2]{0:T(128)S(1)} %pad_add_fusion.place_ref, ...), custom_call_target="tpu_custom_call" | custom-call | flops 41943040 | bytes 466952 | tf_op jit(solution)/shard_map/pallas_call | solution.py:46
  7.9 4.8 %all-to-all-start = ((bf16[4,16,512]{2,1,0:T(8,128)(2,1)}), bf16[4,16,512]{2,1,0:T(8,128)(2,1)S(1)}, u32[]{:S(2)}, u32[]{:S(2)}) async-start(bf16[4,16,512]{2,1,0:T(8,128)(2,1)} %bitcast.8), calls=%async_computation | async-start | bytes 131072 | tf_op jit(solution)/shard_map/all_to_all | solution.py:308
  12.7 4.7 %collective-permute-start.1 = (bf16[48,512]{1,0:T(8,128)(2,1)S(1)}, bf16[48,512]{1,0:T(8,128)(2,1)S(1)}, u32[]{:S(2)}, u32[]{:S(2)}) collective-permute-start(bf16[48,512]{1,0:T(8,128)(2,1)S(1)} %get-tuple-element.40), channel_id=1, source_target_pairs={{8,16},{16,8},{12,20},{20,12},{24,32},{32,24},{28,36},{36,28},{40,... | collective-permute-start | bytes 147464 | tf_op jit(solution)/shard_map/ppermute | solution.py:34
  17.4 1.9 %collective-permute-start.2 = (bf16[48,512]{1,0:T(8,128)(2,1)S(1)}, bf16[48,512]{1,0:T(8,128)(2,1)S(1)}, u32[]{:S(2)}, u32[]{:S(2)}) collective-permute-start(bf16[48,512]{1,0:T(8,128)(2,1)S(1)} %get-tuple-element.41), channel_id=1, source_target_pairs={{0,8},{8,0},{4,12},{12,4},{16,24},{24,16},{20,28},{28,20},{32,40},... | collective-permute-start | bytes 147464 | tf_op jit(solution)/shard_map/ppermute | solution.py:34
  19.4 0.0 all-to-all-done
  19.4 2.7 %collective-permute-done.1.two = bf16[48,512]{1,0:T(8,128)(2,1)S(1)} collective-permute-done((bf16[48,512]{1,0:T(8,128)(2,1)S(1)}, bf16[48,512]{1,0:T(8,128)(2,1)S(1)}, u32[]{:S(2)}, u32[]{:S(2)}) %collective-permute-start.1) | collective-permute-done | bytes 49184 | tf_op jit(solution)/shard_map/ppermute | solution.py:34
  22.0 1.4 %collective-permute-done.2.one = bf16[48,512]{1,0:T(8,128)(2,1)S(1)} collective-permute-done((bf16[48,512]{1,0:T(8,128)(2,1)S(1)}, bf16[48,512]{1,0:T(8,128)(2,1)S(1)}, u32[]{:S(2)}, u32[]{:S(2)}) %collective-permute-start.2) | collective-permute-done | bytes 49184 | tf_op jit(solution)/shard_map/ppermute | solution.py:34
  23.4 0.0 copy-done.4
  23.4 0.0 copy-done.1
  23.4 0.0 copy-done.2
  23.4 2.6 %shard_map.152 = (bf16[512,256]{1,0:T(8,128)(2,1)S(1)}, bf16[512,256]{1,0:T(8,128)(2,1)S(1)}, bf16[48,512]{1,0:T(8,128)(2,1)S(1)}, bf16[48,512]{1,0:T(8,128)(2,1)S(1)}, bf16[64,512]{1,0:T(8,128)(2,1)}) custom-call(bf16[512,256]{1,0:T(8,128)(2,1)S(1)} %get-tuple-element.39.field_ref, bf16[48,512]{1,0:T(8,128)(2,1)S(1)} %collective-permute-done.1.two, ...), custom_call_target="tpu_custom_call" | custom-call | flops 889192448 | bytes 2826240 | tf_op jit(solution)/shard_map/pallas_call | solution.py:46
  26.0 4.8 %all-to-all-start.1 = ((bf16[4,16,512]{2,1,0:T(8,128)(2,1)}), bf16[4,16,512]{2,1,0:T(8,128)(2,1)S(1)}, u32[]{:S(2)}, u32[]{:S(2)}) async-start(bf16[4,16,512]{2,1,0:T(8,128)(2,1)} %bitcast.10), calls=%async_computation.1 | async-start | bytes 131072 | tf_op jit(solution)/shard_map/all_to_all | solution.py:308
  30.8 4.5 %collective-permute-start.3 = (bf16[48,512]{1,0:T(8,128)(2,1)S(1)}, bf16[48,512]{1,0:T(8,128)(2,1)S(1)}, u32[]{:S(2)}, u32[]{:S(2)}) collective-permute-start(bf16[48,512]{1,0:T(8,128)(2,1)S(1)} %get-tuple-element.54), channel_id=1, source_target_pairs={{8,16},{16,8},{12,20},{20,12},{24,32},{32,24},{28,36},{36,28},{40,... | collective-permute-start | bytes 147464 | tf_op jit(solution)/shard_map/ppermute | solution.py:34
  35.3 1.9 %collective-permute-start.4 = (bf16[48,512]{1,0:T(8,128)(2,1)S(1)}, bf16[48,512]{1,0:T(8,128)(2,1)S(1)}, u32[]{:S(2)}, u32[]{:S(2)}) collective-permute-start(bf16[48,512]{1,0:T(8,128)(2,1)S(1)} %get-tuple-element.55), channel_id=1, source_target_pairs={{0,8},{8,0},{4,12},{12,4},{16,24},{24,16},{20,28},{28,20},{32,40},... | collective-permute-start | bytes 147464 | tf_op jit(solution)/shard_map/ppermute | solution.py:34
  37.2 0.0 all-to-all-done.1
  37.2 2.9 %collective-permute-done.3.two = bf16[48,512]{1,0:T(8,128)(2,1)S(1)} collective-permute-done((bf16[48,512]{1,0:T(8,128)(2,1)S(1)}, bf16[48,512]{1,0:T(8,128)(2,1)S(1)}, u32[]{:S(2)}, u32[]{:S(2)}) %collective-permute-start.3) | collective-permute-done | bytes 49184 | tf_op jit(solution)/shard_map/ppermute | solution.py:34
  40.1 1.2 %collective-permute-done.4.one = bf16[48,512]{1,0:T(8,128)(2,1)S(1)} collective-permute-done((bf16[48,512]{1,0:T(8,128)(2,1)S(1)}, bf16[48,512]{1,0:T(8,128)(2,1)S(1)}, u32[]{:S(2)}, u32[]{:S(2)}) %collective-permute-start.4) | collective-permute-done | bytes 49184 | tf_op jit(solution)/shard_map/ppermute | solution.py:34
  41.3 2.6 %shard_map.153 = (bf16[512,256]{1,0:T(8,128)(2,1)S(1)}, bf16[512,256]{1,0:T(8,128)(2,1)S(1)}, bf16[48,512]{1,0:T(8,128)(2,1)S(1)}, bf16[48,512]{1,0:T(8,128)(2,1)S(1)}, bf16[64,512]{1,0:T(8,128)(2,1)}) custom-call(bf16[512,256]{1,0:T(8,128)(2,1)S(1)} %get-tuple-element.53.field_ref, bf16[48,512]{1,0:T(8,128)(2,1)S(1)} %collective-permute-done.3.two, ...), custom_call_target="tpu_custom_call" | custom-call | flops 889192448 | bytes 2826240 | tf_op jit(solution)/shard_map/pallas_call | solution.py:46
  43.8 4.8 %all-to-all-start.2 = ((bf16[4,16,512]{2,1,0:T(8,128)(2,1)}), bf16[4,16,512]{2,1,0:T(8,128)(2,1)S(1)}, u32[]{:S(2)}, u32[]{:S(2)}) async-start(bf16[4,16,512]{2,1,0:T(8,128)(2,1)} %bitcast.12), calls=%async_computation.2 | async-start | bytes 131072 | tf_op jit(solution)/shard_map/all_to_all | solution.py:308
  48.6 4.7 %collective-permute-start.5 = (bf16[48,512]{1,0:T(8,128)(2,1)S(1)}, bf16[48,512]{1,0:T(8,128)(2,1)S(1)}, u32[]{:S(2)}, u32[]{:S(2)}) collective-permute-start(bf16[48,512]{1,0:T(8,128)(2,1)S(1)} %get-tuple-element.59), channel_id=1, source_target_pairs={{8,16},{16,8},{12,20},{20,12},{24,32},{32,24},{28,36},{36,28},{40,... | collective-permute-start | bytes 147464 | tf_op jit(solution)/shard_map/ppermute | solution.py:34
  53.3 1.9 %collective-permute-start.6 = (bf16[48,512]{1,0:T(8,128)(2,1)S(1)}, bf16[48,512]{1,0:T(8,128)(2,1)S(1)}, u32[]{:S(2)}, u32[]{:S(2)}) collective-permute-start(bf16[48,512]{1,0:T(8,128)(2,1)S(1)} %get-tuple-element.60), channel_id=1, source_target_pairs={{0,8},{8,0},{4,12},{12,4},{16,24},{24,16},{20,28},{28,20},{32,40},... | collective-permute-start | bytes 147464 | tf_op jit(solution)/shard_map/ppermute | solution.py:34
  55.3 0.0 all-to-all-done.2
  55.3 2.7 %collective-permute-done.5.two = bf16[48,512]{1,0:T(8,128)(2,1)S(1)} collective-permute-done((bf16[48,512]{1,0:T(8,128)(2,1)S(1)}, bf16[48,512]{1,0:T(8,128)(2,1)S(1)}, u32[]{:S(2)}, u32[]{:S(2)}) %collective-permute-start.5) | collective-permute-done | bytes 49184 | tf_op jit(solution)/shard_map/ppermute | solution.py:34
  57.9 1.4 %collective-permute-done.6.one = bf16[48,512]{1,0:T(8,128)(2,1)S(1)} collective-permute-done((bf16[48,512]{1,0:T(8,128)(2,1)S(1)}, bf16[48,512]{1,0:T(8,128)(2,1)S(1)}, u32[]{:S(2)}, u32[]{:S(2)}) %collective-permute-start.6) | collective-permute-done | bytes 49184 | tf_op jit(solution)/shard_map/ppermute | solution.py:34
  59.3 1.2 %shard_map.154 = (f32[512,128]{1,0:T(8,128)S(1)}, bf16[512,128]{1,0:T(8,128)(2,1)S(1)}, bf16[16,512]{1,0:T(8,128)(2,1)S(1)}) custom-call(bf16[512,256]{1,0:T(8,128)(2,1)S(1)} %get-tuple-element.58.field_ref, bf16[48,512]{1,0:T(8,128)(2,1)S(1)} %collective-permute-done.5.two, bf16[48,512]{1,0:T(8,128)(2,1)S(1)} %collective-permute-done.6.one, ...), custom_call_target="tpu_custom_call" | custom-call | flops 444596224 | bytes 1531904 | tf_op jit(solution)/shard_map/pallas_call | solution.py:46
  60.5 1.9 %collective-permute-start.7 = (bf16[16,512]{1,0:T(8,128)(2,1)S(1)}, bf16[16,512]{1,0:T(8,128)(2,1)S(1)}, u32[]{:S(2)}, u32[]{:S(2)}) collective-permute-start(bf16[16,512]{1,0:T(8,128)(2,1)S(1)} %get-tuple-element.65), channel_id=1, source_target_pairs={{0,1},{1,0},{2,3},{3,2},{4,5},{5,4},{6,7},{7,6},{8,9},{9,8},{10,11... | collective-permute-start | bytes 49160 | tf_op jit(solution)/shard_map/ppermute | solution.py:34
  62.4 0.0 copy-start.3
  62.4 0.8 %shard_map.155 = (f32[512,128]{1,0:T(8,128)}, f32[512,128]{1,0:T(8,128)S(1)}) custom-call(f32[512,128]{1,0:T(8,128)S(1)} %get-tuple-element.62.residual_ref, bf16[512,128]{1,0:T(8,128)(2,1)S(1)} %get-tuple-element.63.rounded_ref, s32[32,128]{1,0:T(8,128)S(1)} %get-tuple-element.37.own_lists.lists), custom_call_target="tpu_custom_call" | custom-call | flops 111149056 | bytes 409600 | tf_op jit(solution)/shard_map/pallas_call | solution.py:46
  63.3 2.8 %collective-permute-done.7.incoming = bf16[16,512]{1,0:T(8,128)(2,1)S(1)} collective-permute-done((bf16[16,512]{1,0:T(8,128)(2,1)S(1)}, bf16[16,512]{1,0:T(8,128)(2,1)S(1)}, u32[]{:S(2)}, u32[]{:S(2)}) %collective-permute-start.7) | collective-permute-done | bytes 16416 | tf_op jit(solution)/shard_map/ppermute | solution.py:34
  66.1 0.0 copy-done.3
  66.1 1.1 %shard_map.156 = f32[512,128]{1,0:T(8,128)} custom-call(f32[512,128]{1,0:T(8,128)S(1)} %get-tuple-element.64.half_ref, bf16[16,512]{1,0:T(8,128)(2,1)S(1)} %collective-permute-done.7.incoming, s32[32,128]{1,0:T(8,128)S(1)} %get-tuple-element.37.own_lists.lists, bf16[64,64]{1,0:T(8,128)(2,1)S(1)} %copy-done.3, ...), custom_call_target="tpu_custom_call" | custom-call | flops 111149056 | bytes 827392 | tf_op jit(solution)/shard_map/pallas_call | solution.py:46
Async XLA Ops:
  2.7 3.7 %collective-permute-start = (bf16[1056,128]{1,0:T(8,128)(2,1)}, bf16[1056,128]{1,0:T(8,128)(2,1)S(1)}, u32[]{:S(2)}, u32[]{:S(2)}) collective-permute-start(bf16[1056,128]{1,0:T(8,128)(2,1)} %get-tuple-element.35.mine), channel_id=1, source_target_pairs={{0,4},{4,0},{8,12},{12,8},{16,20},{20,16},{24,28},{28,24},{32,36},... | collective-permute-start | bytes 811016 | tf_op jit(solution)/shard_map/ppermute | solution.py:34
  4.8 1.0 %copy-start = (bf16[1056,128]{1,0:T(8,128)(2,1)S(1)}, bf16[1056,128]{1,0:T(8,128)(2,1)}, u32[]{:S(2)}) copy-start(bf16[1056,128]{1,0:T(8,128)(2,1)} %get-tuple-element.35.mine) | copy-start | bytes 811012
  5.7 17.7 %copy-start.4 = (bf16[64,1024]{1,0:T(8,128)(2,1)S(1)}, bf16[64,1024]{1,0:T(8,128)(2,1)}, u32[]{:S(2)}) copy-start(bf16[64,1024]{1,0:T(8,128)(2,1)} %get-tuple-element.51.refs_8_.wide) | copy-start | bytes 393220
  6.4 17.0 %copy-start.1 = (f32[64,8,128]{2,1,0:T(8,128)S(1)}, f32[64,8,128]{2,1,0:T(8,128)}, u32[]{:S(2)}) copy-start(f32[64,8,128]{2,1,0:T(8,128)} %param.15) | copy-start | bytes 786436
  6.4 17.0 %copy-start.2 = (f32[64,8,128]{2,1,0:T(8,128)S(1)}, f32[64,8,128]{2,1,0:T(8,128)}, u32[]{:S(2)}) copy-start(f32[64,8,128]{2,1,0:T(8,128)} %param.14) | copy-start | bytes 786436
  7.9 11.4 %all-to-all-start = ((bf16[4,16,512]{2,1,0:T(8,128)(2,1)}), bf16[4,16,512]{2,1,0:T(8,128)(2,1)S(1)}, u32[]{:S(2)}, u32[]{:S(2)}) async-start(bf16[4,16,512]{2,1,0:T(8,128)(2,1)} %bitcast.8), calls=%async_computation | async-start | bytes 131072 | tf_op jit(solution)/shard_map/all_to_all | solution.py:308
  12.7 9.3 %collective-permute-start.1 = (bf16[48,512]{1,0:T(8,128)(2,1)S(1)}, bf16[48,512]{1,0:T(8,128)(2,1)S(1)}, u32[]{:S(2)}, u32[]{:S(2)}) collective-permute-start(bf16[48,512]{1,0:T(8,128)(2,1)S(1)} %get-tuple-element.40), channel_id=1, source_target_pairs={{8,16},{16,8},{12,20},{20,12},{24,32},{32,24},{28,36},{36,28},{40,... | collective-permute-start | bytes 147464 | tf_op jit(solution)/shard_map/ppermute | solution.py:34
  17.4 6.0 %collective-permute-start.2 = (bf16[48,512]{1,0:T(8,128)(2,1)S(1)}, bf16[48,512]{1,0:T(8,128)(2,1)S(1)}, u32[]{:S(2)}, u32[]{:S(2)}) collective-permute-start(bf16[48,512]{1,0:T(8,128)(2,1)S(1)} %get-tuple-element.41), channel_id=1, source_target_pairs={{0,8},{8,0},{4,12},{12,4},{16,24},{24,16},{20,28},{28,20},{32,40},... | collective-permute-start | bytes 147464 | tf_op jit(solution)/shard_map/ppermute | solution.py:34
  26.0 11.2 %all-to-all-start.1 = ((bf16[4,16,512]{2,1,0:T(8,128)(2,1)}), bf16[4,16,512]{2,1,0:T(8,128)(2,1)S(1)}, u32[]{:S(2)}, u32[]{:S(2)}) async-start(bf16[4,16,512]{2,1,0:T(8,128)(2,1)} %bitcast.10), calls=%async_computation.1 | async-start | bytes 131072 | tf_op jit(solution)/shard_map/all_to_all | solution.py:308
  30.8 9.3 %collective-permute-start.3 = (bf16[48,512]{1,0:T(8,128)(2,1)S(1)}, bf16[48,512]{1,0:T(8,128)(2,1)S(1)}, u32[]{:S(2)}, u32[]{:S(2)}) collective-permute-start(bf16[48,512]{1,0:T(8,128)(2,1)S(1)} %get-tuple-element.54), channel_id=1, source_target_pairs={{8,16},{16,8},{12,20},{20,12},{24,32},{32,24},{28,36},{36,28},{40,... | collective-permute-start | bytes 147464 | tf_op jit(solution)/shard_map/ppermute | solution.py:34
  35.3 6.0 %collective-permute-start.4 = (bf16[48,512]{1,0:T(8,128)(2,1)S(1)}, bf16[48,512]{1,0:T(8,128)(2,1)S(1)}, u32[]{:S(2)}, u32[]{:S(2)}) collective-permute-start(bf16[48,512]{1,0:T(8,128)(2,1)S(1)} %get-tuple-element.55), channel_id=1, source_target_pairs={{0,8},{8,0},{4,12},{12,4},{16,24},{24,16},{20,28},{28,20},{32,40},... | collective-permute-start | bytes 147464 | tf_op jit(solution)/shard_map/ppermute | solution.py:34
  43.8 11.4 %all-to-all-start.2 = ((bf16[4,16,512]{2,1,0:T(8,128)(2,1)}), bf16[4,16,512]{2,1,0:T(8,128)(2,1)S(1)}, u32[]{:S(2)}, u32[]{:S(2)}) async-start(bf16[4,16,512]{2,1,0:T(8,128)(2,1)} %bitcast.12), calls=%async_computation.2 | async-start | bytes 131072 | tf_op jit(solution)/shard_map/all_to_all | solution.py:308
  48.6 9.3 %collective-permute-start.5 = (bf16[48,512]{1,0:T(8,128)(2,1)S(1)}, bf16[48,512]{1,0:T(8,128)(2,1)S(1)}, u32[]{:S(2)}, u32[]{:S(2)}) collective-permute-start(bf16[48,512]{1,0:T(8,128)(2,1)S(1)} %get-tuple-element.59), channel_id=1, source_target_pairs={{8,16},{16,8},{12,20},{20,12},{24,32},{32,24},{28,36},{36,28},{40,... | collective-permute-start | bytes 147464 | tf_op jit(solution)/shard_map/ppermute | solution.py:34
  53.3 6.0 %collective-permute-start.6 = (bf16[48,512]{1,0:T(8,128)(2,1)S(1)}, bf16[48,512]{1,0:T(8,128)(2,1)S(1)}, u32[]{:S(2)}, u32[]{:S(2)}) collective-permute-start(bf16[48,512]{1,0:T(8,128)(2,1)S(1)} %get-tuple-element.60), channel_id=1, source_target_pairs={{0,8},{8,0},{4,12},{12,4},{16,24},{24,16},{20,28},{28,20},{32,40},... | collective-permute-start | bytes 147464 | tf_op jit(solution)/shard_map/ppermute | solution.py:34
  60.5 5.6 %collective-permute-start.7 = (bf16[16,512]{1,0:T(8,128)(2,1)S(1)}, bf16[16,512]{1,0:T(8,128)(2,1)S(1)}, u32[]{:S(2)}, u32[]{:S(2)}) collective-permute-start(bf16[16,512]{1,0:T(8,128)(2,1)S(1)} %get-tuple-element.65), channel_id=1, source_target_pairs={{0,1},{1,0},{2,3},{3,2},{4,5},{5,4},{6,7},{7,6},{8,9},{9,8},{10,11... | collective-permute-start | bytes 49160 | tf_op jit(solution)/shard_map/ppermute | solution.py:34
  62.4 3.7 %copy-start.3 = (bf16[64,64]{1,0:T(8,128)(2,1)S(1)}, bf16[64,64]{1,0:T(8,128)(2,1)}, u32[]{:S(2)}) copy-start(bf16[64,64]{1,0:T(8,128)(2,1)} %inverse.1) | copy-start | bytes 24580

commit v8 on v6

--- a/solution.py
+++ b/solution.py
@@ -83,7 +83,7 @@
 def first_kernel(*refs):
     sources, (message, wide_ref), targets, (ints, arrived) = refs[:13], refs[13:15], refs[15:28], refs[28:]
     copies = [pltpu.make_async_copy(a, b, arrived.at[i]) for i, (a, b) in enumerate(zip(sources, targets))]
-    for copy in copies:
+    for copy in copies[8:10] + copies[:8] + copies[10:]:
         copy.start()
     near, far, sub, elem_type, face_type, neighbours, pair, partner, guess, rhs, diag, face, smooth = targets
     for copy in copies[:8]:
@@ -98,16 +98,16 @@
     ints[21:22, :PAIRS] = pair[...].astype(F32)
     ints[22:23, :] = partner[...].astype(F32)
     message[2 * ROWS :, :] = ints[...].astype(BF)
-    for i, field in enumerate((guess, rhs)):
-        copies[8 + i].wait()
-        blocks = [field[pl.ds(r, DOF, stride=RHS), :].astype(BF) for r in range(RHS)]
-        message[i * ROWS : (i + 1) * ROWS, :] = jnp.concatenate(blocks, axis=0)
     for copy in copies[10:]:
         copy.wait()
     for d in range(FACES + 1):
         both = (diag[0], diag[1]) if d == 0 else (face[d - 1, 0], face[d - 1, 1])
         wide_ref[:, d * 2 * DOF : (d + 1) * 2 * DOF] = jnp.concatenate(both, axis=1)
     wide_ref[:, WIDE:] = jnp.concatenate([smooth[0], smooth[1]], axis=1)
+    for i, field in enumerate((guess, rhs)):
+        copies[8 + i].wait()
+        blocks = [field[pl.ds(r, DOF, stride=RHS), :].astype(BF) for r in range(RHS)]
+        message[i * ROWS : (i + 1) * ROWS, :] = jnp.concatenate(blocks, axis=0)
 
 
 def tables(lists, core, odd, local_ref, halo_ref, mask_ref):
@@ -402,7 +402,7 @@
     return (solved.reshape(shape), residual.reshape(shape))
 
 
-SENT = (SIDE + 16, SIDE + 16, SIDE)
+SENT = (SIDE, SIDE, SIDE)
 
 
 def solution(mesh):

time: 67.9 us -> 68 us (level)
  no operation moved by 1% of the time
where the time goes in v8:
time: 68 us; the launch traced here: 67.5 us
  starting transfers between devices  26.8 us (39%)
  blocking collectives  25.7 us (38%)
  Pallas kernels  10.8 us (16%)
  waiting for transfers between devices  2.32 us (3%)
  local copies, waits for them, and re-layouts  0.98 us (1%)
  between operations  0.83 us (1%)
    ppermute x8, starting transfers between devices, swap(): return lax.ppermute(array, axis, route)  26.8 us
    all_to_all x3, blocking collectives, exchange(): side = lax.all_to_all(side, 'sub', 0, 0, tiled=True)  25.7 us
    pallas_call x8, Pallas kernels, call(): pl.pallas_call(kernel, out_shape=[jax.ShapeDtypeStruct(s, d) for s, d in...  10.8 us
    ppermute x8, waiting for transfers between devices, swap(): return lax.ppermute(array, axis, route)  2.32 us
  transfers between devices with their start and end apart: 8, of which 1 were waited for; matrix products, arithmetic and copies ran while one was open for 0% of the time, Pallas kernels for 2%

profile of v8, /device:TPU:240, one launch (start us, length us, event | category | flops | bytes accessed | tf_op | source)
XLA Modules:
  0.0 67.5 jit_solution(294705975324918153)
XLA Ops:
  0.6 2.2 %shard_map.149 = (bf16[1056,128]{1,0:T(8,128)(2,1)}, bf16[64,1024]{1,0:T(8,128)(2,1)}) custom-call(s32[2,32]{1,0:T(2,128)} %refs_0_.1, s32[2,8]{1,0:T(2,128)} %refs_1_.1, s32[1,8]{1,0:T(1,128)} %bitcast.29, s32[1,128]{1,0:T(1,128)} %bitcast.30, s32[6,128]{1,0:T(8,128)} %refs_4_.1, s32[6,128]{1,0:T(8,128)} %refs_5_.1, s32[1,16]{1,0:T(1,128)} %bitcast.31, ...), custom_call_target="tpu_custom_call" | custom-call | bytes 662944 | tf_op jit(solution)/shard_map/pallas_call | solution.py:46
  2.9 1.9 %collective-permute-start = (bf16[1056,128]{1,0:T(8,128)(2,1)}, bf16[1056,128]{1,0:T(8,128)(2,1)S(1)}, u32[]{:S(2)}, u32[]{:S(2)}) collective-permute-start(bf16[1056,128]{1,0:T(8,128)(2,1)} %get-tuple-element.35.mine), channel_id=1, source_target_pairs={{0,4},{4,0},{8,12},{12,8},{16,20},{20,16},{24,28},{28,24},{32,36},... | collective-permute-start | bytes 811016 | tf_op jit(solution)/shard_map/ppermute | solution.py:34
  4.8 0.1 pad_add_fusion.place_ref
  4.9 0.0 copy-start
  4.9 1.0 %copy-done = bf16[1056,128]{1,0:T(8,128)(2,1)S(1)} copy-done((bf16[1056,128]{1,0:T(8,128)(2,1)S(1)}, bf16[1056,128]{1,0:T(8,128)(2,1)}, u32[]{:S(2)}) %copy-start) | copy-done | bytes 270360
  5.8 0.0 copy-start.4
  5.9 0.7 shard_map.150
  6.5 0.0 collective-permute-done.other.refs_10_
  6.5 0.0 copy-start.1
  6.5 0.0 copy-start.2
  6.5 1.0 %shard_map.151 = (bf16[512,256]{1,0:T(8,128)(2,1)S(1)}, bf16[160,256]{1,0:T(8,128)(2,1)S(1)}, bf16[128,768]{1,0:T(8,128)(2,1)S(1)}, bf16[128,768]{1,0:T(8,128)(2...) custom-call(s32[2]{0:T(128)S(1)} %pad_add_fusion.place_ref, ...), custom_call_target="tpu_custom_call" | custom-call | flops 41943040 | bytes 466952 | tf_op jit(solution)/shard_map/pallas_call | solution.py:46
  7.5 3.3 %collective-permute-start.1 = (bf16[64,512]{1,0:T(8,128)(2,1)S(1)}, bf16[64,512]{1,0:T(8,128)(2,1)S(1)}, u32[]{:S(2)}, u32[]{:S(2)}) collective-permute-start(bf16[64,512]{1,0:T(8,128)(2,1)S(1)} %get-tuple-element.40), channel_id=1, source_target_pairs={{8,16},{16,8},{12,20},{20,12},{24,32},{32,24},{28,36},{36,28},{40,... | collective-permute-start | bytes 196616 | tf_op jit(solution)/shard_map/ppermute | solution.py:34
  10.8 4.0 %collective-permute-start.2 = (bf16[64,512]{1,0:T(8,128)(2,1)S(1)}, bf16[64,512]{1,0:T(8,128)(2,1)S(1)}, u32[]{:S(2)}, u32[]{:S(2)}) collective-permute-start(bf16[64,512]{1,0:T(8,128)(2,1)S(1)} %get-tuple-element.41), channel_id=1, source_target_pairs={{0,8},{8,0},{4,12},{12,4},{16,24},{24,16},{20,28},{28,20},{32,40},... | collective-permute-start | bytes 196616 | tf_op jit(solution)/shard_map/ppermute | solution.py:34
  14.8 9.7 %all_to_all.33 = bf16[4,16,512]{2,1,0:T(8,128)(2,1)S(1)} all-to-all(bf16[4,16,512]{2,1,0:T(8,128)(2,1)S(1)} %bitcast.24), channel_id=1, replica_groups=mesh['dom'=128,'sub'=4] {'sub'}, dimensions={0} | all-to-all | bytes 131072 | tf_op jit(solution)/shard_map/all_to_all | solution.py:305
  24.5 0.0 collective-permute-done.1.two
  24.5 0.0 collective-permute-done.2.one
  24.5 0.0 copy-done.4
  24.5 0.0 copy-done.1
  24.6 0.0 copy-done.2
  24.6 2.0 %shard_map.152 = (f32[512,256]{1,0:T(8,128)S(1)}, bf16[512,256]{1,0:T(8,128)(2,1)S(1)}, bf16[64,512]{1,0:T(8,128)(2,1)S(1)}, bf16[64,512]{1,0:T(8,128)(2,1)S(1)}, bf16[64,512]{1,0:T(8,128)(2,1)S(1)}) custom-call(bf16[512,256]{1,0:T(8,128)(2,1)S(1)} %get-tuple-element.39.field_ref, bf16[64,512]{1,0:T(8,128)(2,1)S(1)} %collective-permute-done.1.two, ...), custom_call_target="tpu_custom_call" | custom-call | flops 889192448 | bytes 2859008 | tf_op jit(solution)/shard_map/pallas_call | solution.py:46
  26.5 1.9 %collective-permute-start.3 = (bf16[64,512]{1,0:T(8,128)(2,1)S(1)}, bf16[64,512]{1,0:T(8,128)(2,1)S(1)}, u32[]{:S(2)}, u32[]{:S(2)}) collective-permute-start(bf16[64,512]{1,0:T(8,128)(2,1)S(1)} %get-tuple-element.54), channel_id=1, source_target_pairs={{8,16},{16,8},{12,20},{20,12},{24,32},{32,24},{28,36},{36,28},{40,... | collective-permute-start | bytes 196616 | tf_op jit(solution)/shard_map/ppermute | solution.py:34
  28.5 5.0 %collective-permute-start.4 = (bf16[64,512]{1,0:T(8,128)(2,1)S(1)}, bf16[64,512]{1,0:T(8,128)(2,1)S(1)}, u32[]{:S(2)}, u32[]{:S(2)}) collective-permute-start(bf16[64,512]{1,0:T(8,128)(2,1)S(1)} %get-tuple-element.55), channel_id=1, source_target_pairs={{0,8},{8,0},{4,12},{12,4},{16,24},{24,16},{20,28},{28,20},{32,40},... | collective-permute-start | bytes 196616 | tf_op jit(solution)/shard_map/ppermute | solution.py:34
  33.5 8.0 %all_to_all.34 = bf16[4,16,512]{2,1,0:T(8,128)(2,1)S(1)} all-to-all(bf16[4,16,512]{2,1,0:T(8,128)(2,1)S(1)} %bitcast.27), channel_id=1, replica_groups=mesh['dom'=128,'sub'=4] {'sub'}, dimensions={0} | all-to-all | bytes 131072 | tf_op jit(solution)/shard_map/all_to_all | solution.py:305
  41.5 0.0 collective-permute-done.3.two
  41.5 0.0 collective-permute-done.4.one
  41.5 1.9 %shard_map.153 = (f32[512,256]{1,0:T(8,128)S(1)}, bf16[512,256]{1,0:T(8,128)(2,1)S(1)}, bf16[64,512]{1,0:T(8,128)(2,1)S(1)}, bf16[64,512]{1,0:T(8,128)(2,1)S(1)}, bf16[64,512]{1,0:T(8,128)(2,1)S(1)}) custom-call(bf16[512,256]{1,0:T(8,128)(2,1)S(1)} %get-tuple-element.53.field_ref, bf16[64,512]{1,0:T(8,128)(2,1)S(1)} %collective-permute-done.3.two, ...), custom_call_target="tpu_custom_call" | custom-call | flops 889192448 | bytes 3121152 | tf_op jit(solution)/shard_map/pallas_call | solution.py:46
  43.5 1.9 %collective-permute-start.5 = (bf16[64,512]{1,0:T(8,128)(2,1)S(1)}, bf16[64,512]{1,0:T(8,128)(2,1)S(1)}, u32[]{:S(2)}, u32[]{:S(2)}) collective-permute-start(bf16[64,512]{1,0:T(8,128)(2,1)S(1)} %get-tuple-element.59), channel_id=1, source_target_pairs={{8,16},{16,8},{12,20},{20,12},{24,32},{32,24},{28,36},{36,28},{40,... | collective-permute-start | bytes 196616 | tf_op jit(solution)/shard_map/ppermute | solution.py:34
  45.4 6.3 %collective-permute-start.6 = (bf16[64,512]{1,0:T(8,128)(2,1)S(1)}, bf16[64,512]{1,0:T(8,128)(2,1)S(1)}, u32[]{:S(2)}, u32[]{:S(2)}) collective-permute-start(bf16[64,512]{1,0:T(8,128)(2,1)S(1)} %get-tuple-element.60), channel_id=1, source_target_pairs={{0,8},{8,0},{4,12},{12,4},{16,24},{24,16},{20,28},{28,20},{32,40},... | collective-permute-start | bytes 196616 | tf_op jit(solution)/shard_map/ppermute | solution.py:34
  51.7 8.0 %all_to_all.35 = bf16[4,16,512]{2,1,0:T(8,128)(2,1)S(1)} all-to-all(bf16[4,16,512]{2,1,0:T(8,128)(2,1)S(1)} %bitcast.23), channel_id=1, replica_groups=mesh['dom'=128,'sub'=4] {'sub'}, dimensions={0} | all-to-all | bytes 131072 | tf_op jit(solution)/shard_map/all_to_all | solution.py:305
  59.6 0.0 collective-permute-done.5.two
  59.6 0.0 collective-permute-done.6.one
  59.7 1.2 %shard_map.154 = (f32[512,128]{1,0:T(8,128)S(1)}, bf16[512,128]{1,0:T(8,128)(2,1)S(1)}, bf16[16,512]{1,0:T(8,128)(2,1)S(1)}) custom-call(bf16[512,256]{1,0:T(8,128)(2,1)S(1)} %get-tuple-element.58.field_ref, bf16[64,512]{1,0:T(8,128)(2,1)S(1)} %collective-permute-done.5.two, bf16[64,512]{1,0:T(8,128)(2,1)S(1)} %collective-permute-done.6.one, ...), custom_call_target="tpu_custom_call" | custom-call | flops 444596224 | bytes 1564672 | tf_op jit(solution)/shard_map/pallas_call | solution.py:46
  60.8 2.5 %collective-permute-start.7 = (bf16[16,512]{1,0:T(8,128)(2,1)S(1)}, bf16[16,512]{1,0:T(8,128)(2,1)S(1)}, u32[]{:S(2)}, u32[]{:S(2)}) collective-permute-start(bf16[16,512]{1,0:T(8,128)(2,1)S(1)} %get-tuple-element.65), channel_id=1, source_target_pairs={{0,1},{1,0},{2,3},{3,2},{4,5},{5,4},{6,7},{7,6},{8,9},{9,8},{10,11... | collective-permute-start | bytes 49160 | tf_op jit(solution)/shard_map/ppermute | solution.py:34
  63.3 0.0 copy-start.3
  63.3 0.8 %shard_map.155 = (f32[512,128]{1,0:T(8,128)}, f32[512,128]{1,0:T(8,128)S(1)}) custom-call(f32[512,128]{1,0:T(8,128)S(1)} %get-tuple-element.62.residual_ref, bf16[512,128]{1,0:T(8,128)(2,1)S(1)} %get-tuple-element.63.rounded_ref, s32[32,128]{1,0:T(8,128)S(1)} %get-tuple-element.37.own_lists.lists), custom_call_target="tpu_custom_call" | custom-call | flops 111149056 | bytes 409600 | tf_op jit(solution)/shard_map/pallas_call | solution.py:46
  64.2 2.3 %collective-permute-done.7.incoming = bf16[16,512]{1,0:T(8,128)(2,1)S(1)} collective-permute-done((bf16[16,512]{1,0:T(8,128)(2,1)S(1)}, bf16[16,512]{1,0:T(8,128)(2,1)S(1)}, u32[]{:S(2)}, u32[]{:S(2)}) %collective-permute-start.7) | collective-permute-done | bytes 16416 | tf_op jit(solution)/shard_map/ppermute | solution.py:34
  66.5 0.0 copy-done.3
  66.5 1.1 %shard_map.156 = f32[512,128]{1,0:T(8,128)} custom-call(f32[512,128]{1,0:T(8,128)S(1)} %get-tuple-element.64.half_ref, bf16[16,512]{1,0:T(8,128)(2,1)S(1)} %collective-permute-done.7.incoming, s32[32,128]{1,0:T(8,128)S(1)} %get-tuple-element.37.own_lists.lists, bf16[64,64]{1,0:T(8,128)(2,1)S(1)} %copy-done.3, f32[512,256]{1,0:T(8,128)S(1)} %get-tuple-element.66.iterate), custom_call_target="tpu_custom_call" | custom-call | flops 111149056 | bytes 827392 | tf_op jit(solution)/shard_map/pallas_call | solution.py:46
Async XLA Ops:
  2.9 3.7 %collective-permute-start = (bf16[1056,128]{1,0:T(8,128)(2,1)}, bf16[1056,128]{1,0:T(8,128)(2,1)S(1)}, u32[]{:S(2)}, u32[]{:S(2)}) collective-permute-start(bf16[1056,128]{1,0:T(8,128)(2,1)} %get-tuple-element.35.mine), channel_id=1, source_target_pairs={{0,4},{4,0},{8,12},{12,8},{16,20},{20,16},{24,28},{28,24},{32,36},... | collective-permute-start | bytes 811016 | tf_op jit(solution)/shard_map/ppermute | solution.py:34
  4.9 1.0 %copy-start = (bf16[1056,128]{1,0:T(8,128)(2,1)S(1)}, bf16[1056,128]{1,0:T(8,128)(2,1)}, u32[]{:S(2)}) copy-start(bf16[1056,128]{1,0:T(8,128)(2,1)} %get-tuple-element.35.mine) | copy-start | bytes 811012
  5.8 18.7 %copy-start.4 = (bf16[64,1024]{1,0:T(8,128)(2,1)S(1)}, bf16[64,1024]{1,0:T(8,128)(2,1)}, u32[]{:S(2)}) copy-start(bf16[64,1024]{1,0:T(8,128)(2,1)} %get-tuple-element.51.refs_8_.wide) | copy-start | bytes 393220
  6.5 18.0 %copy-start.1 = (f32[64,8,128]{2,1,0:T(8,128)S(1)}, f32[64,8,128]{2,1,0:T(8,128)}, u32[]{:S(2)}) copy-start(f32[64,8,128]{2,1,0:T(8,128)} %param.15) | copy-start | bytes 786436
  6.5 18.0 %copy-start.2 = (f32[64,8,128]{2,1,0:T(8,128)S(1)}, f32[64,8,128]{2,1,0:T(8,128)}, u32[]{:S(2)}) copy-start(f32[64,8,128]{2,1,0:T(8,128)} %param.14) | copy-start | bytes 786436
  7.5 17.0 %collective-permute-start.1 = (bf16[64,512]{1,0:T(8,128)(2,1)S(1)}, bf16[64,512]{1,0:T(8,128)(2,1)S(1)}, u32[]{:S(2)}, u32[]{:S(2)}) collective-permute-start(bf16[64,512]{1,0:T(8,128)(2,1)S(1)} %get-tuple-element.40), channel_id=1, source_target_pairs={{8,16},{16,8},{12,20},{20,12},{24,32},{32,24},{28,36},{36,28},{40,... | collective-permute-start | bytes 196616 | tf_op jit(solution)/shard_map/ppermute | solution.py:34
  10.8 13.8 %collective-permute-start.2 = (bf16[64,512]{1,0:T(8,128)(2,1)S(1)}, bf16[64,512]{1,0:T(8,128)(2,1)S(1)}, u32[]{:S(2)}, u32[]{:S(2)}) collective-permute-start(bf16[64,512]{1,0:T(8,128)(2,1)S(1)} %get-tuple-element.41), channel_id=1, source_target_pairs={{0,8},{8,0},{4,12},{12,4},{16,24},{24,16},{20,28},{28,20},{32,40},... | collective-permute-start | bytes 196616 | tf_op jit(solution)/shard_map/ppermute | solution.py:34
  26.5 15.0 %collective-permute-start.3 = (bf16[64,512]{1,0:T(8,128)(2,1)S(1)}, bf16[64,512]{1,0:T(8,128)(2,1)S(1)}, u32[]{:S(2)}, u32[]{:S(2)}) collective-permute-start(bf16[64,512]{1,0:T(8,128)(2,1)S(1)} %get-tuple-element.54), channel_id=1, source_target_pairs={{8,16},{16,8},{12,20},{20,12},{24,32},{32,24},{28,36},{36,28},{40,... | collective-permute-start | bytes 196616 | tf_op jit(solution)/shard_map/ppermute | solution.py:34
  28.5 13.0 %collective-permute-start.4 = (bf16[64,512]{1,0:T(8,128)(2,1)S(1)}, bf16[64,512]{1,0:T(8,128)(2,1)S(1)}, u32[]{:S(2)}, u32[]{:S(2)}) collective-permute-start(bf16[64,512]{1,0:T(8,128)(2,1)S(1)} %get-tuple-element.55), channel_id=1, source_target_pairs={{0,8},{8,0},{4,12},{12,4},{16,24},{24,16},{20,28},{28,20},{32,40},... | collective-permute-start | bytes 196616 | tf_op jit(solution)/shard_map/ppermute | solution.py:34
  43.5 16.2 %collective-permute-start.5 = (bf16[64,512]{1,0:T(8,128)(2,1)S(1)}, bf16[64,512]{1,0:T(8,128)(2,1)S(1)}, u32[]{:S(2)}, u32[]{:S(2)}) collective-permute-start(bf16[64,512]{1,0:T(8,128)(2,1)S(1)} %get-tuple-element.59), channel_id=1, source_target_pairs={{8,16},{16,8},{12,20},{20,12},{24,32},{32,24},{28,36},{36,28},{40,... | collective-permute-start | bytes 196616 | tf_op jit(solution)/shard_map/ppermute | solution.py:34
  45.4 14.3 %collective-permute-start.6 = (bf16[64,512]{1,0:T(8,128)(2,1)S(1)}, bf16[64,512]{1,0:T(8,128)(2,1)S(1)}, u32[]{:S(2)}, u32[]{:S(2)}) collective-permute-start(bf16[64,512]{1,0:T(8,128)(2,1)S(1)} %get-tuple-element.60), channel_id=1, source_target_pairs={{0,8},{8,0},{4,12},{12,4},{16,24},{24,16},{20,28},{28,20},{32,40},... | collective-permute-start | bytes 196616 | tf_op jit(solution)/shard_map/ppermute | solution.py:34
  60.8 5.6 %collective-permute-start.7 = (bf16[16,512]{1,0:T(8,128)(2,1)S(1)}, bf16[16,512]{1,0:T(8,128)(2,1)S(1)}, u32[]{:S(2)}, u32[]{:S(2)}) collective-permute-start(bf16[16,512]{1,0:T(8,128)(2,1)S(1)} %get-tuple-element.65), channel_id=1, source_target_pairs={{0,1},{1,0},{2,3},{3,2},{4,5},{5,4},{6,7},{7,6},{8,9},{9,8},{10,11... | collective-permute-start | bytes 49160 | tf_op jit(solution)/shard_map/ppermute | solution.py:34
  63.3 3.2 %copy-start.3 = (bf16[64,64]{1,0:T(8,128)(2,1)S(1)}, bf16[64,64]{1,0:T(8,128)(2,1)}, u32[]{:S(2)}) copy-start(bf16[64,64]{1,0:T(8,128)(2,1)} %inverse.1) | copy-start | bytes 24580

commit v9 on v6

--- a/solution.py
+++ b/solution.py
@@ -83,7 +83,7 @@
 def first_kernel(*refs):
     sources, (message, wide_ref), targets, (ints, arrived) = refs[:13], refs[13:15], refs[15:28], refs[28:]
     copies = [pltpu.make_async_copy(a, b, arrived.at[i]) for i, (a, b) in enumerate(zip(sources, targets))]
-    for copy in copies:
+    for copy in copies[8:10] + copies[:8] + copies[10:]:
         copy.start()
     near, far, sub, elem_type, face_type, neighbours, pair, partner, guess, rhs, diag, face, smooth = targets
     for copy in copies[:8]:

time: 67.9 us -> 67.9 us (level)
  no operation moved by 1% of the time
where the time goes in v9:
time: 67.9 us; the launch traced here: 67.4 us
  starting transfers between devices  26.8 us (39%)
  blocking collectives  25.7 us (38%)
  Pallas kernels  10.7 us (16%)
  waiting for transfers between devices  2.31 us (3%)
  local copies, waits for them, and re-layouts  0.98 us (1%)
  between operations  0.83 us (1%)
    ppermute x8, starting transfers between devices, swap(): return lax.ppermute(array, axis, route)  26.8 us
    all_to_all x3, blocking collectives, exchange(): side = lax.all_to_all(side, 'sub', 0, 0, tiled=True)  25.7 us
    pallas_call x8, Pallas kernels, call(): pl.pallas_call(kernel, out_shape=[jax.ShapeDtypeStruct(s, d) for s, d in...  10.7 us
    ppermute x8, waiting for transfers between devices, swap(): return lax.ppermute(array, axis, route)  2.31 us
  transfers between devices with their start and end apart: 8, of which 1 were waited for; matrix products, arithmetic and copies ran while one was open for 0% of the time, Pallas kernels for 2%

profile of v9, /device:TPU:240, one launch (start us, length us, event | category | flops | bytes accessed | tf_op | source)
XLA Modules:
  0.0 67.4 jit_solution(10456272688952271708)
XLA Ops:
  0.6 2.1 %shard_map.149 = (bf16[1056,128]{1,0:T(8,128)(2,1)}, bf16[64,1024]{1,0:T(8,128)(2,1)}) custom-call(s32[2,32]{1,0:T(2,128)} %refs_0_.1, s32[2,8]{1,0:T(2,128)} %refs_1_.1, s32[1,8]{1,0:T(1,128)} %bitcast.29, s32[1,128]{1,0:T(1,128)} %bitcast.30, s32[6,128]{1,0:T(8,128)} %refs_4_.1, s32[6,128]{1,0:T(8,128)} %refs_5_.1, s32[1,16]{1,0:T(1,128)} %bitcast.31, ...), custom_call_target="tpu_custom_call" | custom-call | bytes 662944 | tf_op jit(solution)/shard_map/pallas_call | solution.py:46
  2.7 1.9 %collective-permute-start = (bf16[1056,128]{1,0:T(8,128)(2,1)}, bf16[1056,128]{1,0:T(8,128)(2,1)S(1)}, u32[]{:S(2)}, u32[]{:S(2)}) collective-permute-start(bf16[1056,128]{1,0:T(8,128)(2,1)} %get-tuple-element.35.mine), channel_id=1, source_target_pairs={{0,4},{4,0},{8,12},{12,8},{16,20},{20,16},{24,28},{28,24},{32,36},... | collective-permute-start | bytes 811016 | tf_op jit(solution)/shard_map/ppermute | solution.py:34
  4.7 0.1 pad_add_fusion.place_ref
  4.8 0.0 copy-start
  4.8 1.0 %copy-done = bf16[1056,128]{1,0:T(8,128)(2,1)S(1)} copy-done((bf16[1056,128]{1,0:T(8,128)(2,1)S(1)}, bf16[1056,128]{1,0:T(8,128)(2,1)}, u32[]{:S(2)}) %copy-start) | copy-done | bytes 270360
  5.7 0.0 copy-start.4
  5.7 0.7 shard_map.150
  6.4 0.0 collective-permute-done.other.refs_10_
  6.4 0.0 copy-start.1
  6.4 0.0 copy-start.2
  6.4 1.0 %shard_map.151 = (bf16[512,256]{1,0:T(8,128)(2,1)S(1)}, bf16[160,256]{1,0:T(8,128)(2,1)S(1)}, bf16[128,768]{1,0:T(8,128)(2,1)S(1)}, bf16[128,768]{1,0:T(8,128)(2...) custom-call(s32[2]{0:T(128)S(1)} %pad_add_fusion.place_ref, ...), custom_call_target="tpu_custom_call" | custom-call | flops 41943040 | bytes 466952 | tf_op jit(solution)/shard_map/pallas_call | solution.py:46
  7.4 3.3 %collective-permute-start.1 = (bf16[80,512]{1,0:T(8,128)(2,1)S(1)}, bf16[80,512]{1,0:T(8,128)(2,1)S(1)}, u32[]{:S(2)}, u32[]{:S(2)}) collective-permute-start(bf16[80,512]{1,0:T(8,128)(2,1)S(1)} %get-tuple-element.40), channel_id=1, source_target_pairs={{8,16},{16,8},{12,20},{20,12},{24,32},{32,24},{28,36},{36,28},{40,... | collective-permute-start | bytes 245768 | tf_op jit(solution)/shard_map/ppermute | solution.py:34
  10.6 4.0 %collective-permute-start.2 = (bf16[80,512]{1,0:T(8,128)(2,1)S(1)}, bf16[80,512]{1,0:T(8,128)(2,1)S(1)}, u32[]{:S(2)}, u32[]{:S(2)}) collective-permute-start(bf16[80,512]{1,0:T(8,128)(2,1)S(1)} %get-tuple-element.41), channel_id=1, source_target_pairs={{0,8},{8,0},{4,12},{12,4},{16,24},{24,16},{20,28},{28,20},{32,40},... | collective-permute-start | bytes 245768 | tf_op jit(solution)/shard_map/ppermute | solution.py:34
  14.7 9.7 %all_to_all.33 = bf16[4,16,512]{2,1,0:T(8,128)(2,1)S(1)} all-to-all(bf16[4,16,512]{2,1,0:T(8,128)(2,1)S(1)} %bitcast.24), channel_id=1, replica_groups=mesh['dom'=128,'sub'=4] {'sub'}, dimensions={0} | all-to-all | bytes 131072 | tf_op jit(solution)/shard_map/all_to_all | solution.py:305
  24.4 0.0 collective-permute-done.1.two
  24.4 0.0 collective-permute-done.2.one
  24.4 0.0 copy-done.4
  24.4 0.0 copy-done.1
  24.4 0.0 copy-done.2
  24.4 1.9 %shard_map.152 = (f32[512,256]{1,0:T(8,128)S(1)}, bf16[512,256]{1,0:T(8,128)(2,1)S(1)}, bf16[80,512]{1,0:T(8,128)(2,1)S(1)}, bf16[80,512]{1,0:T(8,128)(2,1)S(1)}, bf16[64,512]{1,0:T(8,128)(2,1)S(1)}) custom-call(bf16[512,256]{1,0:T(8,128)(2,1)S(1)} %get-tuple-element.39.field_ref, bf16[80,512]{1,0:T(8,128)(2,1)S(1)} %collective-permute-done.1.two, ...), custom_call_target="tpu_custom_call" | custom-call | flops 889192448 | bytes 2891776 | tf_op jit(solution)/shard_map/pallas_call | solution.py:46
  26.4 1.9 %collective-permute-start.3 = (bf16[80,512]{1,0:T(8,128)(2,1)S(1)}, bf16[80,512]{1,0:T(8,128)(2,1)S(1)}, u32[]{:S(2)}, u32[]{:S(2)}) collective-permute-start(bf16[80,512]{1,0:T(8,128)(2,1)S(1)} %get-tuple-element.54), channel_id=1, source_target_pairs={{8,16},{16,8},{12,20},{20,12},{24,32},{32,24},{28,36},{36,28},{40,... | collective-permute-start | bytes 245768 | tf_op jit(solution)/shard_map/ppermute | solution.py:34
  28.3 5.0 %collective-permute-start.4 = (bf16[80,512]{1,0:T(8,128)(2,1)S(1)}, bf16[80,512]{1,0:T(8,128)(2,1)S(1)}, u32[]{:S(2)}, u32[]{:S(2)}) collective-permute-start(bf16[80,512]{1,0:T(8,128)(2,1)S(1)} %get-tuple-element.55), channel_id=1, source_target_pairs={{0,8},{8,0},{4,12},{12,4},{16,24},{24,16},{20,28},{28,20},{32,40},... | collective-permute-start | bytes 245768 | tf_op jit(solution)/shard_map/ppermute | solution.py:34
  33.4 8.0 %all_to_all.34 = bf16[4,16,512]{2,1,0:T(8,128)(2,1)S(1)} all-to-all(bf16[4,16,512]{2,1,0:T(8,128)(2,1)S(1)} %bitcast.27), channel_id=1, replica_groups=mesh['dom'=128,'sub'=4] {'sub'}, dimensions={0} | all-to-all | bytes 131072 | tf_op jit(solution)/shard_map/all_to_all | solution.py:305
  41.4 0.0 collective-permute-done.3.two
  41.4 0.0 collective-permute-done.4.one
  41.4 1.9 %shard_map.153 = (f32[512,256]{1,0:T(8,128)S(1)}, bf16[512,256]{1,0:T(8,128)(2,1)S(1)}, bf16[80,512]{1,0:T(8,128)(2,1)S(1)}, bf16[80,512]{1,0:T(8,128)(2,1)S(1)}, bf16[64,512]{1,0:T(8,128)(2,1)S(1)}) custom-call(bf16[512,256]{1,0:T(8,128)(2,1)S(1)} %get-tuple-element.53.field_ref, bf16[80,512]{1,0:T(8,128)(2,1)S(1)} %collective-permute-done.3.two, ...), custom_call_target="tpu_custom_call" | custom-call | flops 889192448 | bytes 3153920 | tf_op jit(solution)/shard_map/pallas_call | solution.py:46
  43.3 1.9 %collective-permute-start.5 = (bf16[80,512]{1,0:T(8,128)(2,1)S(1)}, bf16[80,512]{1,0:T(8,128)(2,1)S(1)}, u32[]{:S(2)}, u32[]{:S(2)}) collective-permute-start(bf16[80,512]{1,0:T(8,128)(2,1)S(1)} %get-tuple-element.59), channel_id=1, source_target_pairs={{8,16},{16,8},{12,20},{20,12},{24,32},{32,24},{28,36},{36,28},{40,... | collective-permute-start | bytes 245768 | tf_op jit(solution)/shard_map/ppermute | solution.py:34
  45.2 6.3 %collective-permute-start.6 = (bf16[80,512]{1,0:T(8,128)(2,1)S(1)}, bf16[80,512]{1,0:T(8,128)(2,1)S(1)}, u32[]{:S(2)}, u32[]{:S(2)}) collective-permute-start(bf16[80,512]{1,0:T(8,128)(2,1)S(1)} %get-tuple-element.60), channel_id=1, source_target_pairs={{0,8},{8,0},{4,12},{12,4},{16,24},{24,16},{20,28},{28,20},{32,40},... | collective-permute-start | bytes 245768 | tf_op jit(solution)/shard_map/ppermute | solution.py:34
  51.5 8.0 %all_to_all.35 = bf16[4,16,512]{2,1,0:T(8,128)(2,1)S(1)} all-to-all(bf16[4,16,512]{2,1,0:T(8,128)(2,1)S(1)} %bitcast.23), channel_id=1, replica_groups=mesh['dom'=128,'sub'=4] {'sub'}, dimensions={0} | all-to-all | bytes 131072 | tf_op jit(solution)/shard_map/all_to_all | solution.py:305
  59.5 0.0 collective-permute-done.5.two
  59.5 0.0 collective-permute-done.6.one
  59.5 1.2 %shard_map.154 = (f32[512,128]{1,0:T(8,128)S(1)}, bf16[512,128]{1,0:T(8,128)(2,1)S(1)}, bf16[16,512]{1,0:T(8,128)(2,1)S(1)}) custom-call(bf16[512,256]{1,0:T(8,128)(2,1)S(1)} %get-tuple-element.58.field_ref, bf16[80,512]{1,0:T(8,128)(2,1)S(1)} %collective-permute-done.5.two, bf16[80,512]{1,0:T(8,128)(2,1)S(1)} %collective-permute-done.6.one, ...), custom_call_target="tpu_custom_call" | custom-call | flops 444596224 | bytes 1597440 | tf_op jit(solution)/shard_map/pallas_call | solution.py:46
  60.7 2.5 %collective-permute-start.7 = (bf16[16,512]{1,0:T(8,128)(2,1)S(1)}, bf16[16,512]{1,0:T(8,128)(2,1)S(1)}, u32[]{:S(2)}, u32[]{:S(2)}) collective-permute-start(bf16[16,512]{1,0:T(8,128)(2,1)S(1)} %get-tuple-element.65), channel_id=1, source_target_pairs={{0,1},{1,0},{2,3},{3,2},{4,5},{5,4},{6,7},{7,6},{8,9},{9,8},{10,11... | collective-permute-start | bytes 49160 | tf_op jit(solution)/shard_map/ppermute | solution.py:34
  63.2 0.0 copy-start.3
  63.2 0.8 %shard_map.155 = (f32[512,128]{1,0:T(8,128)}, f32[512,128]{1,0:T(8,128)S(1)}) custom-call(f32[512,128]{1,0:T(8,128)S(1)} %get-tuple-element.62.residual_ref, bf16[512,128]{1,0:T(8,128)(2,1)S(1)} %get-tuple-element.63.rounded_ref, s32[32,128]{1,0:T(8,128)S(1)} %get-tuple-element.37.own_lists.lists), custom_call_target="tpu_custom_call" | custom-call | flops 111149056 | bytes 409600 | tf_op jit(solution)/shard_map/pallas_call | solution.py:46
  64.0 2.3 %collective-permute-done.7.incoming = bf16[16,512]{1,0:T(8,128)(2,1)S(1)} collective-permute-done((bf16[16,512]{1,0:T(8,128)(2,1)S(1)}, bf16[16,512]{1,0:T(8,128)(2,1)S(1)}, u32[]{:S(2)}, u32[]{:S(2)}) %collective-permute-start.7) | collective-permute-done | bytes 16416 | tf_op jit(solution)/shard_map/ppermute | solution.py:34
  66.3 0.0 copy-done.3
  66.3 1.1 %shard_map.156 = f32[512,128]{1,0:T(8,128)} custom-call(f32[512,128]{1,0:T(8,128)S(1)} %get-tuple-element.64.half_ref, bf16[16,512]{1,0:T(8,128)(2,1)S(1)} %collective-permute-done.7.incoming, s32[32,128]{1,0:T(8,128)S(1)} %get-tuple-element.37.own_lists.lists, bf16[64,64]{1,0:T(8,128)(2,1)S(1)} %copy-done.3, f32[512,256]{1,0:T(8,128)S(1)} %get-tuple-element.66.iterate), custom_call_target="tpu_custom_call" | custom-call | flops 111149056 | bytes 827392 | tf_op jit(solution)/shard_map/pallas_call | solution.py:46
Async XLA Ops:
  2.7 3.7 %collective-permute-start = (bf16[1056,128]{1,0:T(8,128)(2,1)}, bf16[1056,128]{1,0:T(8,128)(2,1)S(1)}, u32[]{:S(2)}, u32[]{:S(2)}) collective-permute-start(bf16[1056,128]{1,0:T(8,128)(2,1)} %get-tuple-element.35.mine), channel_id=1, source_target_pairs={{0,4},{4,0},{8,12},{12,8},{16,20},{20,16},{24,28},{28,24},{32,36},... | collective-permute-start | bytes 811016 | tf_op jit(solution)/shard_map/ppermute | solution.py:34
  4.8 1.0 %copy-start = (bf16[1056,128]{1,0:T(8,128)(2,1)S(1)}, bf16[1056,128]{1,0:T(8,128)(2,1)}, u32[]{:S(2)}) copy-start(bf16[1056,128]{1,0:T(8,128)(2,1)} %get-tuple-element.35.mine) | copy-start | bytes 811012
  5.7 18.7 %copy-start.4 = (bf16[64,1024]{1,0:T(8,128)(2,1)S(1)}, bf16[64,1024]{1,0:T(8,128)(2,1)}, u32[]{:S(2)}) copy-start(bf16[64,1024]{1,0:T(8,128)(2,1)} %get-tuple-element.51.refs_8_.wide) | copy-start | bytes 393220
  6.4 18.0 %copy-start.1 = (f32[64,8,128]{2,1,0:T(8,128)S(1)}, f32[64,8,128]{2,1,0:T(8,128)}, u32[]{:S(2)}) copy-start(f32[64,8,128]{2,1,0:T(8,128)} %param.15) | copy-start | bytes 786436
  6.4 18.0 %copy-start.2 = (f32[64,8,128]{2,1,0:T(8,128)S(1)}, f32[64,8,128]{2,1,0:T(8,128)}, u32[]{:S(2)}) copy-start(f32[64,8,128]{2,1,0:T(8,128)} %param.14) | copy-start | bytes 786436
  7.4 17.0 %collective-permute-start.1 = (bf16[80,512]{1,0:T(8,128)(2,1)S(1)}, bf16[80,512]{1,0:T(8,128)(2,1)S(1)}, u32[]{:S(2)}, u32[]{:S(2)}) collective-permute-start(bf16[80,512]{1,0:T(8,128)(2,1)S(1)} %get-tuple-element.40), channel_id=1, source_target_pairs={{8,16},{16,8},{12,20},{20,12},{24,32},{32,24},{28,36},{36,28},{40,... | collective-permute-start | bytes 245768 | tf_op jit(solution)/shard_map/ppermute | solution.py:34
  10.6 13.8 %collective-permute-start.2 = (bf16[80,512]{1,0:T(8,128)(2,1)S(1)}, bf16[80,512]{1,0:T(8,128)(2,1)S(1)}, u32[]{:S(2)}, u32[]{:S(2)}) collective-permute-start(bf16[80,512]{1,0:T(8,128)(2,1)S(1)} %get-tuple-element.41), channel_id=1, source_target_pairs={{0,8},{8,0},{4,12},{12,4},{16,24},{24,16},{20,28},{28,20},{32,40},... | collective-permute-start | bytes 245768 | tf_op jit(solution)/shard_map/ppermute | solution.py:34
  26.4 15.0 %collective-permute-start.3 = (bf16[80,512]{1,0:T(8,128)(2,1)S(1)}, bf16[80,512]{1,0:T(8,128)(2,1)S(1)}, u32[]{:S(2)}, u32[]{:S(2)}) collective-permute-start(bf16[80,512]{1,0:T(8,128)(2,1)S(1)} %get-tuple-element.54), channel_id=1, source_target_pairs={{8,16},{16,8},{12,20},{20,12},{24,32},{32,24},{28,36},{36,28},{40,... | collective-permute-start | bytes 245768 | tf_op jit(solution)/shard_map/ppermute | solution.py:34
  28.3 13.0 %collective-permute-start.4 = (bf16[80,512]{1,0:T(8,128)(2,1)S(1)}, bf16[80,512]{1,0:T(8,128)(2,1)S(1)}, u32[]{:S(2)}, u32[]{:S(2)}) collective-permute-start(bf16[80,512]{1,0:T(8,128)(2,1)S(1)} %get-tuple-element.55), channel_id=1, source_target_pairs={{0,8},{8,0},{4,12},{12,4},{16,24},{24,16},{20,28},{28,20},{32,40},... | collective-permute-start | bytes 245768 | tf_op jit(solution)/shard_map/ppermute | solution.py:34
  43.3 16.2 %collective-permute-start.5 = (bf16[80,512]{1,0:T(8,128)(2,1)S(1)}, bf16[80,512]{1,0:T(8,128)(2,1)S(1)}, u32[]{:S(2)}, u32[]{:S(2)}) collective-permute-start(bf16[80,512]{1,0:T(8,128)(2,1)S(1)} %get-tuple-element.59), channel_id=1, source_target_pairs={{8,16},{16,8},{12,20},{20,12},{24,32},{32,24},{28,36},{36,28},{40,... | collective-permute-start | bytes 245768 | tf_op jit(solution)/shard_map/ppermute | solution.py:34
  45.2 14.3 %collective-permute-start.6 = (bf16[80,512]{1,0:T(8,128)(2,1)S(1)}, bf16[80,512]{1,0:T(8,128)(2,1)S(1)}, u32[]{:S(2)}, u32[]{:S(2)}) collective-permute-start(bf16[80,512]{1,0:T(8,128)(2,1)S(1)} %get-tuple-element.60), channel_id=1, source_target_pairs={{0,8},{8,0},{4,12},{12,4},{16,24},{24,16},{20,28},{28,20},{32,40},... | collective-permute-start | bytes 245768 | tf_op jit(solution)/shard_map/ppermute | solution.py:34
  60.7 5.6 %collective-permute-start.7 = (bf16[16,512]{1,0:T(8,128)(2,1)S(1)}, bf16[16,512]{1,0:T(8,128)(2,1)S(1)}, u32[]{:S(2)}, u32[]{:S(2)}) collective-permute-start(bf16[16,512]{1,0:T(8,128)(2,1)S(1)} %get-tuple-element.65), channel_id=1, source_target_pairs={{0,1},{1,0},{2,3},{3,2},{4,5},{5,4},{6,7},{7,6},{8,9},{9,8},{10,11... | collective-permute-start | bytes 49160 | tf_op jit(solution)/shard_map/ppermute | solution.py:34
  63.2 3.2 %copy-start.3 = (bf16[64,64]{1,0:T(8,128)(2,1)S(1)}, bf16[64,64]{1,0:T(8,128)(2,1)}, u32[]{:S(2)}) copy-start(bf16[64,64]{1,0:T(8,128)(2,1)} %inverse.1) | copy-start | bytes 24580
